TPU v7x, 32 devices: a whole 2x2x4 slice. The times are simulated.
32 devices in a mesh: seq: 16 (over z, y, x), tensor: 2 (over core).
Axes of the slice: x: 2, y: 2, z: 4, core: 2. Of those that a mesh axis runs over, the one named last changes fastest.
Arguments:
- text_in: bfloat16 [4096, 768], P('seq'), may hold values from -6 to 6
- layout_in: bfloat16 [4096, 192], P('seq'), may hold values from -6 to 6
- text_cot: bfloat16 [4096, 768], P('seq'), may hold values from -6 to 6
- layout_cot: bfloat16 [4096, 192], P('seq'), may hold values from -6 to 6
- doc_ids: int32 [4096], P('seq'), may hold values from 0 to 3, as said below
- span_ids: int32 [4096], P('seq'), may hold values from 0 to 15, as said below
- intersection_flags: int32 [4096], P('seq'), may hold values 0 or 1
- text_qkv: bfloat16 [3, 768, 768], P(None, None, 'tensor'), may hold values from -0.21875 to 0.21875
- text_qv_bias: bfloat16 [2, 768], P(None, 'tensor'), may hold values from -3 to 3
- text_out: bfloat16 [768, 768], P('tensor'), may hold values from -3.5 to 3.5
- text_out_bias: bfloat16 [2, 768], replicated, may hold values from -3 to 3
- text_gains: bfloat16 [2, 768], replicated, may hold values from 0.25 to 1.75
- text_shifts: bfloat16 [2, 768], replicated, may hold values from -3 to 3
- text_up: bfloat16 [768, 3072], P(None, 'tensor'), may hold values from -0.21875 to 0.21875
- text_up_bias: bfloat16 [3072], P('tensor'), may hold values from -3 to 3
- text_down: bfloat16 [3072, 768], P('tensor'), may hold values from -0.109375 to 0.109375
- layout_qkv: bfloat16 [3, 192, 192], P(None, None, 'tensor'), may hold values from -0.4375 to 0.4375
- layout_qv_bias: bfloat16 [2, 192], P(None, 'tensor'), may hold values from -3 to 3
- layout_out: bfloat16 [192, 192], P('tensor'), may hold values from -6 to 6
- layout_out_bias: bfloat16 [2, 192], replicated, may hold values from -3 to 3
- layout_gains: bfloat16 [2, 192], replicated, may hold values from 0.25 to 1.75
- layout_shifts: bfloat16 [2, 192], replicated, may hold values from -3 to 3
- layout_up: bfloat16 [192, 768], P(None, 'tensor'), may hold values from -0.4375 to 0.4375
- layout_up_bias: bfloat16 [768], P('tensor'), may hold values from -3 to 3
- layout_down: bfloat16 [768, 192], P('tensor'), may hold values from -0.21875 to 0.21875
Outputs:
- text_result: bfloat16 [4096, 768], P('seq')
- layout_result: bfloat16 [4096, 192], P('seq')
- text_in_grad: bfloat16 [4096, 768], P('seq')
- layout_in_grad: bfloat16 [4096, 192], P('seq')
- text_qkv_grad: float32 [3, 768, 768], P(None, None, 'tensor')
- text_qv_bias_grad: float32 [2, 768], P(None, 'tensor')
- text_out_grad: float32 [768, 768], P('tensor')
- text_out_bias_grad: float32 [2, 768], replicated
- text_gains_grad: float32 [2, 768], replicated
- text_shifts_grad: float32 [2, 768], replicated
- text_up_grad: float32 [768, 3072], P(None, 'tensor')
- text_up_bias_grad: float32 [3072], P('tensor')
- text_down_grad: float32 [3072, 768], P('tensor')
- layout_qkv_grad: float32 [3, 192, 192], P(None, None, 'tensor')
- layout_qv_bias_grad: float32 [2, 192], P(None, 'tensor')
- layout_out_grad: float32 [192, 192], P('tensor')
- layout_out_bias_grad: float32 [2, 192], replicated
- layout_gains_grad: float32 [2, 192], replicated
- layout_shifts_grad: float32 [2, 192], replicated
- layout_up_grad: float32 [192, 768], P(None, 'tensor')
- layout_up_bias_grad: float32 [768], P('tensor')
- layout_down_grad: float32 [768, 192], P('tensor')
Inputs may be any that keep to these rules, and one draw needn't show every extreme that they name: `doc_ids`: never falls along the rows; every document lies inside one aligned block of 2048 rows and has at most 2048 rows; the first such block is one whole document. `span_ids`: never falls along the rows; each aligned block of 512 rows holds exactly two windows, each with an id of its own that no other row carries, and neither window has exactly 256 rows.
All inputs are finite; a program needn't handle non-finite values. No bound on the sum of `intersection_flags` on one device may be relied on, other than what follows from the above.
Results may differ from a plain program's by a relative error of at most 0.017.
The roundings to bfloat16 on the way count: a program that leaves them out, or rounds other values in their place, can miss the bound.
Values may be sent and summed in bfloat16 or wider, within the bound.
No kernel may reach another device: no remote copies, remote signals or barrier semaphores. Data moves between devices by JAX's collectives and lax.ppermute only.
A program may use at most 128 MiB of HBM per device.

v0:
```python
from functools import partial

import jax
import jax.numpy as jnp
from jax import lax
from jax.sharding import PartitionSpec as P

HT = 64
HL = 16


EPS = 1e-06
NEG = -1e30


def partner(shard, axis, apart):
    return lax.ppermute(shard, axis, [(i, i ^ 1 << apart) for i in range(lax.axis_size(axis))])


def shortened(shard):
    return jax.tree.map(lambda a: a.astype(jnp.bfloat16) if a.dtype == jnp.float32 else a, shard)


def split_heads(matrix, head_size):
    return matrix.reshape(matrix.shape[0], -1, head_size)


def paired(left_text, left_layout, right_text, right_layout, text_scale, layout_scale):
    text_part = jnp.einsum(
        "qhe,khe->hqk",
        split_heads(left_text, HT),
        split_heads(right_text, HT),
        preferred_element_type=jnp.float32,
    )
    layout_part = jnp.einsum(
        "qhe,khe->hqk",
        split_heads(left_layout, HL),
        split_heads(right_layout, HL),
        preferred_element_type=jnp.float32,
    )
    return text_part * text_scale + layout_part * layout_scale


def visible_pairs(row_doc, row_span, col_doc, col_span):
    return ((row_doc[:, None] == col_doc[None, :]) & (row_span[:, None] == col_span[None, :]))[None]


def masked_scores(query_text, query_layout, key_group, visible):
    return jnp.where(
        visible,
        paired(query_text, query_layout, key_group[0], key_group[2], HT ** (-0.5), HL ** (-0.5)),
        NEG,
    )


def recompute(
    query_text,
    query_layout,
    context_grad_text,
    context_grad_layout,
    key_group,
    visible,
    highest,
    totals,
):
    scores = masked_scores(query_text, query_layout, key_group, visible)
    weights = jnp.where(visible, jnp.exp(scores - highest[:, :, None]), 0.0)
    probability = weights / totals[:, :, None]
    prob_grads = paired(
        context_grad_text, context_grad_layout, key_group[1], key_group[3], 1.0, 1.0
    )
    return (probability, prob_grads)


def key_value_grads(
    score_grads, prob_low, query_text, query_layout, context_grad_text, context_grad_layout
):
    key_grad_text = jnp.einsum(
        "hqk,qhe->khe", score_grads, split_heads(query_text, HT), preferred_element_type=jnp.float32
    ) * HT ** (-0.5)
    value_grad_text = jnp.einsum(
        "hqk,qhe->khe",
        prob_low,
        split_heads(context_grad_text, HT),
        preferred_element_type=jnp.float32,
    )
    key_grad_layout = jnp.einsum(
        "hqk,qhe->khe",
        score_grads,
        split_heads(query_layout, HL),
        preferred_element_type=jnp.float32,
    ) * HL ** (-0.5)
    value_grad_layout = jnp.einsum(
        "hqk,qhe->khe",
        prob_low,
        split_heads(context_grad_layout, HL),
        preferred_element_type=jnp.float32,
    )
    return (key_grad_text, value_grad_text, key_grad_layout, value_grad_layout)


def norm_forward(total, gain, shift):
    center = total - jnp.mean(total, axis=-1, keepdims=True)
    inverse = lax.rsqrt(jnp.mean(center * center, axis=-1, keepdims=True) + EPS)
    normed = center * inverse
    return (normed * gain.astype(jnp.float32) + shift.astype(jnp.float32), normed, inverse)


def norm_backward(upstream, normed, inverse, gain):
    scaled = upstream * gain.astype(jnp.float32)
    total_grad = inverse * (
        scaled
        - jnp.mean(scaled, axis=-1, keepdims=True)
        - normed * jnp.mean(scaled * normed, axis=-1, keepdims=True)
    )
    return (total_grad, jnp.sum(upstream * normed, axis=0), jnp.sum(upstream, axis=0))


def project(inputs, qkv_weight, qv_bias):
    queries = (
        jnp.dot(inputs, qkv_weight[0], preferred_element_type=jnp.float32) + qv_bias[0]
    ).astype(jnp.bfloat16)
    key_rows = jnp.dot(inputs, qkv_weight[1], preferred_element_type=jnp.float32).astype(
        jnp.bfloat16
    )
    values = (
        jnp.dot(inputs, qkv_weight[2], preferred_element_type=jnp.float32) + qv_bias[1]
    ).astype(jnp.bfloat16)
    return (queries, key_rows, values)


def finish_attention(inputs, attended, out_bias, norm_gains, norm_shifts, up_weight, up_bias):
    hidden, normed_one, inverse_one = norm_forward(
        inputs.astype(jnp.float32) + attended + out_bias[0], norm_gains[0], norm_shifts[0]
    )
    hidden_low = hidden.astype(jnp.bfloat16)
    before = jnp.dot(hidden_low, up_weight, preferred_element_type=jnp.float32) + up_bias
    activated = jax.nn.gelu(before, approximate=False).astype(jnp.bfloat16)
    return (hidden, hidden_low, normed_one, inverse_one, before, activated)


def ffn_backward(cotangent, normed_two, inverse_two, norm_gains, kept, up_weight, down_weight):
    hidden, hidden_low, normed_one, inverse_one, before, activated = kept
    second_grad, gain_two, shift_two = norm_backward(
        cotangent, normed_two, inverse_two, norm_gains[1]
    )
    ffn_grad = second_grad.astype(jnp.bfloat16)
    down_grad = jnp.einsum("ti,td->id", activated, ffn_grad, preferred_element_type=jnp.float32)
    bias_two = jnp.sum(ffn_grad.astype(jnp.float32), axis=0)
    act_grad = jnp.einsum("td,id->ti", ffn_grad, down_weight, preferred_element_type=jnp.float32)
    gelu_back = jax.vjp(partial(jax.nn.gelu, approximate=False), before)[1]
    before_grad = gelu_back(act_grad)[0].astype(jnp.bfloat16)
    up_grad = jnp.einsum("td,ti->di", hidden_low, before_grad, preferred_element_type=jnp.float32)
    up_bias_grad = jnp.sum(before_grad.astype(jnp.float32), axis=0)
    hidden_part = jnp.einsum(
        "ti,di->td", before_grad, up_weight, preferred_element_type=jnp.float32
    )
    return (
        second_grad,
        hidden_part,
        down_grad,
        up_grad,
        up_bias_grad,
        bias_two,
        gain_two,
        shift_two,
    )


def attention_backward(hidden_grad, kept, norm_gains, context, out_weight):
    hidden, hidden_low, normed_one, inverse_one, before, activated = kept
    first_grad, gain_one, shift_one = norm_backward(
        hidden_grad, normed_one, inverse_one, norm_gains[0]
    )
    attended_grad = first_grad.astype(jnp.bfloat16)
    out_grad = jnp.einsum("th,td->hd", context, attended_grad, preferred_element_type=jnp.float32)
    bias_one = jnp.sum(attended_grad.astype(jnp.float32), axis=0)
    context_grad = jnp.einsum(
        "td,hd->th", attended_grad, out_weight, preferred_element_type=jnp.float32
    ).astype(jnp.bfloat16)
    return (first_grad, context_grad, out_grad, bias_one, gain_one, shift_one)


def project_backward(inputs, qkv_weight, query_grad, key_grad, value_grad):
    stacked = jnp.stack([query_grad, key_grad, value_grad])
    qkv_grad = jnp.einsum("td,sth->sdh", inputs, stacked, preferred_element_type=jnp.float32)
    bias_grad = jnp.stack(
        [
            jnp.sum(query_grad.astype(jnp.float32), axis=0),
            jnp.sum(value_grad.astype(jnp.float32), axis=0),
        ]
    )
    input_part = jnp.einsum("sth,sdh->td", stacked, qkv_weight, preferred_element_type=jnp.float32)
    return (qkv_grad, bias_grad, input_part)


def per_device(
    text_in,
    layout_in,
    text_cot,
    layout_cot,
    doc_ids,
    span_ids,
    intersection_flags,
    text_qkv,
    text_qv_bias,
    text_out,
    text_out_bias,
    text_gains,
    text_shifts,
    text_up,
    text_up_bias,
    text_down,
    layout_qkv,
    layout_qv_bias,
    layout_out,
    layout_out_bias,
    layout_gains,
    layout_shifts,
    layout_up,
    layout_up_bias,
    layout_down,
):
    row_count = text_in.shape[0]
    query_text, key_text, value_text = project(text_in, text_qkv, text_qv_bias)
    query_layout, key_layout, value_layout = project(layout_in, layout_qkv, layout_qv_bias)
    own_keys = (key_text, value_text, key_layout, value_layout)
    partner_doc, partner_span = partner((doc_ids, span_ids), "seq", 0)
    partner_keys = partner((key_text, value_text, key_layout, value_layout), "seq", 0)
    all_keys = tuple(
        (jnp.concatenate([own, other], axis=0) for own, other in zip(own_keys, partner_keys))
    )
    col_doc = jnp.concatenate([doc_ids, partner_doc], axis=0)
    col_span = jnp.concatenate([span_ids, partner_span], axis=0)
    visible = visible_pairs(doc_ids, span_ids, col_doc, col_span)
    scores = masked_scores(query_text, query_layout, all_keys, visible)
    highest = jnp.max(scores, axis=2)
    weights = jnp.where(visible, jnp.exp(scores - highest[:, :, None]), 0.0)
    totals = jnp.sum(weights, axis=2)
    probs_low = (weights / totals[:, :, None]).astype(jnp.bfloat16)
    context_text = (
        jnp.einsum(
            "hqk,khe->qhe",
            probs_low,
            split_heads(all_keys[1], HT),
            preferred_element_type=jnp.float32,
        )
        .reshape(row_count, -1)
        .astype(jnp.bfloat16)
    )
    context_layout = (
        jnp.einsum(
            "hqk,khe->qhe",
            probs_low,
            split_heads(all_keys[3], HL),
            preferred_element_type=jnp.float32,
        )
        .reshape(row_count, -1)
        .astype(jnp.bfloat16)
    )
    attended_text, attended_layout = lax.psum(
        (
            jnp.dot(context_text, text_out, preferred_element_type=jnp.float32),
            jnp.dot(context_layout, layout_out, preferred_element_type=jnp.float32),
        ),
        "tensor",
    )
    text_kept = finish_attention(
        text_in, attended_text, text_out_bias, text_gains, text_shifts, text_up, text_up_bias
    )
    layout_kept = finish_attention(
        layout_in,
        attended_layout,
        layout_out_bias,
        layout_gains,
        layout_shifts,
        layout_up,
        layout_up_bias,
    )
    ffn_text, ffn_layout = lax.psum(
        (
            jnp.dot(text_kept[5], text_down, preferred_element_type=jnp.float32),
            jnp.dot(layout_kept[5], layout_down, preferred_element_type=jnp.float32),
        ),
        "tensor",
    )
    text_result, text_normed_two, text_inverse_two = norm_forward(
        text_kept[0] + ffn_text + text_out_bias[1], text_gains[1], text_shifts[1]
    )
    layout_result, layout_normed_two, layout_inverse_two = norm_forward(
        layout_kept[0] + ffn_layout + layout_out_bias[1], layout_gains[1], layout_shifts[1]
    )
    keep_rows = (1 - intersection_flags).astype(jnp.float32)[:, None]
    (
        text_second,
        text_hidden_part,
        text_down_grad,
        text_up_grad,
        text_up_bias_grad,
        text_bias_two,
        text_gain_two,
        text_shift_two,
    ) = ffn_backward(
        text_cot.astype(jnp.float32) * keep_rows,
        text_normed_two,
        text_inverse_two,
        text_gains,
        text_kept,
        text_up,
        text_down,
    )
    (
        layout_second,
        layout_hidden_part,
        layout_down_grad,
        layout_up_grad,
        layout_up_bias_grad,
        layout_bias_two,
        layout_gain_two,
        layout_shift_two,
    ) = ffn_backward(
        layout_cot.astype(jnp.float32) * keep_rows,
        layout_normed_two,
        layout_inverse_two,
        layout_gains,
        layout_kept,
        layout_up,
        layout_down,
    )
    hidden_sum_text, hidden_sum_layout = lax.psum((text_hidden_part, layout_hidden_part), "tensor")
    text_first, context_grad_text, text_out_grad, text_bias_one, text_gain_one, text_shift_one = (
        attention_backward(
            text_second + hidden_sum_text, text_kept, text_gains, context_text, text_out
        )
    )
    (
        layout_first,
        context_grad_layout,
        layout_out_grad,
        layout_bias_one,
        layout_gain_one,
        layout_shift_one,
    ) = attention_backward(
        layout_second + hidden_sum_layout, layout_kept, layout_gains, context_layout, layout_out
    )
    probability, prob_grads = recompute(
        query_text,
        query_layout,
        context_grad_text,
        context_grad_layout,
        all_keys,
        visible,
        highest,
        totals,
    )
    row_delta = jnp.sum(probability * prob_grads, axis=2)
    score_grads = (probability * (prob_grads - row_delta[:, :, None])).astype(jnp.bfloat16)
    prob_low = probability.astype(jnp.bfloat16)
    query_grad_text = jnp.einsum(
        "hqk,khe->qhe",
        score_grads,
        split_heads(all_keys[0], HT),
        preferred_element_type=jnp.float32,
    ) * HT ** (-0.5)
    query_grad_layout = jnp.einsum(
        "hqk,khe->qhe",
        score_grads,
        split_heads(all_keys[2], HL),
        preferred_element_type=jnp.float32,
    ) * HL ** (-0.5)
    spread = key_value_grads(
        score_grads, prob_low, query_text, query_layout, context_grad_text, context_grad_layout
    )
    returned = partner(shortened(tuple((member[row_count:] for member in spread))), "seq", 0)
    key_grads = tuple((member[:row_count] + back for member, back in zip(spread, returned)))
    key_grad_text, value_grad_text, key_grad_layout, value_grad_layout = key_grads
    text_qkv_grad, text_qv_bias_grad, text_input_part = project_backward(
        text_in,
        text_qkv,
        query_grad_text.reshape(row_count, -1).astype(jnp.bfloat16),
        key_grad_text.reshape(row_count, -1).astype(jnp.bfloat16),
        value_grad_text.reshape(row_count, -1).astype(jnp.bfloat16),
    )
    layout_qkv_grad, layout_qv_bias_grad, layout_input_part = project_backward(
        layout_in,
        layout_qkv,
        query_grad_layout.reshape(row_count, -1).astype(jnp.bfloat16),
        key_grad_layout.reshape(row_count, -1).astype(jnp.bfloat16),
        value_grad_layout.reshape(row_count, -1).astype(jnp.bfloat16),
    )
    input_sum_text, input_sum_layout = (
        lax.psum(text_input_part.astype(jnp.bfloat16), "tensor").astype(jnp.float32),
        lax.psum(layout_input_part.astype(jnp.bfloat16), "tensor").astype(jnp.float32),
    )
    text_in_grad = (text_first + input_sum_text).astype(jnp.bfloat16)
    layout_in_grad = (layout_first + input_sum_layout).astype(jnp.bfloat16)
    (
        text_qkv_grad,
        text_qv_bias_grad,
        text_out_grad,
        text_bias_one,
        text_gain_one,
        text_shift_one,
        layout_qkv_grad,
        layout_qv_bias_grad,
        layout_out_grad,
        layout_bias_one,
        layout_gain_one,
        layout_shift_one,
        text_down_grad,
        text_up_grad,
        text_up_bias_grad,
        text_bias_two,
        text_gain_two,
        text_shift_two,
        layout_down_grad,
        layout_up_grad,
        layout_up_bias_grad,
        layout_bias_two,
        layout_gain_two,
        layout_shift_two,
    ) = lax.psum(
        (
            text_qkv_grad,
            text_qv_bias_grad,
            text_out_grad,
            text_bias_one,
            text_gain_one,
            text_shift_one,
            layout_qkv_grad,
            layout_qv_bias_grad,
            layout_out_grad,
            layout_bias_one,
            layout_gain_one,
            layout_shift_one,
            text_down_grad,
            text_up_grad,
            text_up_bias_grad,
            text_bias_two,
            text_gain_two,
            text_shift_two,
            layout_down_grad,
            layout_up_grad,
            layout_up_bias_grad,
            layout_bias_two,
            layout_gain_two,
            layout_shift_two,
        ),
        "seq",
    )
    return (
        text_result.astype(jnp.bfloat16),
        layout_result.astype(jnp.bfloat16),
        text_in_grad,
        layout_in_grad,
        text_qkv_grad,
        text_qv_bias_grad,
        text_out_grad,
        jnp.stack([text_bias_one, text_bias_two]),
        jnp.stack([text_gain_one, text_gain_two]),
        jnp.stack([text_shift_one, text_shift_two]),
        text_up_grad,
        text_up_bias_grad,
        text_down_grad,
        layout_qkv_grad,
        layout_qv_bias_grad,
        layout_out_grad,
        jnp.stack([layout_bias_one, layout_bias_two]),
        jnp.stack([layout_gain_one, layout_gain_two]),
        jnp.stack([layout_shift_one, layout_shift_two]),
        layout_up_grad,
        layout_up_bias_grad,
        layout_down_grad,
    )


def solution(mesh):
    return jax.shard_map(
        per_device,
        mesh=mesh,
        in_specs=(
            P("seq", None),
            P("seq", None),
            P("seq", None),
            P("seq", None),
            P("seq"),
            P("seq"),
            P("seq"),
            P(None, None, "tensor"),
            P(None, "tensor"),
            P("tensor", None),
            P(),
            P(),
            P(),
            P(None, "tensor"),
            P("tensor"),
            P("tensor", None),
            P(None, None, "tensor"),
            P(None, "tensor"),
            P("tensor", None),
            P(),
            P(),
            P(),
            P(None, "tensor"),
            P("tensor"),
            P("tensor", None),
        ),
        out_specs=(
            P("seq", None),
            P("seq", None),
            P("seq", None),
            P("seq", None),
            P(None, None, "tensor"),
            P(None, "tensor"),
            P("tensor", None),
            P(),
            P(),
            P(),
            P(None, "tensor"),
            P("tensor"),
            P("tensor", None),
            P(None, None, "tensor"),
            P(None, "tensor"),
            P("tensor", None),
            P(),
            P(),
            P(),
            P(None, "tensor"),
            P("tensor"),
            P("tensor", None),
        ),
        check_vma=False,
    )
```

profile of v0, /device:TPU:0, one launch (start us, length us, event | category | flops | bytes accessed | tf_op | source)
XLA Modules:
  0.0 657.2 jit_solution(7054139835741036088)
XLA Ops:
  7.3 3.0 collective-permute-start.1
  17.0 2.0 collective-permute-start.3
  20.6 2.1 fusion.9
  32.6 2.3 fusion.85
  34.9 5.2 fusion.84
  40.0 2.2 fusion.73
  50.7 16.0 %all-reduce.18.cloned.1.call-done = (f32[256,768]{1,0:T(8,128)}, f32[256,192]{0,1:T(8,128)}) async-done(((f32[256,768]{1,0:T(8,128)}, f32[256,192]{0,1:T(8,128)}), (f32[256,768]{1,0:T(8,128)}, f32[256,192]{0,1:T(8,128)})) %all-reduce.18.cloned.1.call-update) | async-done | bytes 983056 | tf_op jit(solution)/shard_map/psum | solution.py:261
  71.5 5.2 multiply_convert_fusion.1
  80.1 20.2 %all-reduce.16.cloned.1.call-done = (f32[256,768]{1,0:T(8,128)}, f32[256,192]{0,1:T(8,128)}) async-done(((f32[256,768]{1,0:T(8,128)}, f32[256,192]{0,1:T(8,128)}), (f32[256,768]{1,0:T(8,128)}, f32[256,192]{0,1:T(8,128)})) %all-reduce.16.cloned.1.call-update) | async-done | bytes 983056 | tf_op jit(solution)/shard_map/psum | solution.py:280
  104.9 2.2 convert_reduce_fusion.3
  119.2 3.0 fusion.61
  122.3 3.1 fusion.70
  125.4 12.7 %all-reduce.14.cloned.1.call-done = (f32[256,768]{1,0:T(8,128)}, f32[256,192]{0,1:T(8,128)}) async-done(((f32[256,768]{1,0:T(8,128)}, f32[256,192]{0,1:T(8,128)}), (f32[256,768]{1,0:T(8,128)}, f32[256,192]{0,1:T(8,128)})) %all-reduce.14.cloned.1.call-update) | async-done | bytes 983056 | tf_op jit(solution)/shard_map/psum | solution.py:330
  138.1 2.1 multiply_reduce_fusion.2
  146.0 2.3 fusion.92
  149.4 3.8 multiply_reduce_fusion
  168.9 2.6 collective-permute-done.8
  176.3 3.0 fusion.8
  180.3 2.5 convolution_bitcast_fusion
  184.0 79.5 %all-reduce = (f32[2,384]{1,0:T(2,128)}, f32[1,768]{1,0:T(1,128)S(1)}, f32[1,768]{1,0:T(1,128)S(1)}, f32[1,768]{1,0:T(1,128)S(1)}, f32[1,768]{1,0:T(1,128)S(1)},...) all-reduce(f32[2,384]{1,0:T(2,128)S(1)} %pad_maximum_fusion.13, ...), channel_id=1, replica_groups=mesh['seq'=16,'tensor'=2] {'seq'}, use_global_device_ids=true, to_apply=%region_30.31 | all-reduce | flops 8640 | bytes 69120 | tf_op jit(solution)/shard_map/psum | solution.py:422
  270.4 363.1 %all-reduce.12.cloned.1.call-done = (f32[3,768,384]{1,2,0:T(8,128)}, f32[384,768]{1,0:T(8,128)}, f32[768,1536]{1,0:T(8,128)}, f32[1536,768]{1,0:T(8,128)}, f32[3...) async-done(((f32[3,768,384]{1,2,0:T(8,128)}, f32[384,768]{1,0:T(8,128)}, f32[768,1536]{1,0:T(8,128)}, f32[1536,768]{1,0:T(8,128)}, ...) | async-done | bytes 15040528 | tf_op jit(solution)/shard_map/psum | solution.py:422
  633.5 5.3 copy.69
  640.6 5.5 copy.89
  646.2 2.4 copy.90
  (391 shorter events, 90.9 us)
Async XLA Ops:
  7.2 64.3 %copy-start = (bf16[768,1536]{1,0:T(8,128)(2,1)S(1)}, bf16[768,1536]{1,0:T(8,128)(2,1)}, u32[]{:S(2)}) copy-start(bf16[768,1536]{1,0:T(8,128)(2,1)} %param.38) | copy-start | bytes 7077892
  7.2 11.9 %copy-start.18 = (bf16[256,768]{1,0:T(8,128)(2,1)S(1)}, bf16[256,768]{1,0:T(8,128)(2,1)}, u32[]{:S(2)}) copy-start(bf16[256,768]{1,0:T(8,128)(2,1)} %param.25) | copy-start | bytes 1179652
  7.2 11.8 %copy-start.99 = (bf16[2,384]{1,0:T(2,128)(2,1)S(1)}, bf16[2,384]{1,0:T(2,128)(2,1)}, u32[]{:S(2)}) copy-start(bf16[2,384]{1,0:T(2,128)(2,1)} %param.33) | copy-start | bytes 4612
  7.2 59.4 %all-reduce.18.cloned.1.call-start = ((), (), s32[]{:S(2)}) async-start(), calls=%async_computation.3 | async-start | bytes 1966080 | tf_op jit(solution)/shard_map/psum | solution.py:261
  7.3 17.2 %collective-permute-start.1 = (s32[256]{0:T(256)}, s32[256]{0:T(256)S(1)}, u32[]{:S(2)}, u32[]{:S(2)}) collective-permute-start(s32[256]{0:T(256)} %param.29), channel_id=1, source_target_pairs={{0,2},{2,0},{4,6},{6,4},{8,10},{10,8},{12,14},{14,12},{16,18},{18,... | collective-permute-start | bytes 3080 | tf_op jit(solution)/shard_map/ppermute | solution.py:17
  10.3 14.4 %collective-permute-start.2 = (s32[256]{0:T(256)}, s32[256]{0:T(256)S(1)}, u32[]{:S(2)}, u32[]{:S(2)}) collective-permute-start(s32[256]{0:T(256)} %param.30), channel_id=1, source_target_pairs={{0,2},{2,0},{4,6},{6,4},{8,10},{10,8},{12,14},{14,12},{16,18},{18,... | collective-permute-start | bytes 3080 | tf_op jit(solution)/shard_map/ppermute | solution.py:17
  11.5 14.1 %collective-permute-start.4 = (bf16[256,96]{0,1:T(8,128)(2,1)S(1)}, bf16[256,96]{0,1:T(8,128)(2,1)}, u32[]{:S(2)}, u32[]{:S(2)}) collective-permute-start(bf16[256,96]{0,1:T(8,128)(2,1)S(1)} %convolution_convert_fusion.5), channel_id=1, source_target_pairs={{0,2},{2,0},{4,6},{6,4},{8,10},{10,8},{12,14},{14,12},{16,18},{18,... | collective-permute-start | bytes 147464 | tf_op jit(solution)/shard_map/ppermute | solution.py:17
  15.3 11.6 %collective-permute-start.5 = (bf16[256,96]{0,1:T(8,128)(2,1)S(1)}, bf16[256,96]{0,1:T(8,128)(2,1)}, u32[]{:S(2)}, u32[]{:S(2)}) collective-permute-start(bf16[256,96]{0,1:T(8,128)(2,1)S(1)} %fusion.15), channel_id=1, source_target_pairs={{0,2},{2,0},{4,6},{6,4},{8,10},{10,8},{12,14},{14,12},{16,18},{18,... | collective-permute-start | bytes 147464 | tf_op jit(solution)/shard_map/ppermute | solution.py:17
  17.0 7.4 %copy-start.49 = (bf16[256,384]{1,0:T(8,128)(2,1)}, bf16[256,384]{1,0:T(8,128)(2,1)S(1)}, u32[]{:S(2)}) copy-start(bf16[256,384]{1,0:T(8,128)(2,1)S(1)} %convolution_convert_fusion.2) | copy-start | bytes 589828
  17.0 10.8 %collective-permute-start.3 = (bf16[256,384]{1,0:T(8,128)(2,1)S(1)}, bf16[256,384]{1,0:T(8,128)(2,1)}, u32[]{:S(2)}, u32[]{:S(2)}) collective-permute-start(bf16[256,384]{1,0:T(8,128)(2,1)S(1)} %convolution_convert_fusion.2), channel_id=1, source_target_pairs={{0,2},{2,0},{4,6},{6,4},{8,10},{10,8},{12,14},{14,12},{16,18},{18,... | collective-permute-start | bytes 589832 | tf_op jit(solution)/shard_map/ppermute | solution.py:17
  24.5 8.1 %copy-start.14 = (bf16[256,384]{0,1:T(8,128)(2,1)}, bf16[256,384]{0,1:T(8,128)(2,1)S(1)}, u32[]{:S(2)}) copy-start(bf16[256,384]{0,1:T(8,128)(2,1)S(1)} %copy.62) | copy-start | bytes 589828
  24.5 6.1 collective-permute-start
  27.8 14.4 %copy-start.24 = (bf16[512,96]{0,1:T(8,128)(2,1)}, bf16[512,96]{0,1:T(8,128)(2,1)S(1)}, u32[]{:S(2)}) copy-start(bf16[512,96]{0,1:T(8,128)(2,1)S(1)} %pad_maximum_fusion.7) | copy-start | bytes 294916
  46.5 53.8 %all-reduce.16.cloned.1.call-start = ((), (), s32[]{:S(2)}) async-start(), calls=%async_computation.2 | async-start | bytes 1966080 | tf_op jit(solution)/shard_map/psum | solution.py:280
  79.3 58.8 %all-reduce.14.cloned.1.call-start = ((), (), s32[]{:S(2)}) async-start(), calls=%async_computation.1 | async-start | bytes 1966080 | tf_op jit(solution)/shard_map/psum | solution.py:330
  117.2 149.9 %all-reduce.20.cloned.1.call-start = ((), (), s32[]{:S(2)}) async-start(), calls=%async_computation.4 | async-start | bytes 983040 | tf_op jit(solution)/shard_map/psum | solution.py:392
  158.6 9.4 %copy-start.33 = (f32[512,6,16]{0,2,1:T(8,128)S(1)}, f32[512,6,16]{0,2,1:T(8,128)}, u32[]{:S(2)}) copy-start(f32[512,6,16]{0,2,1:T(8,128)} %convolution_bitcast_fusion.5) | copy-start | bytes 589828
  158.6 12.9 %copy-start.34 = (f32[512,6,16]{0,2,1:T(8,128)S(1)}, f32[512,6,16]{0,2,1:T(8,128)}, u32[]{:S(2)}) copy-start(f32[512,6,16]{0,2,1:T(8,128)} %fusion.12) | copy-start | bytes 589828
  160.2 7.8 %collective-permute-start.9 = (bf16[256,6,16]{0,2,1:T(8,128)(2,1)}, bf16[256,6,16]{0,2,1:T(8,128)(2,1)}, u32[]{:S(2)}, u32[]{:S(2)}) collective-permute-start(bf16[256,6,16]{0,2,1:T(8,128)(2,1)} %slice.194), channel_id=1, source_target_pairs={{0,2},{2,0},{4,6},{6,4},{8,10},{10,8},{12,14},{14,12},{16,18},{18,... | collective-permute-start | bytes 147464 | tf_op jit(solution)/shard_map/ppermute | solution.py:17
  162.8 12.3 %copy-start.11 = (f32[512,6,64]{0,2,1:T(8,128)S(1)}, f32[512,6,64]{0,2,1:T(8,128)}, u32[]{:S(2)}) copy-start(f32[512,6,64]{0,2,1:T(8,128)} %fusion.7) | copy-start | bytes 2359300
  162.8 10.5 %collective-permute-start.7 = (bf16[256,6,64]{0,2,1:T(8,128)(2,1)S(1)}, bf16[256,6,64]{0,2,1:T(8,128)(2,1)}, u32[]{:S(2)}, u32[]{:S(2)}) collective-permute-start(bf16[256,6,64]{0,2,1:T(8,128)(2,1)S(1)} %slice.192), channel_id=1, source_target_pairs={{0,2},{2,0},{4,6},{6,4},{8,10},{10,8},{12,14},{14,12},{16,18},{18,... | collective-permute-start | bytes 589832 | tf_op jit(solution)/shard_map/ppermute | solution.py:17
  164.2 7.3 %collective-permute-start.8 = (bf16[256,6,16]{0,2,1:T(8,128)(2,1)S(1)}, bf16[256,6,16]{0,2,1:T(8,128)(2,1)S(1)}, u32[]{:S(2)}, u32[]{:S(2)}) collective-permute-start(bf16[256,6,16]{0,2,1:T(8,128)(2,1)S(1)} %slice.195), channel_id=1, source_target_pairs={{0,2},{2,0},{4,6},{6,4},{8,10},{10,8},{12,14},{14,12},{16,18},{18,... | collective-permute-start | bytes 147464 | tf_op jit(solution)/shard_map/ppermute | solution.py:17
  167.7 7.4 %collective-permute-start.6 = (bf16[256,6,64]{0,2,1:T(8,128)(2,1)}, bf16[256,6,64]{0,2,1:T(8,128)(2,1)}, u32[]{:S(2)}, u32[]{:S(2)}) collective-permute-start(bf16[256,6,64]{0,2,1:T(8,128)(2,1)} %slice.193), channel_id=1, source_target_pairs={{0,2},{2,0},{4,6},{6,4},{8,10},{10,8},{12,14},{14,12},{16,18},{18,... | collective-permute-start | bytes 589832 | tf_op jit(solution)/shard_map/ppermute | solution.py:17
  179.3 454.2 %all-reduce.12.cloned.1.call-start = ((), (), s32[]{:S(2)}) async-start(), calls=%async_computation | async-start | bytes 30277632 | tf_op jit(solution)/shard_map/psum | solution.py:422
  (113 other events, 312.9 us)
Sparse Core Ops, SparseCore 0:
  46.6 20.0 all-reduce.17
  79.5 20.7 all-reduce.15
  117.3 20.7 all-reduce.13
  179.5 18.8 all-reduce.19
  207.5 425.9 all-reduce.11
where the time goes:
time: 659 us; the launch traced here: 657 us
  waiting for transfers between devices  417 us (63%)
  blocking collectives  79.5 us (12%)
  matrix products  67.6 us (10%)
  other arithmetic  37.7 us (6%)
  local copies, waits for them, and re-layouts  28.9 us (4%)
  between operations  15.1 us (2%)
  starting transfers between devices  11.9 us (2%)
    psum x1, waiting for transfers between devices, per_device(): lax.psum((text_qkv_grad, text_qv_bias_grad, text_out_grad, text_bias_one,...  363 us
    psum x1, blocking collectives, per_device(): lax.psum((text_qkv_grad, text_qv_bias_grad, text_out_grad, text_bias_one,...  79.5 us
    unnamed x252, local copies, waits for them, and re-layouts  22.5 us
    psum x1, waiting for transfers between devices, per_device(): lax.psum((jnp.dot(text_kept[5], text_down, preferred_element_type=jnp.flo...  20.2 us
    psum x1, waiting for transfers between devices, per_device(): lax.psum((jnp.dot(context_text, text_out, preferred_element_type=jnp.floa...  16 us
  transfers between devices with their start and end apart: 15, of which 7 were waited for; matrix products, arithmetic and copies ran while one was open for 7% of the time, Pallas kernels for 0%

commit v1 on v0

v1 whole, which is shorter than its diff:
```python
from functools import partial

import jax
import jax.numpy as jnp
from jax import lax
from jax.experimental import pallas as pl
from jax.experimental.pallas import tpu as pltpu
from jax.sharding import PartitionSpec as P

HT = 64
HL = 16
EPS = 1e-06
NEG = -1e30
BF = jnp.bfloat16
F32 = jnp.float32
LANES = 128


def exchange(shard, mask, axis="seq"):
    return lax.ppermute(shard, axis, [(i, i ^ mask) for i in range(lax.axis_size(axis))])


def over_cores(shard):
    return exchange(shard, 1, "tensor")


def dot(left, right):
    return lax.dot_general(left, right, (((1,), (0,)), ((), ())), preferred_element_type=F32)


def dot_nt(left, right):
    return lax.dot_general(left, right, (((1,), (1,)), ((), ())), preferred_element_type=F32)


def dot_tn(left, right):
    return lax.dot_general(left, right, (((0,), (0,)), ((), ())), preferred_element_type=F32)


def call(kernel, outs, *args, scratch=(), smem=0, anys=(), flops=10**8):
    specs = []
    for at in range(len(args)):
        if at < smem:
            specs.append(pl.BlockSpec(memory_space=pltpu.SMEM))
        elif at in anys:
            specs.append(pl.BlockSpec(memory_space=pl.ANY))
        else:
            specs.append(pl.BlockSpec(memory_space=pltpu.VMEM))
    moved = sum(a.size * a.dtype.itemsize for a in args) + sum(
        o.size * o.dtype.itemsize for o in outs
    )
    return pl.pallas_call(
        kernel,
        out_shape=tuple(outs),
        in_specs=specs,
        out_specs=tuple(pl.BlockSpec(memory_space=pltpu.VMEM) for _ in outs),
        scratch_shapes=list(scratch),
        compiler_params=pltpu.CompilerParams(vmem_limit_bytes=48 * 1024 * 1024),
        cost_estimate=pl.CostEstimate(flops=flops, bytes_accessed=moved, transcendentals=0),
    )(*args)


def shape(dims, dtype):
    return jax.ShapeDtypeStruct(tuple(dims), dtype)


def project_rows(text_rows, layout_rows, weight_t, bias_t, weight_l, bias_l, which, write):
    text_part = dot(text_rows, weight_t[which])
    layout_part = dot(layout_rows, weight_l[which])
    if which != 1:
        row = which // 2
        text_part = text_part + bias_t[row : row + 1, :].astype(F32)
        layout_part = layout_part + bias_l[row : row + 1, :].astype(F32)
    pad = jnp.zeros((layout_part.shape[0], LANES - layout_part.shape[1]), F32)
    write(text_part.astype(BF), jnp.concatenate([layout_part, pad], axis=1).astype(BF))


def project_kernel(xt, xl, wt, bt, wl, bl, q_out, k_out, v_out):
    width = wt.shape[2]
    for which, out in enumerate((q_out, k_out, v_out)):

        def write(text_part, layout_part, out=out):
            out[:, :width] = text_part
            out[:, width:] = layout_part

        project_rows(xt[...], xl[...], wt, bt, wl, bl, which, write)


def hidden_bias(keys, columns):
    rows = keys.shape[1]
    down = jnp.broadcast_to(keys, (LANES, rows)).T
    parts = [
        jnp.where(down == keys[:, at : at + LANES], 0.0, NEG).astype(F32)
        for at in range(0, columns, LANES)
    ]
    return jnp.concatenate(parts, axis=1)


def head_mask(member, head, text_value, layout_value, axis):
    dims = (1, 2 * LANES) if axis == 1 else (2 * LANES, 1)
    at = lax.broadcasted_iota(jnp.int32, dims, axis)
    text = (at >= member * HT) & (at < (member + 1) * HT)
    layout = (at >= LANES + head * HL) & (at < LANES + (head + 1) * HL)
    return jnp.where(text, text_value, jnp.where(layout, layout_value, 0.0)).astype(F32)


def pair_of(ref, pair, width):
    return jnp.concatenate([ref[:, LANES * pair : LANES * (pair + 1)], ref[:, width:]], axis=1)


def probabilities(key_pair, query_head, bias):
    scores = dot_nt(key_pair, query_head) + bias
    weights = jnp.exp(scores - jnp.max(scores, axis=0, keepdims=True))
    return weights * (1.0 / jnp.sum(weights, axis=0, keepdims=True))


SCALE_T = HT ** (-0.5)
SCALE_L = HL ** (-0.5)


def attend_kernel(
    q_own, k_own, v_own, xt, xl, wt, bt, wl, bl, keys, out_t, out_l, part_out, k_all, v_all, context
):
    rows, width = q_own.shape[0], wt.shape[2]
    for which, own, target in ((1, k_own, k_all), (2, v_own, v_all)):
        target[:rows, :] = own[...]

        def write(text_part, layout_part, target=target):
            target[rows:, :width] = text_part
            target[rows:, width:] = layout_part

        project_rows(xt[...], xl[...], wt, bt, wl, bl, which, write)
    bias = hidden_bias(keys[...], rows)
    layout_sum = jnp.zeros((LANES, rows), F32)
    for pair in range(width // LANES):
        query_pair, key_pair = pair_of(q_own, pair, width), pair_of(k_all, pair, width)
        value_turned = pair_of(v_all, pair, width).T
        text_sum = jnp.zeros((LANES, rows), F32)
        for member in range(2):
            head = 2 * pair + member
            mask = head_mask(member, head, SCALE_T, SCALE_L, 1).astype(BF)
            probs_low = probabilities(key_pair, query_pair * mask, bias).astype(BF)
            turned = dot(value_turned, probs_low) * head_mask(member, head, 1.0, 1.0, 0)
            text_sum += turned[:LANES]
            layout_sum += turned[LANES:]
        context[:, LANES * pair : LANES * (pair + 1)] = text_sum.T.astype(BF)
    context[:, width:] = layout_sum.T.astype(BF)
    text_width = out_t.shape[1]
    part_out[:, :text_width] = dot(context[:, :width], out_t[...])
    part_out[:, text_width:] = dot(
        context[:, width : width + out_l.shape[0]], out_l[...]
    )


def norm_parts(total):
    center = total - jnp.mean(total, axis=1, keepdims=True)
    inverse = lax.rsqrt(jnp.mean(center * center, axis=1, keepdims=True) + EPS)
    return center * inverse, inverse


def norm_back(upstream, normed, inverse, gain):
    scaled = upstream * gain
    return inverse * (
        scaled
        - jnp.mean(scaled, axis=1, keepdims=True)
        - normed * jnp.mean(scaled * normed, axis=1, keepdims=True)
    )


def gelu_parts(before):
    share = 0.5 * (1.0 + lax.erf(before * (0.5**0.5)))
    slope = share + before * (jnp.exp(-0.5 * before * before) * 0.3989422804014327)
    return before * share, slope


def forward_kernel(
    idx, xt, xl, part, back, ob_t, ob_l, g_t, g_l, s_t, s_l, up_t, ub_t, dn_t, up_l, ub_l, dn_l,
    hidden_out, normed_out, inverse_out, mine_out, low_out, slope_t, slope_l, ffn_out,
):
    width = xt.shape[1]
    whole = part.shape[1]
    half = mine_out.shape[0]
    streams = (
        (0, width, xt, ob_t, g_t, s_t, up_t, ub_t, dn_t, slope_t),
        (width, whole, xl, ob_l, g_l, s_l, up_l, ub_l, dn_l, slope_l),
    )
    for at, (lo, hi, x, ob, g, s, up, ub, dn, slope_out) in enumerate(streams):
        total = x[...].astype(F32) + (part[:, lo:hi] + back[:, lo:hi]) + ob[0:1, :].astype(F32)
        normed, inverse = norm_parts(total)
        hidden = normed * g[0:1, :].astype(F32) + s[0:1, :].astype(F32)
        hidden_out[:, lo:hi] = hidden
        normed_out[:, lo:hi] = normed
        inverse_out[:, LANES * at : LANES * (at + 1)] = jnp.broadcast_to(
            inverse, (inverse.shape[0], LANES)
        )
        low_out[:, lo:hi] = hidden.astype(BF)
    mine_out[...] = low_out[pl.ds(pl.multiple_of(idx[3] * half, half), half), :]
    for lo, hi, x, ob, g, s, up, ub, dn, slope_out in streams:
        rows_low = low_out[:, lo:hi]
        units = up.shape[1]
        step = min(units, 384)
        total = None
        for cut in range(0, units, step):
            before = dot(rows_low, up[:, cut : cut + step]) + ub[:, cut : cut + step].astype(F32)
            activated, slope = gelu_parts(before)
            slope_out[:, cut : cut + step] = slope
            term = dot(activated.astype(BF), dn[cut : cut + step, :])
            total = term if total is None else total + term
        ffn_out[:, lo:hi] = total


def second_norm_kernel(
    idx, hidden, part, back, ct, cl, keep, ob_t, ob_l, g_t, g_l, s_t, s_l,
    rt_out, rl_out, second_out, low_out, mine_out, sums_out,
):
    width, whole = ct.shape[1], hidden.shape[1]
    half = mine_out.shape[0]
    for lo, hi, cot, ob, g, s, result in (
        (0, width, ct, ob_t, g_t, s_t, rt_out),
        (width, whole, cl, ob_l, g_l, s_l, rl_out),
    ):
        total = hidden[:, lo:hi] + (part[:, lo:hi] + back[:, lo:hi]) + ob[1:2, :].astype(F32)
        normed, inverse = norm_parts(total)
        gain = g[1:2, :].astype(F32)
        result[...] = (normed * gain + s[1:2, :].astype(F32)).astype(BF)
        upstream = cot[...].astype(F32) * keep[...]
        grad = norm_back(upstream, normed, inverse, gain)
        second_out[:, lo:hi] = grad
        low = grad.astype(BF)
        low_out[:, lo:hi] = low
        sums_out[0:1, lo:hi] = jnp.sum(upstream * normed, axis=0, keepdims=True)
        sums_out[1:2, lo:hi] = jnp.sum(upstream, axis=0, keepdims=True)
        sums_out[2:3, lo:hi] = jnp.sum(low.astype(F32), axis=0, keepdims=True)
    mine_out[...] = low_out[pl.ds(pl.multiple_of(idx[3] * half, half), half), :]


def ffn_back_kernel(grad, slope_t, slope_l, up_t, dn_t, up_l, dn_l, part_out, bias_t, bias_l):
    width = up_t.shape[0]
    whole = grad.shape[1]
    for lo, hi, slope, up, dn, bias in (
        (0, width, slope_t, up_t, dn_t, bias_t),
        (width, whole, slope_l, up_l, dn_l, bias_l),
    ):
        rows = grad[:, lo:hi]
        units = up.shape[1]
        step = min(units, 384)
        total = None
        for cut in range(0, units, step):
            act_grad = dot_nt(rows, dn[cut : cut + step, :])
            before_grad = (act_grad * slope[:, cut : cut + step]).astype(BF)
            bias[:, cut : cut + step] = jnp.sum(before_grad.astype(F32), axis=0, keepdims=True)
            term = dot_nt(before_grad, up[:, cut : cut + step])
            total = term if total is None else total + term
        part_out[:, lo:hi] = total


def first_norm_kernel(
    second, part, back, normed_in, inverse_in, g_t, g_l, first_out, low_out, sums_out
):
    width, whole = g_t.shape[1], second.shape[1]
    for at, (lo, hi, g) in enumerate(((0, width, g_t), (width, whole, g_l))):
        upstream = second[:, lo:hi] + (part[:, lo:hi] + back[:, lo:hi])
        normed = normed_in[:, lo:hi]
        inverse = inverse_in[:, LANES * at : LANES * at + 1]
        grad = norm_back(upstream, normed, inverse, g[0:1, :].astype(F32))
        first_out[:, lo:hi] = grad
        low = grad.astype(BF)
        low_out[:, lo:hi] = low
        sums_out[0:1, lo:hi] = jnp.sum(upstream * normed, axis=0, keepdims=True)
        sums_out[1:2, lo:hi] = jnp.sum(upstream, axis=0, keepdims=True)
        sums_out[2:3, lo:hi] = jnp.sum(low.astype(F32), axis=0, keepdims=True)


def unit_grads_kernel(idx, *refs):
    (
        low_parts, grad_parts, (up_t, dn_t, dn_l, ub_t, up_l, ub_l),
        (up_keep, up_send, dn_keep, dn_send),
        (low, grad, w_up, w_dn, w_dnl, held, sems),
    ) = refs[:7], refs[7:14], refs[14:20], refs[20:24], refs[24:]
    quarter = idx[1] * 2 + idx[0]
    zz = idx[2]
    copies = []
    for parts, target in ((low_parts, low), (grad_parts, grad)):
        at = 0
        for part in parts:
            count = part.shape[0]
            copies.append((part, target.at[pl.ds(at, count), :]))
            at += count
    units, units_l = w_dn.shape[0], w_dnl.shape[0]
    start = pl.multiple_of(quarter * units, units)
    copies.append((up_t.at[:, pl.ds(start, units)], w_up))
    copies.append((dn_t.at[pl.ds(start, units), :], w_dn))
    copies.append((dn_l.at[pl.ds(pl.multiple_of(quarter * units_l, units_l), units_l), :], w_dnl))
    copies = [pltpu.make_async_copy(s, d, sems.at[k]) for k, (s, d) in enumerate(copies)]
    for c in copies:
        c.start()
    for c in copies:
        c.wait()
    width = w_up.shape[0]
    piece = width // 4
    slot_rows = 16

    def grads(lo, hi, up, bias, down):
        before = dot(low[:, lo:hi], up) + bias
        activated, slope = gelu_parts(before)
        before_grad = (dot_nt(grad[:, lo:hi], down) * slope).astype(BF)
        return activated.astype(BF), before_grad

    act_t, back_t = grads(0, width, w_up[...], ub_t[:, pl.ds(start, units)].astype(F32), w_dn[...])
    act_l, back_l = grads(width, low.shape[1], up_l[...], ub_l[...].astype(F32), w_dnl[...])

    def place_layout(matrix):
        pad = jnp.zeros((matrix.shape[0], LANES - matrix.shape[1]), F32)
        padded = jnp.concatenate([matrix, pad], axis=1)
        for k in range(4):
            for slot in range(3):
                first = slot_rows * (3 * k + slot)
                held[k ^ zz, piece : piece + slot_rows, LANES * slot : LANES * (slot + 1)] = padded[
                    first : first + slot_rows
                ]

    def hand_out(keep, send):
        for at in range(2):
            keep[at] = held[2 * at]
            send[at] = held[2 * at + 1].astype(BF)

    up_grad = dot_tn(low[:, :width], back_t)
    for k in range(4):
        held[k ^ zz, :piece, :] = up_grad[piece * k : piece * (k + 1)]
    place_layout(dot_tn(low[:, width:], back_l))
    hand_out(up_keep, up_send)
    down_grad = dot_tn(act_t, grad[:, :width])
    part = piece // 2
    for k in range(4):
        for side in range(2):
            held[k ^ zz, part * side : part * (side + 1), :] = down_grad[
                part * k : part * (k + 1), units * side : units * (side + 1)
            ]
    place_layout(dot_tn(grad[:, width:], act_l))
    hand_out(dn_keep, dn_send)


def attention_back_kernel(
    idx, q_own, k_all, v_all, xt, xl, xt_p, xl_p, wt, bt, wl, bl, keys, out_t, out_l, ag_own, ag_p,
    sums_two, sums_one, bias_t, bias_l,
    keep_out, send_out, part_out, small_out,
    q_all, g_all, x_all, ag_all, context, dq, dk, dv, matrices, held,
):
    rows, width = q_own.shape[0], wt.shape[2]
    wide, whole = xt.shape[1], ag_own.shape[1]
    bx, by, zz = idx[0], idx[1], idx[2]
    x_all[:rows, :wide] = xt[...]
    x_all[:rows, wide:] = xl[...]
    x_all[rows:, :wide] = xt_p[...]
    x_all[rows:, wide:] = xl_p[...]
    ag_all[:rows, :] = ag_own[...]
    ag_all[rows:, :] = ag_p[...]
    q_all[:rows, :] = q_own[...]

    def write(text_part, layout_part):
        q_all[rows:, :width] = text_part
        q_all[rows:, width:] = layout_part

    project_rows(xt_p[...], xl_p[...], wt, bt, wl, bl, 0, write)
    g_all[:, :width] = dot_nt(ag_all[:, :wide], out_t[...]).astype(BF)
    layout_grad = dot_nt(ag_all[:, wide:], out_l[...])
    pad = jnp.zeros((2 * rows, LANES - layout_grad.shape[1]), F32)
    g_all[:, width:] = jnp.concatenate([layout_grad, pad], axis=1).astype(BF)
    bias = hidden_bias(keys[...], 2 * rows)
    zero_turned, zero = jnp.zeros((LANES, 2 * rows), F32), jnp.zeros((2 * rows, LANES), F32)
    layout_context, layout_dq, layout_dk, layout_dv = zero_turned, zero_turned, zero, zero
    for pair in range(width // LANES):
        query_pair, key_pair = pair_of(q_all, pair, width), pair_of(k_all, pair, width)
        grad_pair, value_pair = pair_of(g_all, pair, width), pair_of(v_all, pair, width)
        key_turned, value_turned = key_pair.T, value_pair.T
        text_context, text_dq, text_dk, text_dv = zero_turned, zero_turned, zero, zero
        for member in range(2):
            head = 2 * pair + member
            query_head = query_pair * head_mask(member, head, SCALE_T, SCALE_L, 1).astype(BF)
            grad_head = grad_pair * head_mask(member, head, 1.0, 1.0, 1).astype(BF)
            probs = probabilities(key_pair, query_head, bias)
            probs_low = probs.astype(BF)
            prob_grads = dot_nt(value_pair, grad_head)
            delta = jnp.sum(probs * prob_grads, axis=0, keepdims=True)
            score_grads = (probs * (prob_grads - delta)).astype(BF)
            value_part = dot(probs_low, grad_head)
            text_dv += value_part[:, :LANES]
            layout_dv += value_part[:, LANES:]
            key_part = dot(score_grads, query_head)
            text_dk += key_part[:, :LANES]
            layout_dk += key_part[:, LANES:]
            query_part = dot(key_turned, score_grads) * head_mask(member, head, SCALE_T, SCALE_L, 0)
            text_dq += query_part[:LANES]
            layout_dq += query_part[LANES:]
            context_part = dot(value_turned, probs_low) * head_mask(member, head, 1.0, 1.0, 0)
            text_context += context_part[:LANES]
            layout_context += context_part[LANES:]
        columns = slice(LANES * pair, LANES * (pair + 1))
        context[:, columns] = text_context.T.astype(BF)
        dq[:, columns] = text_dq.T.astype(BF)
        dk[:, columns] = text_dk.astype(BF)
        dv[:, columns] = text_dv.astype(BF)
    context[:, width:] = layout_context.T.astype(BF)
    dq[:, width:] = layout_dq.T.astype(BF)
    dk[:, width:] = layout_dk.astype(BF)
    dv[:, width:] = layout_dv.astype(BF)

    heads_l = wl.shape[2]
    total_t = total_l = None
    for which, grad in enumerate((dq, dk, dv)):
        term_t = dot_nt(grad[:rows, :width], wt[which])
        term_l = dot_nt(grad[:rows, width : width + heads_l], wl[which])
        total_t = term_t if which == 0 else total_t + term_t
        total_l = term_l if which == 0 else total_l + term_l
    part_out[:, :wide] = total_t
    part_out[:, wide:] = total_l

    small_out[...] = jnp.zeros_like(small_out)
    small_out[0:3, :whole] = sums_two[...]
    small_out[3:6, :whole] = sums_one[...]
    units, room = bias_t.shape[1], small_out.shape[1]
    small_out[6:7, :] = bias_t[:, :room]
    small_out[7:8, : units - room] = bias_t[:, room:]
    small_out[8:9, : bias_l.shape[1]] = bias_l[...]
    small_out[9:10, : dq.shape[1]] = jnp.sum(dq[:rows, :].astype(F32), axis=0, keepdims=True)
    small_out[10:11, : dv.shape[1]] = jnp.sum(dv[:rows, :].astype(F32), axis=0, keepdims=True)

    side = wide // 2
    start = pl.multiple_of(bx * side, side)
    x_side = x_all[:, pl.ds(start, side)]
    thin = side // 8

    def place(matrix, lowest):
        for y in range(2):
            for z in range(4):
                first = thin * (4 * y + z)
                held[(y ^ by) * 4 + (z ^ zz), lowest : lowest + thin, :] = matrix[
                    first : first + thin
                ]

    for which, grad in enumerate((dq, dk, dv)):
        place(dot_tn(x_side, grad[:, :width]), thin * which)
        matrices[which] = dot_tn(x_all[:, wide:], grad[:, width:])
    place(dot_tn(context[:, :width], ag_all[:, pl.ds(start, side)]), 3 * thin)
    matrices[3] = dot_tn(ag_all[:, wide:], context[:, width:])
    left, right = matrices[2 * bx], matrices[2 * bx + 1]
    strip = left.shape[0] // 8
    for y in range(2):
        for z in range(4):
            first = strip * (4 * y + z)
            both = jnp.concatenate(
                [left[first : first + strip], right[first : first + strip]], axis=0
            )
            for slot in range(3):
                held[
                    (y ^ by) * 4 + (z ^ zz), 4 * thin : 4 * thin + 16, LANES * slot : LANES * (slot + 1)
                ] = both[16 * slot : 16 * slot + 16]
    for k in range(4):
        keep_out[k] = held[k]
        send_out[k] = held[4 + k].astype(BF)


def turned_layout(matrix):
    count = matrix.shape[0]
    fill = -count % LANES
    if fill:
        matrix = jnp.concatenate([matrix, jnp.zeros((fill, LANES), F32)], axis=0)
    return matrix.T[:, :count]


def pieces_of(refs, idx):
    for at in range(4):
        for group in range(2):
            for k in range(2):
                yield refs[2 * at + group], k, (idx[1] * 2 + idx[0]) ^ at, (2 * k + group) ^ idx[2]


def unpack_layout(piece, k, lowest, table, quarter, place):
    for slot in range(3):
        first = pl.multiple_of(place * 48 + 16 * slot, 16)
        table[quarter, pl.ds(first, 16), :] = piece[
            k, lowest : lowest + 16, LANES * slot : LANES * (slot + 1)
        ].astype(F32)


def up_result_kernel(idx, *refs):
    pieces, (out_t, out_l), (table,) = refs[:8], refs[8:10], refs[10:]
    rows, columns = out_t.shape[0] // 4, out_t.shape[1] // 4
    for piece, k, quarter, place in pieces_of(pieces, idx):
        out_t[
            pl.ds(pl.multiple_of(place * rows, rows), rows),
            pl.ds(pl.multiple_of(quarter * columns, columns), columns),
        ] = piece[k, :rows, :].astype(F32)
        unpack_layout(piece, k, rows, table, quarter, place)
    thin = out_l.shape[1] // 4
    for q in range(4):
        out_l[:, thin * q : thin * (q + 1)] = table[q][:, :thin]


def down_result_kernel(idx, *refs):
    pieces, (out_t, out_l), (table,) = refs[:8], refs[8:10], refs[10:]
    rows, columns = out_t.shape[0] // 16, out_t.shape[1] // 2
    for piece, k, quarter, place in pieces_of(pieces, idx):
        first = pl.multiple_of((quarter * 4 + place) * rows, rows)
        for side in range(2):
            out_t[pl.ds(first, rows), columns * side : columns * (side + 1)] = piece[
                k, rows * side : rows * (side + 1), :
            ].astype(F32)
        unpack_layout(piece, k, 2 * rows, table, quarter, place)
    thin = out_l.shape[0] // 4
    for q in range(4):
        out_l[thin * q : thin * (q + 1), :] = turned_layout(table[q])[:thin]


def attention_result_kernel(idx, *refs):
    pieces, (qkv_t, out_t, qkv_l, out_l), (table,) = refs[:8], refs[8:12], refs[12:]
    side = qkv_t.shape[1] // 2
    thin, strip = side // 8, qkv_l.shape[1] // 8
    for piece, k, quarter, place in pieces_of(pieces, idx):
        x, y = quarter & 1, quarter >> 1
        eighth = y * 4 + place
        first = pl.multiple_of(x * side + eighth * thin, 16)
        for which in range(3):
            qkv_t[which, pl.ds(first, thin), :] = piece[
                k, thin * which : thin * (which + 1), :
            ].astype(F32)
        out_t[
            pl.ds(pl.multiple_of(eighth * thin, 16), thin), pl.ds(pl.multiple_of(x * side, side), side)
        ] = piece[k, 3 * thin : 4 * thin, :].astype(F32)
        both = jnp.concatenate(
            [
                piece[k, 4 * thin : 4 * thin + 16, LANES * slot : LANES * (slot + 1)].astype(F32)
                for slot in range(3)
            ],
            axis=0,
        )
        for member in range(2):
            table[2 * x + member, pl.ds(pl.multiple_of(eighth * strip, 8), strip), :] = both[
                strip * member : strip * (member + 1)
            ]
    heads_l = qkv_l.shape[2]
    for which in range(3):
        qkv_l[which] = table[which][:, :heads_l]
    out_l[...] = turned_layout(table[3])[:heads_l]


def gathered(own):
    even = jnp.stack([own, exchange(own, 8)])
    odd = exchange(even, 4)
    even_x, odd_y = exchange(even, 1), exchange(odd, 2)
    even_y, odd_x = exchange(even, 2), exchange(odd, 1)
    even_xy, odd_xy = exchange(even_x, 2), exchange(odd_y, 1)
    return even, odd, even_x, odd_x, even_y, odd_y, even_xy, odd_xy


def reduced(keep, send):
    total = keep + exchange(send, 4).astype(F32)
    own = total[0] + exchange(total[1].astype(BF), 8).astype(F32)
    mask = 16
    while mask < lax.axis_size("seq"):
        own = own + exchange(own, mask)
        mask *= 2
    return own.astype(BF)


def per_device(
    text_in,
    layout_in,
    text_cot,
    layout_cot,
    doc_ids,
    span_ids,
    intersection_flags,
    text_qkv,
    text_qv_bias,
    text_out,
    text_out_bias,
    text_gains,
    text_shifts,
    text_up,
    text_up_bias,
    text_down,
    layout_qkv,
    layout_qv_bias,
    layout_out,
    layout_out_bias,
    layout_gains,
    layout_shifts,
    layout_up,
    layout_up_bias,
    layout_down,
):
    rows, wide = text_in.shape
    thin = layout_in.shape[1]
    whole = wide + thin
    width, width_l = text_qkv.shape[2], layout_qkv.shape[2]
    padded = width + LANES
    units, units_l = text_up.shape[1], layout_up.shape[1]
    half = rows // 2
    place = lax.axis_index("seq")
    idx = jnp.stack(
        [place & 1, (place >> 1) & 1, (place >> 2) & 3, lax.axis_index("tensor")]
    ).astype(jnp.int32)
    quarter = place & 3
    quarter_l = units_l // 4

    own_key = (doc_ids * 65536 + span_ids).astype(F32)[None, :]
    text_other, layout_other = exchange(text_in, 1), exchange(layout_in, 1)
    keys = jnp.concatenate([own_key, exchange(own_key, 1)], axis=1)
    keep_rows = (1 - intersection_flags).astype(F32)[:, None]
    bias_up_t, bias_up_l = text_up_bias[None, :], layout_up_bias[None, :]
    quarter_up_l = lax.dynamic_slice_in_dim(layout_up, quarter * quarter_l, quarter_l, 1)
    quarter_ub_l = lax.dynamic_slice_in_dim(bias_up_l, quarter * quarter_l, quarter_l, 1)

    qkv_weights = (text_qkv, text_qv_bias, layout_qkv, layout_qv_bias)
    q_own, k_own, v_own = call(
        project_kernel, [shape((rows, padded), BF)] * 3, text_in, layout_in, *qkv_weights
    )
    attended, k_all, v_all = call(
        attend_kernel,
        [shape((rows, whole), F32)] + [shape((2 * rows, padded), BF)] * 2,
        q_own, k_own, v_own, text_other, layout_other, *qkv_weights, keys, text_out, layout_out,
        scratch=[pltpu.VMEM((rows, padded), BF)],
    )
    hidden, normed, inverse, low_mine, low, slope_t, slope_l, ffn = call(
        forward_kernel,
        [
            shape((rows, whole), F32),
            shape((rows, whole), F32),
            shape((rows, 2 * LANES), F32),
            shape((half, whole), BF),
            shape((rows, whole), BF),
            shape((rows, units), F32),
            shape((rows, units_l), F32),
            shape((rows, whole), F32),
        ],
        idx, text_in, layout_in, attended, over_cores(attended), text_out_bias, layout_out_bias,
        text_gains, layout_gains, text_shifts, layout_shifts, text_up, bias_up_t, text_down,
        layout_up, bias_up_l, layout_down, smem=1, flops=14 * 10**8,
    )
    ffn_back = over_cores(ffn)
    low_far = [exchange(low_mine, mask) for mask in (1, 2, 3)]
    text_result, layout_result, second, grad_low, grad_mine, sums_two = call(
        second_norm_kernel,
        [
            shape((rows, wide), BF),
            shape((rows, thin), BF),
            shape((rows, whole), F32),
            shape((rows, whole), BF),
            shape((half, whole), BF),
            shape((3, whole), F32),
        ],
        idx, hidden, ffn, ffn_back, text_cot, layout_cot, keep_rows, text_out_bias, layout_out_bias,
        text_gains, layout_gains, text_shifts, layout_shifts, smem=1,
    )
    grad_far = [exchange(grad_mine, mask) for mask in (1, 2, 3)]
    hidden_part, bias_t, bias_l = call(
        ffn_back_kernel,
        [shape((rows, whole), F32), shape((1, units), F32), shape((1, units_l), F32)],
        grad_low, slope_t, slope_l, text_up, text_down, layout_up, layout_down, flops=14 * 10**8,
    )
    first, attended_grad, sums_one = call(
        first_norm_kernel,
        [shape((rows, whole), F32), shape((rows, whole), BF), shape((3, whole), F32)],
        second, hidden_part, over_cores(hidden_part), normed, inverse, text_gains, layout_gains,
    )
    attended_grad_other = exchange(attended_grad, 1)

    low_parts, grad_parts = [low], [grad_low]
    for low_one, grad_one in zip(low_far, grad_far):
        low_parts += [low_one, over_cores(low_one)]
        grad_parts += [grad_one, over_cores(grad_one)]
    block = (2, wide // 4 + 16, width)
    up_keep, up_send, down_keep, down_send = call(
        unit_grads_kernel,
        [shape(block, F32), shape(block, BF)] * 2,
        idx, *low_parts, *grad_parts, text_up, text_down, layout_down, bias_up_t, quarter_up_l,
        quarter_ub_l,
        scratch=[
            pltpu.VMEM((4 * rows, whole), BF),
            pltpu.VMEM((4 * rows, whole), BF),
            pltpu.VMEM((wide, units // 4), BF),
            pltpu.VMEM((units // 4, wide), BF),
            pltpu.VMEM((quarter_l, thin), BF),
            pltpu.VMEM((4,) + block[1:], F32),
            pltpu.SemaphoreType.DMA((17,)),
        ],
        smem=1, anys=range(1, 18), flops=24 * 10**8,
    )
    up_own = reduced(up_keep, up_send)
    down_own = reduced(down_keep, down_send)

    keep, send, input_part, small = call(
        attention_back_kernel,
        [
            shape((4,) + block[1:], F32),
            shape((4,) + block[1:], BF),
            shape((rows, whole), F32),
            shape((16, 1024), F32),
        ],
        idx, q_own, k_all, v_all, text_in, layout_in, text_other, layout_other, *qkv_weights, keys,
        text_out, layout_out, attended_grad, attended_grad_other, sums_two, sums_one, bias_t, bias_l,
        scratch=[
            pltpu.VMEM((2 * rows, padded), BF),
            pltpu.VMEM((2 * rows, padded), BF),
            pltpu.VMEM((2 * rows, whole), BF),
            pltpu.VMEM((2 * rows, whole), BF),
            pltpu.VMEM((2 * rows, padded), BF),
            pltpu.VMEM((2 * rows, padded), BF),
            pltpu.VMEM((2 * rows, padded), BF),
            pltpu.VMEM((2 * rows, padded), BF),
            pltpu.VMEM((4, thin, LANES), F32),
            pltpu.VMEM((8,) + block[1:], F32),
        ],
        smem=1, flops=50 * 10**8,
    )
    input_total = input_part + over_cores(input_part)
    text_in_grad = (first[:, :wide] + input_total[:, :wide]).astype(BF)
    layout_in_grad = (first[:, wide:] + input_total[:, wide:]).astype(BF)
    plane = keep + exchange(send, 2).astype(F32)
    attention_own = reduced(
        jnp.stack([plane[0], plane[2]]), jnp.stack([plane[1], plane[3]]).astype(BF)
    )
    mask = 1
    while mask < lax.axis_size("seq"):
        small = small + exchange(small, mask)
        mask *= 2

    up_t, up_l = call(
        up_result_kernel,
        [shape(text_up.shape, F32), shape(layout_up.shape, F32)],
        idx, *gathered(up_own), scratch=[pltpu.VMEM((4, thin, LANES), F32)], smem=1,
    )
    down_t, down_l = call(
        down_result_kernel,
        [shape(text_down.shape, F32), shape(layout_down.shape, F32)],
        idx, *gathered(down_own), scratch=[pltpu.VMEM((4, thin, LANES), F32)], smem=1,
    )
    qkv_t, out_t, qkv_l, out_l = call(
        attention_result_kernel,
        [
            shape(text_qkv.shape, F32),
            shape(text_out.shape, F32),
            shape(layout_qkv.shape, F32),
            shape(layout_out.shape, F32),
        ],
        idx, *gathered(attention_own), scratch=[pltpu.VMEM((4, thin, LANES), F32)], smem=1,
    )
    room = small.shape[1]

    def rows_of(one, two):
        both = jnp.stack([small[one, :whole], small[two, :whole]])
        return both[:, :wide], both[:, wide:]

    gains_t, gains_l = rows_of(3, 0)
    shifts_t, shifts_l = rows_of(4, 1)
    out_bias_t, out_bias_l = rows_of(5, 2)
    up_bias_t = jnp.concatenate([small[6], small[7, : units - room]])
    up_bias_l = small[8, :units_l]
    qv_t, qv_l = small[9:11, :width], small[9:11, width : width + width_l]
    return (
        text_result,
        layout_result,
        text_in_grad,
        layout_in_grad,
        qkv_t,
        qv_t,
        out_t,
        out_bias_t,
        gains_t,
        shifts_t,
        up_t,
        up_bias_t,
        down_t,
        qkv_l,
        qv_l,
        out_l,
        out_bias_l,
        gains_l,
        shifts_l,
        up_l,
        up_bias_l,
        down_l,
    )


def solution(mesh):
    rows, both, halves = P("seq", None), P(), P("tensor", None)
    stack, columns, one = P(None, None, "tensor"), P(None, "tensor"), P("tensor")
    weights_in = (stack, columns, halves, both, both, both, columns, one, halves)
    return jax.shard_map(
        per_device,
        mesh=mesh,
        in_specs=(rows,) * 4 + (P("seq"),) * 3 + weights_in * 2,
        out_specs=(rows,) * 4 + weights_in * 2,
        check_vma=False,
    )
```

time: 659 us -> 266 us (0.40)
  waiting for transfers between devices: 417 us -> 97.7 us
  blocking collectives: 79.5 us -> 0 us
  matrix products: 67.6 us -> 0 us
  Pallas kernels: 0 us -> 48.8 us
  starting transfers between devices: 11.9 us -> 60.2 us
  other arithmetic: 37.7 us -> 12.4 us
  local copies, waits for them, and re-layouts: 28.9 us -> 44.2 us
  between operations: 15.1 us -> 1.52 us
    psum x5 -> x0, waiting for transfers between devices: 412 us -> none  [the longest x1 363 us: per_device(): lax.psum((text_qkv_grad, text_qv_bias_grad, text_out_grad, text_bias_one,...]
    ppermute x10 -> x55, waiting for transfers between devices: 4.54 us -> 97.7 us  [exchange(): lax.ppermute(shard, axis, [(i, i ^ mask) for i in range(lax.axis_size(axi...]
    psum x1 -> x0, blocking collectives: 79.5 us -> none  [per_device(): lax.psum((text_qkv_grad, text_qv_bias_grad, text_out_grad, text_bias_one,...]
    dot_general x39 -> x0, matrix products: 62.5 us -> none  [the longest x2 7.17 us: finish_attention(): jnp.dot(hidden_low, up_weight, preferred_element_type=jnp.float32) + up_bias]
    pallas_call x0 -> x11, Pallas kernels: none -> 48.8 us  [call(): pl.pallas_call(kernel, out_shape=tuple(outs), in_specs=specs, out_specs=t...]
    ppermute x10 -> x55, starting transfers between devices: 11.5 us -> 60.2 us  [exchange(): lax.ppermute(shard, axis, [(i, i ^ mask) for i in range(lax.axis_size(axi...]
    reduce_sum x18 -> x0, other arithmetic: 16.2 us -> none  [the longest x4 6.19 us: norm_backward(): jnp.sum(upstream * normed, axis=0)]
    unnamed x252 -> x166, local copies, waits for them, and re-layouts: 22.5 us -> 30.3 us
  transfers between devices with their start and end apart: 15 -> 55, of which waited for: 7 -> 20; matrix products, arithmetic and copies ran while one was open for 7% -> 10% of each run, Pallas kernels for 0% -> 14%
where the time goes in v1:
time: 266 us; the launch traced here: 265 us
  waiting for transfers between devices  97.7 us (37%)
  starting transfers between devices  60.2 us (23%)
  Pallas kernels  48.8 us (18%)
  local copies, waits for them, and re-layouts  44.2 us (17%)
  other arithmetic  12.4 us (5%)
    ppermute x55, waiting for transfers between devices, exchange(): lax.ppermute(shard, axis, [(i, i ^ mask) for i in range(lax.axis_size(axi...  97.7 us
    ppermute x55, starting transfers between devices, exchange(): lax.ppermute(shard, axis, [(i, i ^ mask) for i in range(lax.axis_size(axi...  60.2 us
    pallas_call x11, Pallas kernels, call(): pl.pallas_call(kernel, out_shape=tuple(outs), in_specs=specs, out_specs=t...  48.8 us
    unnamed x166, local copies, waits for them, and re-layouts  30.3 us
    ppermute x4, local copies, waits for them, and re-layouts, exchange(): lax.ppermute(shard, axis, [(i, i ^ mask) for i in range(lax.axis_size(axi...  6.88 us
  transfers between devices with their start and end apart: 55, of which 20 were waited for; matrix products, arithmetic and copies ran while one was open for 10% of the time, Pallas kernels for 14%

profile of v1, /device:TPU:0, one launch (start us, length us, event | category | flops | bytes accessed | tf_op | source)
XLA Modules:
  0.0 264.9 jit_solution(5562736546825400579)
XLA Ops:
  0.7 3.0 %collective-permute-start = (bf16[256,768]{1,0:T(8,128)(2,1)}, bf16[256,768]{1,0:T(8,128)(2,1)S(1)}, u32[]{:S(2)}, u32[]{:S(2)}) collective-permute-start(bf16[256,768]{1,0:T(8,128)(2,1)} %xt.5), channel_id=1, source_target_pairs={{0,2},{2,0},{4,6},{6,4},{8,10},{10,8},{12,14},{14,12},{16,18},{18,... | collective-permute-start | bytes 1179656 | tf_op jit(solution)/shard_map/ppermute | solution.py:20
  25.7 6.5 %shard_map.410 = (f32[256,960]{1,0:T(8,128)S(1)}, f32[256,960]{1,0:T(8,128)S(1)}, f32[256,256]{1,0:T(8,128)S(1)}, bf16[128,960]{1,0:T(8,128)(2,1)}, bf16[256,960...) custom-call(s32[4]{0:T(128)S(1)} %pad_add_fusion.idx, ...), custom_call_target="tpu_custom_call" | custom-call | flops 1400000000 | bytes 13401104 | tf_op jit(solution)/shard_map/pallas_call | solution.py:51
  36.3 2.7 %collective-permute-start.27 = (bf16[128,960]{1,0:T(8,128)(2,1)}, bf16[128,960]{1,0:T(8,128)(2,1)}, u32[]{:S(2)}, u32[]{:S(2)}) collective-permute-start(bf16[128,960]{1,0:T(8,128)(2,1)} %get-tuple-element.94), channel_id=1, source_target_pairs={{0,6},{2,4},{4,2},{6,0},{8,14},{10,12},{12,10},{14,8},{16,22},{18,... | collective-permute-start | bytes 737288 | tf_op jit(solution)/shard_map/ppermute | solution.py:20
  41.3 5.3 %collective-permute-done.27.refs_5_ = bf16[128,960]{1,0:T(8,128)(2,1)} collective-permute-done((bf16[128,960]{1,0:T(8,128)(2,1)}, bf16[128,960]{1,0:T(8,128)(2,1)}, u32[]{:S(2)}, u32[]{:S(2)}) %collective-permute-start.27) | collective-permute-done | bytes 245792 | tf_op jit(solution)/shard_map/ppermute | solution.py:20
  60.4 6.2 %collective-permute-done.33.refs_12_ = bf16[128,960]{1,0:T(8,128)(2,1)S(1)} collective-permute-done((bf16[128,960]{1,0:T(8,128)(2,1)}, bf16[128,960]{1,0:T(8,128)(2,1)S(1)}, u32[]{:S(2)}, u32[]{:S(2)}) %collective-permute-start.33) | collective-permute-done | bytes 245792 | tf_op jit(solution)/shard_map/ppermute | solution.py:20
  66.6 5.3 %collective-permute-done.31.refs_10_ = bf16[128,960]{1,0:T(8,128)(2,1)S(1)} collective-permute-done((bf16[128,960]{1,0:T(8,128)(2,1)}, bf16[128,960]{1,0:T(8,128)(2,1)S(1)}, u32[]{:S(2)}, u32[]{:S(2)}) %collective-permute-start.31) | collective-permute-done | bytes 245792 | tf_op jit(solution)/shard_map/ppermute | solution.py:20
  74.8 4.6 %shard_map.412 = (f32[256,960]{1,0:T(8,128)S(1)}, f32[1,1536]{1,0:T(1,128)S(1)}, f32[1,384]{1,0:T(1,128)S(1)}) custom-call(bf16[256,960]{1,0:T(8,128)(2,1)S(1)} %get-tuple-element.73.grad.refs_7_, f32[256,1536]{1,0:T(8,128)S(1)} %copy-done.5, f32[256,384]{1,0:T(8,128)S(1)} %copy-done.26, bf16[768,1536]{1,0:T(8,128)(2,1)} %refs_14_.1, ...), custom_call_target="tpu_custom_call" | custom-call | flops 1400000000 | bytes 8461824 | tf_op jit(solution)/shard_map/pallas_call | solution.py:51
  81.9 7.7 %shard_map.416 = (f32[2,208,384]{2,1,0:T(8,128)S(1)}, bf16[2,208,384]{2,1,0:T(8,128)(2,1)S(1)}, f32[2,208,384]{2,1,0:T(8,128)}, bf16[2,208,384]{2,1,0:T(8,128)(2,1)}) custom-call(s32[4]{0:T(128)S(1)} %pad_add_fusion.idx, bf16[256,960]{1,0:T(8,128)(2,1)S(1)} %copy-done.22, bf16[128,960]{1,0:T(8,128)(2,1)} %collective-permute-done.23.refs_1_, ...), custom_call_target="tpu_custom_call" | custom-call | flops 2400000000 | bytes 10755280 | tf_op jit(solution)/shard_map/pallas_call | solution.py:51
  91.7 8.4 %collective-permute-done.35 = bf16[2,208,384]{2,1,0:T(8,128)(2,1)S(1)} collective-permute-done((bf16[2,208,384]{2,1,0:T(8,128)(2,1)S(1)}, bf16[2,208,384]{2,1,0:T(8,128)(2,1)S(1)}, u32[]{:S(2)}, u32[]{:S(2)}) %collective-permute-start.35) | collective-permute-done | bytes 319520 | tf_op jit(solution)/shard_map/ppermute | solution.py:20
  110.2 8.2 %collective-permute-done.6.ag_p = bf16[256,960]{1,0:T(8,128)(2,1)S(1)} collective-permute-done((bf16[256,960]{1,0:T(8,128)(2,1)S(1)}, bf16[256,960]{1,0:T(8,128)(2,1)S(1)}, u32[]{:S(2)}, u32[]{:S(2)}) %collective-permute-start.6) | collective-permute-done | bytes 491552 | tf_op jit(solution)/shard_map/ppermute | solution.py:20
  118.5 12.7 %shard_map.414 = (f32[4,208,384]{2,1,0:T(8,128)}, bf16[4,208,384]{2,1,0:T(8,128)(2,1)S(1)}, f32[256,960]{1,0:T(8,128)S(1)}, f32[16,1024]{1,0:T(8,128)S(1)}) custom-call(s32[4]{0:T(128)S(1)} %pad_add_fusion.idx, bf16[256,512]{1,0:T(8,128)(2,1)S(1)} %copy-done.37, bf16[512,512]{1,0:T(8,128)(2,1)S(1)} %copy-done.64, bf16[512,512]{1,0:T(8,128)(2,1)S(1)} %copy-done.66, ...), custom_call_target="tpu_custom_call" | custom-call | flops 5000000000 | bytes 8783760 | tf_op jit(solution)/shard_map/pallas_call | solution.py:51
  136.3 10.0 %collective-permute-done.46 = bf16[208,384]{1,0:T(8,128)(2,1)S(1)} collective-permute-done((bf16[208,384]{1,0:T(8,128)(2,1)S(1)}, bf16[208,384]{1,0:T(8,128)(2,1)S(1)}, u32[]{:S(2)}, u32[]{:S(2)}) %collective-permute-start.46) | collective-permute-done | bytes 159776 | tf_op jit(solution)/shard_map/ppermute | solution.py:20
  147.7 3.0 %collective-permute-start.9 = (bf16[2,208,384]{2,1,0:T(8,128)(2,1)S(1)}, bf16[2,208,384]{2,1,0:T(8,128)(2,1)S(1)}, u32[]{:S(2)}, u32[]{:S(2)}) collective-permute-start(bf16[2,208,384]{2,1,0:T(8,128)(2,1)S(1)} %pad_maximum_fusion), channel_id=1, source_target_pairs={{0,8},{2,10},{4,12},{6,14},{8,0},{10,2},{12,4},{14,6},{16,24},{18,... | collective-permute-start | bytes 958472 | tf_op jit(solution)/shard_map/ppermute | solution.py:20
  153.0 7.0 %collective-permute-done.9 = bf16[2,208,384]{2,1,0:T(8,128)(2,1)S(1)} collective-permute-done((bf16[2,208,384]{2,1,0:T(8,128)(2,1)S(1)}, bf16[2,208,384]{2,1,0:T(8,128)(2,1)S(1)}, u32[]{:S(2)}, u32[]{:S(2)}) %collective-permute-start.9) | collective-permute-done | bytes 319520 | tf_op jit(solution)/shard_map/ppermute | solution.py:20
  166.5 9.0 %collective-permute-done.21 = f32[16,1024]{1,0:T(8,128)S(1)} collective-permute-done((f32[16,1024]{1,0:T(8,128)S(1)}, f32[16,1024]{1,0:T(8,128)S(1)}, u32[]{:S(2)}, u32[]{:S(2)}) %collective-permute-start.21) | collective-permute-done | bytes 65568 | tf_op jit(solution)/shard_map/ppermute | solution.py:20
  182.0 3.9 %collective-permute-done.22 = f32[16,1024]{1,0:T(8,128)S(1)} collective-permute-done((f32[16,1024]{1,0:T(8,128)S(1)}, f32[16,1024]{1,0:T(8,128)S(1)}, u32[]{:S(2)}, u32[]{:S(2)}) %collective-permute-start.22) | collective-permute-done | bytes 65568 | tf_op jit(solution)/shard_map/ppermute | solution.py:20
  186.5 3.4 %collective-permute-start.11 = (bf16[208,384]{1,0:T(8,128)(2,1)}, bf16[208,384]{1,0:T(8,128)(2,1)}, u32[]{:S(2)}, u32[]{:S(2)}) collective-permute-start(bf16[208,384]{1,0:T(8,128)(2,1)} %fusion.6), channel_id=1, source_target_pairs={{0,16},{2,18},{4,20},{6,22},{8,24},{10,26},{12,28},{14,30},{16,0},... | collective-permute-start | bytes 479240 | tf_op jit(solution)/shard_map/ppermute | solution.py:20
  200.8 3.5 %collective-permute-done.43.refs_6_ = bf16[2,208,384]{2,1,0:T(8,128)(2,1)S(1)} collective-permute-done((bf16[2,208,384]{2,1,0:T(8,128)(2,1)S(1)}, bf16[2,208,384]{2,1,0:T(8,128)(2,1)S(1)}, u32[]{:S(2)}, u32[]{:S(2)}) %collective-permute-start.43) | collective-permute-done | bytes 319520 | tf_op jit(solution)/shard_map/ppermute | solution.py:20
  205.3 12.4 %collective-permute-done.52.refs_5_ = bf16[2,208,384]{2,1,0:T(8,128)(2,1)S(1)} collective-permute-done((bf16[2,208,384]{2,1,0:T(8,128)(2,1)S(1)}, bf16[2,208,384]{2,1,0:T(8,128)(2,1)S(1)}, u32[]{:S(2)}, u32[]{:S(2)}) %collective-permute-start.52) | collective-permute-done | bytes 319520 | tf_op jit(solution)/shard_map/ppermute | solution.py:20
  223.4 4.7 %collective-permute-done.54.refs_7_ = bf16[2,208,384]{2,1,0:T(8,128)(2,1)S(1)} collective-permute-done((bf16[2,208,384]{2,1,0:T(8,128)(2,1)S(1)}, bf16[2,208,384]{2,1,0:T(8,128)(2,1)S(1)}, u32[]{:S(2)}, u32[]{:S(2)}) %collective-permute-start.54) | collective-permute-done | bytes 319520 | tf_op jit(solution)/shard_map/ppermute | solution.py:20
  233.5 3.2 %shard_map.418 = (f32[1536,768]{1,0:T(8,128)}, f32[384,192]{1,0:T(8,128)S(1)}) custom-call(s32[4]{0:T(128)S(1)} %pad_add_fusion.idx, bf16[2,208,384]{2,1,0:T(8,128)(2,1)S(1)} %pad_maximum_fusion.3.refs_0_, bf16[2,208,384]{2,1,0:T(8,128)(2,1)S(1)} %copy-done.33, bf16[2,208,384]{2,1,0:T(8,128)(2,1)S(1)} %collective-permute-done.49.refs_2_, ...), custom_call_target="tpu_custom_call" | custom-call | flops 100000000 | bytes 7569424 | tf_op jit(solution)/shard_map/pallas_call | solution.py:51
  237.6 3.1 %collective-permute-done.44.refs_7_ = bf16[2,208,384]{2,1,0:T(8,128)(2,1)} collective-permute-done((bf16[2,208,384]{2,1,0:T(8,128)(2,1)}, bf16[2,208,384]{2,1,0:T(8,128)(2,1)}, u32[]{:S(2)}, u32[]{:S(2)}) %collective-permute-start.44) | collective-permute-done | bytes 319520 | tf_op jit(solution)/shard_map/ppermute | solution.py:20
  241.7 3.8 %shard_map.417 = (f32[768,1536]{1,0:T(8,128)}, f32[192,384]{1,0:T(8,128)}) custom-call(s32[4]{0:T(128)S(1)} %pad_add_fusion.idx, bf16[2,208,384]{2,1,0:T(8,128)(2,1)S(1)} %pad_maximum_fusion.2.refs_0_, bf16[2,208,384]{2,1,0:T(8,128)(2,1)S(1)} %collective-permute-done.38.refs_1_, bf16[2,208,384]{2,1,0:T(8,128)(2,1)S(1)} %collective-permute-done.39.refs_2_, ...), custom_call_target="tpu_custom_call" | custom-call | flops 100000000 | bytes 7569424 | tf_op jit(solution)/shard_map/pallas_call | solution.py:51
  261.3 3.6 %shard_map.415 = (f32[3,768,384]{2,1,0:T(8,128)}, f32[384,768]{1,0:T(8,128)}, f32[3,192,96]{2,1,0:T(8,128)}, f32[96,192]{1,0:T(8,128)}) custom-call(s32[4]{0:T(128)S(1)} %pad_add_fusion.idx, bf16[2,208,384]{2,1,0:T(8,128)(2,1)S(1)} %pad_maximum_fusion.1.refs_0_, bf16[2,208,384]{2,1,0:T(8,128)(2,1)} %collective-permute-done.12.refs_1_, ...), custom_call_target="tpu_custom_call" | custom-call | flops 100000000 | bytes 7569424 | tf_op jit(solution)/shard_map/pallas_call | solution.py:51
  (314 shorter events, 122.4 us)
Async XLA Ops:
  39.0 20.6 %collective-permute-start.25 = (bf16[128,960]{1,0:T(8,128)(2,1)}, bf16[128,960]{1,0:T(8,128)(2,1)}, u32[]{:S(2)}, u32[]{:S(2)}) collective-permute-start(bf16[128,960]{1,0:T(8,128)(2,1)} %get-tuple-element.94), channel_id=1, source_target_pairs={{0,4},{2,6},{4,0},{6,2},{8,12},{10,14},{12,8},{14,10},{16,20},{18,... | collective-permute-start | bytes 737288 | tf_op jit(solution)/shard_map/ppermute | solution.py:20
  39.5 20.4 %collective-permute-start.23 = (bf16[128,960]{1,0:T(8,128)(2,1)}, bf16[128,960]{1,0:T(8,128)(2,1)}, u32[]{:S(2)}, u32[]{:S(2)}) collective-permute-start(bf16[128,960]{1,0:T(8,128)(2,1)} %get-tuple-element.94), channel_id=1, source_target_pairs={{0,2},{2,0},{4,6},{6,4},{8,10},{10,8},{12,14},{14,12},{16,18},{18,... | collective-permute-start | bytes 737288 | tf_op jit(solution)/shard_map/ppermute | solution.py:20
  59.9 21.4 %collective-permute-start.26 = (bf16[128,960]{1,0:T(8,128)(2,1)}, bf16[128,960]{1,0:T(8,128)(2,1)}, u32[]{:S(2)}, u32[]{:S(2)}) collective-permute-start(bf16[128,960]{1,0:T(8,128)(2,1)} %collective-permute-done.25.refs_3_), channel_id=1, source_target_pairs={{0,1},{1,0},{2,3},{3,2},{4,5},{5,4},{6,7},{7,6},{8,9},{9,8},{10,11... | collective-permute-start | bytes 737288 | tf_op jit(solution)/shard_map/ppermute | solution.py:20
  59.9 22.0 %collective-permute-start.24 = (bf16[128,960]{1,0:T(8,128)(2,1)}, bf16[128,960]{1,0:T(8,128)(2,1)}, u32[]{:S(2)}, u32[]{:S(2)}) collective-permute-start(bf16[128,960]{1,0:T(8,128)(2,1)} %collective-permute-done.23.refs_1_), channel_id=1, source_target_pairs={{0,1},{1,0},{2,3},{3,2},{4,5},{5,4},{6,7},{7,6},{8,9},{9,8},{10,11... | collective-permute-start | bytes 737288 | tf_op jit(solution)/shard_map/ppermute | solution.py:20
  81.3 19.6 %collective-permute-start.5 = (f32[256,960]{0,1:T(8,128)}, f32[256,960]{0,1:T(8,128)}, u32[]{:S(2)}, u32[]{:S(2)}) collective-permute-start(f32[256,960]{0,1:T(8,128)} %copy.81), channel_id=1, source_target_pairs={{0,1},{1,0},{2,3},{3,2},{4,5},{5,4},{6,7},{7,6},{8,9},{9,8},{10,11... | collective-permute-start | bytes 2949128 | tf_op jit(solution)/shard_map/ppermute | solution.py:20
  91.2 18.9 %collective-permute-start.45 = (bf16[2,208,384]{2,1,0:T(8,128)(2,1)}, bf16[2,208,384]{2,1,0:T(8,128)(2,1)S(1)}, u32[]{:S(2)}, u32[]{:S(2)}) collective-permute-start(bf16[2,208,384]{2,1,0:T(8,128)(2,1)} %get-tuple-element.100), channel_id=1, source_target_pairs={{0,8},{2,10},{4,12},{6,14},{8,0},{10,2},{12,4},{14,6},{16,24},{18,... | collective-permute-start | bytes 958472 | tf_op jit(solution)/shard_map/ppermute | solution.py:20
  107.5 28.4 %collective-permute-start.36 = (bf16[208,384]{1,0:T(8,128)(2,1)S(1)}, bf16[208,384]{1,0:T(8,128)(2,1)S(1)}, u32[]{:S(2)}, u32[]{:S(2)}) collective-permute-start(bf16[208,384]{1,0:T(8,128)(2,1)S(1)} %fusion.9), channel_id=1, source_target_pairs={{0,16},{2,18},{4,20},{6,22},{8,24},{10,26},{12,28},{14,30},{16,0},... | collective-permute-start | bytes 479240 | tf_op jit(solution)/shard_map/ppermute | solution.py:20
  131.2 16.1 %collective-permute-start.8 = (bf16[4,208,384]{2,1,0:T(8,128)(2,1)S(1)}, bf16[4,208,384]{2,1,0:T(8,128)(2,1)S(1)}, u32[]{:S(2)}, u32[]{:S(2)}) collective-permute-start(bf16[4,208,384]{2,1,0:T(8,128)(2,1)S(1)} %get-tuple-element.89), channel_id=1, source_target_pairs={{0,4},{2,6},{4,0},{6,2},{8,12},{10,14},{12,8},{14,10},{16,20},{18,... | collective-permute-start | bytes 1916936 | tf_op jit(solution)/shard_map/ppermute | solution.py:20
  146.4 20.0 %collective-permute-start.47 = (bf16[208,384]{1,0:T(8,128)(2,1)S(1)}, bf16[208,384]{1,0:T(8,128)(2,1)S(1)}, u32[]{:S(2)}, u32[]{:S(2)}) collective-permute-start(bf16[208,384]{1,0:T(8,128)(2,1)S(1)} %fusion.2), channel_id=1, source_target_pairs={{0,16},{2,18},{4,20},{6,22},{8,24},{10,26},{12,28},{14,30},{16,0},... | collective-permute-start | bytes 479240 | tf_op jit(solution)/shard_map/ppermute | solution.py:20
  150.7 26.6 %collective-permute-start.41 = (bf16[2,208,384]{2,1,0:T(8,128)(2,1)S(1)}, bf16[2,208,384]{2,1,0:T(8,128)(2,1)S(1)}, u32[]{:S(2)}, u32[]{:S(2)}) collective-permute-start(bf16[2,208,384]{2,1,0:T(8,128)(2,1)S(1)} %pad_maximum_fusion.2.refs_0_), channel_id=1, source_target_pairs={{0,4},{2,6},{4,0},{6,2},{8,12},{10,14},{12,8},{14,10},{16,20},{18,... | collective-permute-start | bytes 958472 | tf_op jit(solution)/shard_map/ppermute | solution.py:20
  160.1 18.5 %collective-permute-start.10 = (bf16[208,384]{1,0:T(8,128)(2,1)S(1)}, bf16[208,384]{1,0:T(8,128)(2,1)S(1)}, u32[]{:S(2)}, u32[]{:S(2)}) collective-permute-start(bf16[208,384]{1,0:T(8,128)(2,1)S(1)} %fusion.8), channel_id=1, source_target_pairs={{0,16},{2,18},{4,20},{6,22},{8,24},{10,26},{12,28},{14,30},{16,0},... | collective-permute-start | bytes 479240 | tf_op jit(solution)/shard_map/ppermute | solution.py:20
  162.7 30.4 %collective-permute-start.39 = (bf16[2,208,384]{2,1,0:T(8,128)(2,1)S(1)}, bf16[2,208,384]{2,1,0:T(8,128)(2,1)S(1)}, u32[]{:S(2)}, u32[]{:S(2)}) collective-permute-start(bf16[2,208,384]{2,1,0:T(8,128)(2,1)S(1)} %pad_maximum_fusion.2.refs_0_), channel_id=1, source_target_pairs={{0,2},{2,0},{4,6},{6,4},{8,10},{10,8},{12,14},{14,12},{16,18},{18,... | collective-permute-start | bytes 958472 | tf_op jit(solution)/shard_map/ppermute | solution.py:20
  163.9 29.9 %collective-permute-start.38 = (bf16[2,208,384]{2,1,0:T(8,128)(2,1)S(1)}, bf16[2,208,384]{2,1,0:T(8,128)(2,1)S(1)}, u32[]{:S(2)}, u32[]{:S(2)}) collective-permute-start(bf16[2,208,384]{2,1,0:T(8,128)(2,1)S(1)} %pad_maximum_fusion.2.refs_0_), channel_id=1, source_target_pairs={{0,8},{2,10},{4,12},{6,14},{8,0},{10,2},{12,4},{14,6},{16,24},{18,... | collective-permute-start | bytes 958472 | tf_op jit(solution)/shard_map/ppermute | solution.py:20
  175.5 18.6 %collective-permute-start.51 = (bf16[2,208,384]{2,1,0:T(8,128)(2,1)S(1)}, bf16[2,208,384]{2,1,0:T(8,128)(2,1)S(1)}, u32[]{:S(2)}, u32[]{:S(2)}) collective-permute-start(bf16[2,208,384]{2,1,0:T(8,128)(2,1)S(1)} %pad_maximum_fusion.3.refs_0_), channel_id=1, source_target_pairs={{0,4},{2,6},{4,0},{6,2},{8,12},{10,14},{12,8},{14,10},{16,20},{18,... | collective-permute-start | bytes 958472 | tf_op jit(solution)/shard_map/ppermute | solution.py:20
  177.2 19.3 %collective-permute-start.48 = (bf16[2,208,384]{2,1,0:T(8,128)(2,1)S(1)}, bf16[2,208,384]{2,1,0:T(8,128)(2,1)S(1)}, u32[]{:S(2)}, u32[]{:S(2)}) collective-permute-start(bf16[2,208,384]{2,1,0:T(8,128)(2,1)S(1)} %pad_maximum_fusion.3.refs_0_), channel_id=1, source_target_pairs={{0,8},{2,10},{4,12},{6,14},{8,0},{10,2},{12,4},{14,6},{16,24},{18,... | collective-permute-start | bytes 958472 | tf_op jit(solution)/shard_map/ppermute | solution.py:20
  194.8 24.0 %collective-permute-start.42 = (bf16[2,208,384]{2,1,0:T(8,128)(2,1)S(1)}, bf16[2,208,384]{2,1,0:T(8,128)(2,1)}, u32[]{:S(2)}, u32[]{:S(2)}) collective-permute-start(bf16[2,208,384]{2,1,0:T(8,128)(2,1)S(1)} %collective-permute-done.38.refs_1_), channel_id=1, source_target_pairs={{0,4},{2,6},{4,0},{6,2},{8,12},{10,14},{12,8},{14,10},{16,20},{18,... | collective-permute-start | bytes 958472 | tf_op jit(solution)/shard_map/ppermute | solution.py:20
  196.6 21.1 %collective-permute-start.52 = (bf16[2,208,384]{2,1,0:T(8,128)(2,1)S(1)}, bf16[2,208,384]{2,1,0:T(8,128)(2,1)S(1)}, u32[]{:S(2)}, u32[]{:S(2)}) collective-permute-start(bf16[2,208,384]{2,1,0:T(8,128)(2,1)S(1)} %collective-permute-done.48.refs_1_), channel_id=1, source_target_pairs={{0,4},{2,6},{4,0},{6,2},{8,12},{10,14},{12,8},{14,10},{16,20},{18,... | collective-permute-start | bytes 958472 | tf_op jit(solution)/shard_map/ppermute | solution.py:20
  196.9 48.6 %collective-permute-start.7 = (f32[256,960]{0,1:T(8,128)}, f32[256,960]{0,1:T(8,128)}, u32[]{:S(2)}, u32[]{:S(2)}) collective-permute-start(f32[256,960]{0,1:T(8,128)} %copy.84), channel_id=1, source_target_pairs={{0,1},{1,0},{2,3},{3,2},{4,5},{5,4},{6,7},{7,6},{8,9},{9,8},{10,11... | collective-permute-start | bytes 2949128 | tf_op jit(solution)/shard_map/ppermute | solution.py:20
  200.1 22.1 %collective-permute-start.50 = (bf16[2,208,384]{2,1,0:T(8,128)(2,1)S(1)}, bf16[2,208,384]{2,1,0:T(8,128)(2,1)S(1)}, u32[]{:S(2)}, u32[]{:S(2)}) collective-permute-start(bf16[2,208,384]{2,1,0:T(8,128)(2,1)S(1)} %collective-permute-done.48.refs_1_), channel_id=1, source_target_pairs={{0,2},{2,0},{4,6},{6,4},{8,10},{10,8},{12,14},{14,12},{16,18},{18,... | collective-permute-start | bytes 958472 | tf_op jit(solution)/shard_map/ppermute | solution.py:20
  205.0 16.3 %collective-permute-start.53 = (bf16[2,208,384]{2,1,0:T(8,128)(2,1)S(1)}, bf16[2,208,384]{2,1,0:T(8,128)(2,1)S(1)}, u32[]{:S(2)}, u32[]{:S(2)}) collective-permute-start(bf16[2,208,384]{2,1,0:T(8,128)(2,1)S(1)} %collective-permute-done.49.refs_2_), channel_id=1, source_target_pairs={{0,4},{2,6},{4,0},{6,2},{8,12},{10,14},{12,8},{14,10},{16,20},{18,... | collective-permute-start | bytes 958472 | tf_op jit(solution)/shard_map/ppermute | solution.py:20
  221.4 16.2 %collective-permute-start.40 = (bf16[2,208,384]{2,1,0:T(8,128)(2,1)S(1)}, bf16[2,208,384]{2,1,0:T(8,128)(2,1)}, u32[]{:S(2)}, u32[]{:S(2)}) collective-permute-start(bf16[2,208,384]{2,1,0:T(8,128)(2,1)S(1)} %collective-permute-done.38.refs_1_), channel_id=1, source_target_pairs={{0,2},{2,0},{4,6},{6,4},{8,10},{10,8},{12,14},{14,12},{16,18},{18,... | collective-permute-start | bytes 958472 | tf_op jit(solution)/shard_map/ppermute | solution.py:20
  222.3 18.5 %collective-permute-start.44 = (bf16[2,208,384]{2,1,0:T(8,128)(2,1)}, bf16[2,208,384]{2,1,0:T(8,128)(2,1)}, u32[]{:S(2)}, u32[]{:S(2)}) collective-permute-start(bf16[2,208,384]{2,1,0:T(8,128)(2,1)} %collective-permute-done.42.refs_5_), channel_id=1, source_target_pairs={{0,2},{2,0},{4,6},{6,4},{8,10},{10,8},{12,14},{14,12},{16,18},{18,... | collective-permute-start | bytes 958472 | tf_op jit(solution)/shard_map/ppermute | solution.py:20
  228.1 24.1 %collective-permute-start.13 = (bf16[2,208,384]{2,1,0:T(8,128)(2,1)S(1)}, bf16[2,208,384]{2,1,0:T(8,128)(2,1)}, u32[]{:S(2)}, u32[]{:S(2)}) collective-permute-start(bf16[2,208,384]{2,1,0:T(8,128)(2,1)S(1)} %pad_maximum_fusion.1.refs_0_), channel_id=1, source_target_pairs={{0,2},{2,0},{4,6},{6,4},{8,10},{10,8},{12,14},{14,12},{16,18},{18,... | collective-permute-start | bytes 958472 | tf_op jit(solution)/shard_map/ppermute | solution.py:20
  229.3 24.1 %collective-permute-start.16 = (bf16[2,208,384]{2,1,0:T(8,128)(2,1)}, bf16[2,208,384]{2,1,0:T(8,128)(2,1)}, u32[]{:S(2)}, u32[]{:S(2)}) collective-permute-start(bf16[2,208,384]{2,1,0:T(8,128)(2,1)} %collective-permute-done.12.refs_1_), channel_id=1, source_target_pairs={{0,4},{2,6},{4,0},{6,2},{8,12},{10,14},{12,8},{14,10},{16,20},{18,... | collective-permute-start | bytes 958472 | tf_op jit(solution)/shard_map/ppermute | solution.py:20
  (111 other events, 814.6 us)

commit v2 on v1

v2 whole, which is shorter than its diff:
```python
from functools import partial

import jax
import jax.numpy as jnp
from jax import lax
from jax.experimental import pallas as pl
from jax.experimental.pallas import tpu as pltpu
from jax.sharding import PartitionSpec as P

HT = 64
HL = 16
EPS = 1e-06
NEG = -1e30
BF = jnp.bfloat16
F32 = jnp.float32
LANES = 128


def exchange(shard, mask, axis="seq"):
    return lax.ppermute(shard, axis, [(i, i ^ mask) for i in range(lax.axis_size(axis))])


def over_cores(shard):
    return exchange(shard, 1, "tensor")


def dot(left, right):
    return lax.dot_general(left, right, (((1,), (0,)), ((), ())), preferred_element_type=F32)


def dot_nt(left, right):
    return lax.dot_general(left, right, (((1,), (1,)), ((), ())), preferred_element_type=F32)


def dot_tn(left, right):
    return lax.dot_general(left, right, (((0,), (0,)), ((), ())), preferred_element_type=F32)


def tied(shard, token):
    return lax.optimization_barrier((shard, token))[0]


def call(kernel, outs, *args, scratch=(), smem=0, anys=(), far=(), pin=(), after=(), flops=10**8, room=16):
    far, pin = list(far), list(pin)
    n_in = len(args)
    args = (*args, *after)
    specs, given = [], []
    for at, arg in enumerate(args):
        if at < smem:
            specs.append(pl.BlockSpec(memory_space=pltpu.SMEM))
        elif at in far:
            specs.append(pl.BlockSpec(memory_space=pltpu.HBM))
            arg = pltpu.with_memory_space_constraint(arg, pltpu.HBM)
        elif at in anys or at >= n_in:
            specs.append(pl.BlockSpec(memory_space=pl.ANY))
        else:
            specs.append(pl.BlockSpec(memory_space=pltpu.VMEM))
        if isinstance(arg, Near):
            arg = pltpu.with_memory_space_constraint(arg.value, pltpu.VMEM)
        given.append(arg)
    moved = sum(a.size * a.dtype.itemsize for a in args) + sum(
        o.size * o.dtype.itemsize for o in outs
    )
    stage = [pltpu.VMEM(args[k].shape, args[k].dtype) for k in far]
    if stage:
        stage.append(pltpu.SemaphoreType.DMA((len(far),)))

    def body(*refs):
        refs = list(refs[:n_in] + refs[len(args) :])
        if not stage:
            return kernel(*refs)
        held, sems = refs[-len(stage) : -1], refs[-1]
        refs = refs[: -len(stage)]
        coming = [
            pltpu.make_async_copy(refs[k], held[at], sems.at[at]) for at, k in enumerate(far)
        ]
        for copy in coming:
            copy.start()
        for copy in coming:
            copy.wait()
        for at, k in enumerate(far):
            refs[k] = held[at]
        kernel(*refs)

    found = pl.pallas_call(
        body,
        out_shape=tuple(
            pltpu.VMEM(o.shape, o.dtype) if k in pin else o for k, o in enumerate(outs)
        ),
        in_specs=specs,
        out_specs=tuple(pl.BlockSpec(memory_space=pltpu.VMEM) for _ in outs),
        scratch_shapes=list(scratch) + stage,
        compiler_params=pltpu.CompilerParams(vmem_limit_bytes=room * 1024 * 1024),
        cost_estimate=pl.CostEstimate(flops=flops, bytes_accessed=moved, transcendentals=0),
    )(*given)
    return tuple(Near(a) if k in pin else a for k, a in enumerate(found))


class Near:
    def __init__(self, value):
        self.value = value
        self.shape, self.dtype, self.size = value.shape, value.dtype, value.size


def shape(dims, dtype):
    return jax.ShapeDtypeStruct(tuple(dims), dtype)


def project_rows(text_rows, layout_columns, weight_t, bias_t, weight_l, bias_l, which, write):
    text_part = dot(text_rows, weight_t[which])
    layout_part = dot_tn(layout_columns, weight_l[which])
    if which != 1:
        row = which // 2
        text_part = text_part + bias_t[row : row + 1, :].astype(F32)
        layout_part = layout_part + bias_l[row : row + 1, :].astype(F32)
    pad = jnp.zeros((layout_part.shape[0], LANES - layout_part.shape[1]), F32)
    write(text_part.astype(BF), jnp.concatenate([layout_part, pad], axis=1).astype(BF))


def turned(matrix):
    rows, columns = matrix.shape
    matrix = matrix.astype(F32)
    if columns % LANES:
        fill = jnp.zeros((rows, -columns % LANES), F32)
        matrix = jnp.concatenate([matrix, fill], axis=1)
    if rows % LANES:
        fill = jnp.zeros((-rows % LANES, matrix.shape[1]), F32)
        matrix = jnp.concatenate([matrix, fill], axis=0)
    return matrix.T[:columns, :rows]


OB, GAIN, SHIFT, UP_T, UP_L, UP_Q = 0, 2, 4, 6, 7, 8


def pack_kernel(
    idx, cl, flags, ob_t, g_t, s_t, ub_t, ob_l, g_l, s_l, ub_l, up_l, dn_l,
    cl_out, keep_out, pack_out, quarter_out,
):
    wide, thin = ob_t.shape[1], ob_l.shape[1]
    pack_out[...] = jnp.zeros_like(pack_out)
    for first, text, layout in ((OB, ob_t, ob_l), (GAIN, g_t, g_l), (SHIFT, s_t, s_l)):
        pack_out[first : first + 2, :wide] = text[...].astype(F32)
        pack_out[first : first + 2, wide : wide + thin] = layout[...].astype(F32)
    pack_out[UP_T : UP_T + 1, :] = ub_t[...].astype(F32)
    pack_out[UP_L : UP_L + 1, : ub_l.shape[1]] = ub_l[...].astype(F32)
    quarter = idx[1] * 2 + idx[0]
    count = up_l.shape[1] // 4

    def cut(ref):
        value = ref[:, :count].astype(F32)
        for q in range(1, 4):
            value = jnp.where(quarter == q, ref[:, count * q : count * (q + 1)].astype(F32), value)
        return value

    pack_out[UP_Q : UP_Q + 1, :count] = cut(ub_l)
    quarter_out[:, :count] = cut(up_l).astype(BF)
    quarter_out[:, LANES : LANES + count] = cut(dn_l).astype(BF)
    cl_out[...] = turned(cl[...]).astype(BF)
    keep_out[...] = jnp.broadcast_to((1 - flags[...]).astype(F32), (LANES, flags.shape[1])).T


def project_kernel(xt, xl, wt, bt, wl, bl, q_out, k_out, v_out, xl_out):
    xl_out[...] = turned(xl[...]).astype(BF)
    width = wt.shape[2]
    for which, out in enumerate((q_out, k_out, v_out)):

        def write(text_part, layout_part, out=out):
            out[:, :width] = text_part
            out[:, width:] = layout_part

        project_rows(xt[...], xl[...], wt, bt, wl, bl, which, write)


def hidden_bias(keys, columns):
    rows = keys.shape[1]
    down = jnp.broadcast_to(keys, (LANES, rows)).T
    parts = [
        jnp.where(down == keys[:, at : at + LANES], 0.0, NEG).astype(F32)
        for at in range(0, columns, LANES)
    ]
    return jnp.concatenate(parts, axis=1)


def head_mask(member, head, text_value, layout_value, axis):
    dims = (1, 2 * LANES) if axis == 1 else (2 * LANES, 1)
    at = lax.broadcasted_iota(jnp.int32, dims, axis)
    text = (at >= member * HT) & (at < (member + 1) * HT)
    layout = (at >= LANES + head * HL) & (at < LANES + (head + 1) * HL)
    return jnp.where(text, text_value, jnp.where(layout, layout_value, 0.0)).astype(F32)


def pair_of(ref, pair, width):
    return jnp.concatenate([ref[:, LANES * pair : LANES * (pair + 1)], ref[:, width:]], axis=1)


def probabilities(key_pair, query_head, bias):
    scores = dot_nt(key_pair, query_head) + bias
    weights = jnp.exp(scores - jnp.max(scores, axis=0, keepdims=True))
    return weights * (1.0 / jnp.sum(weights, axis=0, keepdims=True))


OB, GAIN, SHIFT, UP_T, UP_L, UP_Q = 0, 2, 4, 6, 7, 8
SCALE_T = HT ** (-0.5)
SCALE_L = HL ** (-0.5)


def attend_kernel(
    q_own, k_own, v_own, xt, xl, wt, bt, wl, bl, keys, out_t, out_l, part_out, k_all, v_all, context,
):
    rows, width = q_own.shape[0], wt.shape[2]
    for which, own, target in ((1, k_own, k_all), (2, v_own, v_all)):
        target[:rows, :] = own[...]

        def write(text_part, layout_part, target=target):
            target[rows:, :width] = text_part
            target[rows:, width:] = layout_part

        project_rows(xt[...], xl[...], wt, bt, wl, bl, which, write)
    bias = hidden_bias(keys[...], rows)
    layout_sum = jnp.zeros((LANES, rows), F32)
    for pair in range(width // LANES):
        query_pair, key_pair = pair_of(q_own, pair, width), pair_of(k_all, pair, width)
        value_turned = pair_of(v_all, pair, width).T
        text_sum = jnp.zeros((LANES, rows), F32)
        for member in range(2):
            head = 2 * pair + member
            mask = head_mask(member, head, SCALE_T, SCALE_L, 1).astype(BF)
            probs_low = probabilities(key_pair, query_pair * mask, bias).astype(BF)
            turned = dot(value_turned, probs_low) * head_mask(member, head, 1.0, 1.0, 0)
            text_sum += turned[:LANES]
            layout_sum += turned[LANES:]
        context[:, LANES * pair : LANES * (pair + 1)] = text_sum.T.astype(BF)
    context[:, width:] = layout_sum.T.astype(BF)
    text_width = out_t.shape[1]
    part_out[:, :text_width] = dot(context[:, :width], out_t[...])
    part_out[:, text_width : text_width + out_l.shape[1]] = dot(
        context[:, width : width + out_l.shape[0]], out_l[...]
    )


def norm_parts(total):
    center = total - jnp.mean(total, axis=1, keepdims=True)
    inverse = lax.rsqrt(jnp.mean(center * center, axis=1, keepdims=True) + EPS)
    return center * inverse, inverse


def norm_back(upstream, normed, inverse, gain):
    scaled = upstream * gain
    return inverse * (
        scaled
        - jnp.mean(scaled, axis=1, keepdims=True)
        - normed * jnp.mean(scaled * normed, axis=1, keepdims=True)
    )


def gelu_parts(before):
    share = 0.5 * (1.0 + lax.erf(before * (0.5**0.5)))
    slope = share + before * (jnp.exp(-0.5 * before * before) * 0.3989422804014327)
    return before * share, slope


def norm_kernel(
    idx, xt, xl, part, back, pack, hidden_out, normed_out, inverse_out, mine_out, low_out
):
    width, whole, half = xt.shape[1], hidden_out.shape[1], mine_out.shape[0]
    for at, (lo, hi, x) in enumerate(((0, width, xt), (width, whole, xl))):
        total = x[...].astype(F32) + (part[:, lo:hi] + back[:, lo:hi]) + pack[OB : OB + 1, lo:hi]
        normed, inverse = norm_parts(total)
        hidden = normed * pack[GAIN : GAIN + 1, lo:hi] + pack[SHIFT : SHIFT + 1, lo:hi]
        hidden_out[:, lo:hi] = hidden
        normed_out[:, lo:hi] = normed
        inverse_out[:, LANES * at : LANES * (at + 1)] = jnp.broadcast_to(
            inverse, (inverse.shape[0], LANES)
        )
        low_out[:, lo:hi] = hidden.astype(BF)
    mine_out[...] = low_out[pl.ds(pl.multiple_of(idx[3] * half, half), half), :]


def ffn_kernel(low, pack, up_t, dn_t, up_l, dn_l, slope_t, slope_l, ffn_out):
    width = up_t.shape[0]
    whole = width + up_l.shape[0]
    for lo, hi, up, ub, dn, slope_out in (
        (0, width, up_t, UP_T, dn_t, slope_t),
        (width, whole, up_l, UP_L, dn_l, slope_l),
    ):
        rows_low = low[:, lo:hi]
        units = up.shape[1]
        step = min(units, 384)
        total = None
        for cut in range(0, units, step):
            before = dot(rows_low, up[:, cut : cut + step]) + pack[ub : ub + 1, cut : cut + step]
            activated, slope = gelu_parts(before)
            slope_out[:, cut : cut + step] = slope
            if lo == 0:
                term = dot(activated.astype(BF), dn[cut : cut + step, :])
            else:
                term = dot_nt(activated.astype(BF), dn[:, cut : cut + step])
            total = term if total is None else total + term
        ffn_out[:, lo:hi] = total


def second_norm_kernel(
    idx, hidden, part, back, ct, cl, keep, pack,
    rt_out, rl_out, second_out, low_out, mine_out, sums_out,
):
    width, whole = ct.shape[1], hidden.shape[1]
    half = mine_out.shape[0]
    for lo, hi, cot, result in ((0, width, ct, rt_out), (width, whole, cl, rl_out)):
        total = (
            hidden[:, lo:hi] + (part[:, lo:hi] + back[:, lo:hi]) + pack[OB + 1 : OB + 2, lo:hi]
        )
        normed, inverse = norm_parts(total)
        gain = pack[GAIN + 1 : GAIN + 2, lo:hi]
        value = normed * gain + pack[SHIFT + 1 : SHIFT + 2, lo:hi]
        result[...] = (value if lo == 0 else turned(value)).astype(BF)
        upstream = cot[...].astype(F32) * keep[:, :1]
        grad = norm_back(upstream, normed, inverse, gain)
        second_out[:, lo:hi] = grad
        low = grad.astype(BF)
        low_out[:, lo:hi] = low
        sums_out[0:1, lo:hi] = jnp.sum(upstream * normed, axis=0, keepdims=True)
        sums_out[1:2, lo:hi] = jnp.sum(upstream, axis=0, keepdims=True)
        sums_out[2:3, lo:hi] = jnp.sum(low.astype(F32), axis=0, keepdims=True)
    mine_out[...] = low_out[pl.ds(pl.multiple_of(idx[3] * half, half), half), :]


def ffn_back_kernel(grad, slope_t, slope_l, up_t, dn_t, up_l, dn_l, part_out, bias_t, bias_l):
    width = up_t.shape[0]
    whole = width + up_l.shape[0]
    for lo, hi, slope, up, dn, bias in (
        (0, width, slope_t, up_t, dn_t, bias_t),
        (width, whole, slope_l, up_l, dn_l, bias_l),
    ):
        rows = grad[:, lo:hi]
        units = up.shape[1]
        step = min(units, 384)
        total = None
        for cut in range(0, units, step):
            if lo == 0:
                act_grad = dot_nt(rows, dn[cut : cut + step, :])
            else:
                act_grad = dot(rows, dn[:, cut : cut + step])
            before_grad = (act_grad * slope[:, cut : cut + step]).astype(BF)
            bias[:, cut : cut + step] = jnp.sum(before_grad.astype(F32), axis=0, keepdims=True)
            term = dot_nt(before_grad, up[:, cut : cut + step])
            total = term if total is None else total + term
        part_out[:, lo:hi] = total


def pieces(columns, piece):
    return [(at, min(at + piece, columns)) for at in range(0, columns, piece)]


def first_norm_kernel(
    second, part, back, normed_in, inverse_in, pack, sums_two, bias_t, bias_l,
    first_out, low_out, small_out,
):
    whole, piece = second.shape[1], small_out.shape[1]
    width = whole * 4 // 5
    small_out[...] = jnp.zeros_like(small_out)
    row = 0

    def put(value):
        nonlocal row
        for lo, hi in pieces(value.shape[1], piece):
            small_out[row : row + 1, : hi - lo] = value[:, lo:hi]
            row += 1

    sums = [[], [], []]
    for at, (lo, hi) in enumerate(((0, width), (width, whole))):
        upstream = second[:, lo:hi] + (part[:, lo:hi] + back[:, lo:hi])
        normed = normed_in[:, lo:hi]
        inverse = inverse_in[:, LANES * at : LANES * at + 1]
        grad = norm_back(upstream, normed, inverse, pack[GAIN : GAIN + 1, lo:hi])
        first_out[:, lo:hi] = grad
        low = grad.astype(BF)
        low_out[:, lo:hi] = low
        sums[0].append(jnp.sum(upstream * normed, axis=0, keepdims=True))
        sums[1].append(jnp.sum(upstream, axis=0, keepdims=True))
        sums[2].append(jnp.sum(low.astype(F32), axis=0, keepdims=True))
    for kind in range(3):
        put(jnp.concatenate(sums[kind], axis=1))
        put(sums_two[kind : kind + 1, :])
    put(bias_t[...])
    put(bias_l[...])


def unit_grads_kernel(idx, *refs):
    (
        low_parts, grad_parts, (up_t, dn_t, quarters, pack_in),
        (up_keep, up_send, dn_keep, dn_send),
        (low, grad, w_up, w_dn, w_l, pack, held, sems),
    ) = refs[:5], refs[5:10], refs[10:14], refs[14:18], refs[18:]
    quarter = idx[1] * 2 + idx[0]
    zz = idx[2]
    copies = []
    for parts, target in ((low_parts, low), (grad_parts, grad)):
        at = 0
        for part in parts:
            count = part.shape[0]
            copies.append((part, target.at[pl.ds(at, count), :]))
            at += count
    units = w_dn.shape[0]
    start = pl.multiple_of(quarter * units, units)
    copies.append((up_t.at[:, pl.ds(start, units)], w_up))
    copies.append((dn_t.at[pl.ds(start, units), :], w_dn))
    copies += [(quarters, w_l), (pack_in, pack)]
    copies = [pltpu.make_async_copy(s, d, sems.at[k]) for k, (s, d) in enumerate(copies)]
    for c in copies:
        c.start()
    for c in copies:
        c.wait()
    width = w_up.shape[0]
    piece = width // 4
    slot_rows = 16

    def grads(lo, hi, up, bias, down):
        before = dot(low[:, lo:hi], up) + bias
        activated, slope = gelu_parts(before)
        act_grad = dot_nt(grad[:, lo:hi], down) if lo == 0 else dot(grad[:, lo:hi], down)
        before_grad = (act_grad * slope).astype(BF)
        return activated.astype(BF), before_grad

    whole = width + w_l.shape[0]
    count = w_l.shape[0] // 2
    act_t, back_t = grads(
        0, width, w_up[...], pack[UP_T : UP_T + 1, pl.ds(start, units)], w_dn[...]
    )
    act_l, back_l = grads(
        width,
        whole,
        w_l[:, :count],
        pack[UP_Q : UP_Q + 1, :count],
        w_l[:, LANES : LANES + count],
    )

    def place_layout(matrix):
        pad = jnp.zeros((matrix.shape[0], LANES - matrix.shape[1]), F32)
        padded = jnp.concatenate([matrix, pad], axis=1)
        for k in range(4):
            for slot in range(3):
                first = slot_rows * (3 * k + slot)
                held[k ^ zz, piece : piece + slot_rows, LANES * slot : LANES * (slot + 1)] = padded[
                    first : first + slot_rows
                ]

    def hand_out(keep, send):
        for at in range(2):
            keep[at] = held[2 * at]
            send[at] = held[2 * at + 1].astype(BF)

    up_grad = dot_tn(low[:, :width], back_t)
    for k in range(4):
        held[k ^ zz, :piece, :] = up_grad[piece * k : piece * (k + 1)]
    place_layout(dot_tn(low[:, width:whole], back_l))
    hand_out(up_keep, up_send)
    down_grad = dot_tn(act_t, grad[:, :width])
    part = piece // 2
    for k in range(4):
        for side in range(2):
            held[k ^ zz, part * side : part * (side + 1), :] = down_grad[
                part * k : part * (k + 1), units * side : units * (side + 1)
            ]
    place_layout(dot_tn(grad[:, width:whole], act_l))
    hand_out(dn_keep, dn_send)


def attention_back_kernel(
    k_all, v_all, xt, xl, xt_p, xl_p, wt, bt, wl, bl, keys, out_t, out_l, ag_own, ag_p,
    dq, dk, dv, context, q_all, g_all,
):
    rows, width = xt.shape[0], wt.shape[2]
    wide = out_t.shape[1]
    for at, text_rows, layout_columns in ((0, xt, xl), (rows, xt_p, xl_p)):

        def write(text_part, layout_part, at=at):
            q_all[at : at + rows, :width] = text_part
            q_all[at : at + rows, width:] = layout_part

        project_rows(text_rows[...], layout_columns[...], wt, bt, wl, bl, 0, write)
    for at, grad in ((0, ag_own), (rows, ag_p)):
        g_all[at : at + rows, :width] = dot_nt(grad[:, :wide], out_t[...]).astype(BF)
        layout_grad = dot_nt(grad[:, wide:], out_l[...])
        pad = jnp.zeros((rows, LANES - layout_grad.shape[1]), F32)
        g_all[at : at + rows, width:] = jnp.concatenate([layout_grad, pad], axis=1).astype(BF)
    bias = hidden_bias(keys[...], 2 * rows)
    zero_turned, zero = jnp.zeros((LANES, 2 * rows), F32), jnp.zeros((2 * rows, LANES), F32)
    layout_context, layout_dq, layout_dk, layout_dv = zero_turned, zero_turned, zero, zero
    for pair in range(width // LANES):
        query_pair, key_pair = pair_of(q_all, pair, width), pair_of(k_all, pair, width)
        grad_pair, value_pair = pair_of(g_all, pair, width), pair_of(v_all, pair, width)
        key_turned, value_turned = key_pair.T, value_pair.T
        text_context, text_dq, text_dk, text_dv = zero_turned, zero_turned, zero, zero
        for member in range(2):
            head = 2 * pair + member
            query_head = query_pair * head_mask(member, head, SCALE_T, SCALE_L, 1).astype(BF)
            grad_head = grad_pair * head_mask(member, head, 1.0, 1.0, 1).astype(BF)
            probs = probabilities(key_pair, query_head, bias)
            probs_low = probs.astype(BF)
            prob_grads = dot_nt(value_pair, grad_head)
            delta = jnp.sum(probs * prob_grads, axis=0, keepdims=True)
            score_grads = (probs * (prob_grads - delta)).astype(BF)
            value_part = dot(probs_low, grad_head)
            text_dv += value_part[:, :LANES]
            layout_dv += value_part[:, LANES:]
            key_part = dot(score_grads, query_head)
            text_dk += key_part[:, :LANES]
            layout_dk += key_part[:, LANES:]
            query_part = dot(key_turned, score_grads) * head_mask(member, head, SCALE_T, SCALE_L, 0)
            text_dq += query_part[:LANES]
            layout_dq += query_part[LANES:]
            context_part = dot(value_turned, probs_low) * head_mask(member, head, 1.0, 1.0, 0)
            text_context += context_part[:LANES]
            layout_context += context_part[LANES:]
        columns = slice(LANES * pair, LANES * (pair + 1))
        context[:, columns] = text_context.T.astype(BF)
        dq[:, columns] = text_dq.T.astype(BF)
        dk[:, columns] = text_dk.astype(BF)
        dv[:, columns] = text_dv.astype(BF)
    context[:, width:] = layout_context.T.astype(BF)
    dq[:, width:] = layout_dq.T.astype(BF)
    dk[:, width:] = layout_dk.astype(BF)
    dv[:, width:] = layout_dv.astype(BF)


def input_part_kernel(dq, dk, dv, wt, wl, part_out):
    rows, width, heads_l = part_out.shape[0], wt.shape[2], wl.shape[2]
    wide = wt.shape[1]
    total_t = total_l = None
    for which, grad in enumerate((dq, dk, dv)):
        term_t = dot_nt(grad[:rows, :width], wt[which])
        term_l = dot_nt(grad[:rows, width : width + heads_l], wl[which])
        total_t = term_t if which == 0 else total_t + term_t
        total_l = term_l if which == 0 else total_l + term_l
    part_out[:, :wide] = total_t
    part_out[:, wide : wide + wl.shape[1]] = total_l


def input_grad_kernel(first, part, back, text_out, layout_out):
    wide, whole = text_out.shape[1], first.shape[1]
    text_out[...] = (first[:, :wide] + (part[:, :wide] + back[:, :wide])).astype(BF)
    layout_out[...] = turned(
        first[:, wide:] + (part[:, wide:whole] + back[:, wide:whole])
    ).astype(BF)


def attention_grads_kernel(
    row, idx, dq, dk, dv, context, xt, xl, xt_p, xl_p, ag_own, ag_p, small, small_p,
    keep_out, send_out, matrices, held, sums,
):
    wide, rows = xt.shape[1], xt.shape[0]
    width = keep_out.shape[2]
    bx, by, zz = idx[0], idx[1], idx[2]
    side = wide // 2
    start = pl.multiple_of(bx * side, side)
    thin = side // 8

    def over_rows(left_own, left_other, right):
        both = jnp.concatenate([left_own, left_other], axis=0)
        return dot_tn(both, right)

    def place(matrix, lowest):
        for y in range(2):
            for z in range(4):
                first = thin * (4 * y + z)
                held[(y ^ by) * 4 + (z ^ zz), lowest : lowest + thin, :] = matrix[
                    first : first + thin
                ]

    x_side = jnp.concatenate([xt[:, pl.ds(start, side)], xt_p[:, pl.ds(start, side)]], axis=0)
    for which, grad in enumerate((dq, dk, dv)):
        place(dot_tn(x_side, grad[:, :width]), thin * which)
        matrices[which] = dot(xl[...], grad[:rows, width:]) + dot(xl_p[...], grad[rows:, width:])
    ag_side = jnp.concatenate([ag_own[:, pl.ds(start, side)], ag_p[:, pl.ds(start, side)]], axis=0)
    place(dot_tn(context[:, :width], ag_side), 3 * thin)
    ag_l = jnp.concatenate([ag_own[:, wide:], ag_p[:, wide:]], axis=0)
    matrices[3] = dot_tn(ag_l, context[:, width:])
    sums[...] = small[...] + small_p[...]
    for grad in (dq, dv):
        total = jnp.sum(grad[...].astype(F32), axis=0, keepdims=True)
        for lo, hi in pieces(total.shape[1], width):
            sums[row : row + 1, : hi - lo] = total[:, lo:hi]
            row += 1
    left, right = matrices[2 * bx], matrices[2 * bx + 1]
    strip = left.shape[0] // 8
    for y in range(2):
        for z in range(4):
            eighth = 4 * y + z
            first = strip * eighth
            both = jnp.concatenate(
                [left[first : first + strip], right[first : first + strip]], axis=0
            )[:, : width // 4]
            count = 2 * strip // 4
            packed = jnp.concatenate(
                [both[count * slot : count * (slot + 1)] for slot in range(4)], axis=1
            )
            rest = 16 - count
            held[(y ^ by) * 4 + (z ^ zz), 4 * thin : 4 * thin + 16, :] = jnp.concatenate(
                [packed, sums[rest * eighth : rest * (eighth + 1), :]], axis=0
            )
    for k in range(4):
        keep_out[k] = held[k]
        send_out[k] = held[4 + k].astype(BF)


def pieces_of(refs, idx):
    for at in range(4):
        for group in range(2):
            for k in range(2):
                yield refs[2 * at + group], k, (idx[1] * 2 + idx[0]) ^ at, (2 * k + group) ^ idx[2]


def unpack_layout(piece, k, lowest, table, quarter, place):
    for slot in range(3):
        first = pl.multiple_of(place * 48 + 16 * slot, 16)
        table[quarter, pl.ds(first, 16), :] = piece[
            k, lowest : lowest + 16, LANES * slot : LANES * (slot + 1)
        ].astype(F32)


def units_result_kernel(idx, *refs):
    parts, (up_t, up_l, dn_t, dn_l), (up_table, dn_table) = refs[:16], refs[16:20], refs[20:]
    rows, columns = up_t.shape[0] // 4, up_t.shape[1] // 4
    thin = up_l.shape[1] // 4
    half = rows // 2
    for at, piece in enumerate(parts):
        quarter, place = (idx[1] * 2 + idx[0]) ^ (at & 3), (at >> 2) ^ idx[2]
        up_t[
            pl.ds(pl.multiple_of(place * rows, rows), rows),
            pl.ds(pl.multiple_of(quarter * columns, columns), columns),
        ] = piece[0, :rows, :].astype(F32)
        unpack_layout(piece, 0, rows, up_table, quarter, place)
        first = pl.multiple_of((quarter * 4 + place) * half, half)
        for side in range(2):
            dn_t[pl.ds(first, half), columns * side : columns * (side + 1)] = piece[
                1, half * side : half * (side + 1), :
            ].astype(F32)
        unpack_layout(piece, 1, rows, dn_table, quarter, place)
    for q in range(4):
        up_l[:, thin * q : thin * (q + 1)] = up_table[q][:, :thin]
        dn_l[:, thin * q : thin * (q + 1)] = dn_table[q][:, :thin]


def attention_result_kernel(idx, *refs):
    parts, (qkv_t, out_t, qkv_l, out_l), refs = refs[:8], refs[8:12], refs[12:]
    (bt, gt, st, ubt, qvt, bl, gl, sl, ubl, qvl), (table, sums) = refs[:10], refs[10:]
    side = qkv_t.shape[1] // 2
    thin, strip, heads_l = side // 8, qkv_l.shape[1] // 8, qkv_l.shape[2]
    count = 2 * strip // 4
    rest = 16 - count
    for piece, k, quarter, place in pieces_of(parts, idx):
        x, y = quarter & 1, quarter >> 1
        eighth = y * 4 + place
        first = pl.multiple_of(x * side + eighth * thin, 16)
        for which in range(3):
            qkv_t[which, pl.ds(first, thin), :] = piece[
                k, thin * which : thin * (which + 1), :
            ].astype(F32)
        out_t[
            pl.ds(pl.multiple_of(eighth * thin, 16), thin), pl.ds(pl.multiple_of(x * side, side), side)
        ] = piece[k, 3 * thin : 4 * thin, :].astype(F32)
        last = piece[k, 4 * thin : 4 * thin + 16, :].astype(F32)
        both = jnp.concatenate(
            [last[:count, heads_l * slot : heads_l * (slot + 1)] for slot in range(4)], axis=0
        )
        for member in range(2):
            table[
                2 * x + member, pl.ds(pl.multiple_of(eighth * strip, 8), strip), :heads_l
            ] = both[strip * member : strip * (member + 1)]
        sums[x, eighth, :rest, :] = last[count:, :]
    for which in range(3):
        qkv_l[which] = table[which][:, :heads_l]
    out_l[...] = turned(table[3])[:heads_l]

    at = 0

    def take(columns):
        nonlocal at
        found = []
        for lo, hi in pieces(columns, sums.shape[3]):
            found.append(sums[0, at // rest, at % rest : at % rest + 1, : hi - lo])
            at += 1
        return jnp.concatenate(found, axis=1) if len(found) > 1 else found[0]

    wide, whole = gt.shape[1], gt.shape[1] + gl.shape[1]
    for text_out, layout_out in ((gt, gl), (st, sl), (bt, bl)):
        for row in range(2):
            value = take(whole)
            text_out[row : row + 1, :] = value[:, :wide]
            layout_out[row : row + 1, :] = value[:, wide:]
    ubt[...] = take(ubt.shape[1])
    ubl[...] = take(ubl.shape[1])
    for row in range(2):
        value = take(qvt.shape[1] + LANES)
        qvt[row : row + 1, :] = value[:, : qvt.shape[1]]
        qvl[row : row + 1, :] = value[:, qvt.shape[1] : qvt.shape[1] + qvl.shape[1]]


def gathered(own):
    even = jnp.stack([own, exchange(own, 8)])
    odd = exchange(even, 4)
    even_x, odd_y = exchange(even, 1), exchange(odd, 2)
    even_y, odd_x = exchange(even, 2), exchange(odd, 1)
    even_xy, odd_xy = exchange(even_x, 2), exchange(odd_y, 1)
    return even, odd, even_x, odd_x, even_y, odd_y, even_xy, odd_xy


def gathered_singly(own):
    found = {0: own, 4: exchange(own, 4), 8: exchange(own, 8)}
    found[12] = exchange(found[8], 4)
    for z, first, second in ((0, 1, 2), (4, 2, 1), (8, 1, 2), (12, 2, 1)):
        found[z + first] = exchange(found[z], first)
        found[z + second] = exchange(found[z], second)
        found[z + 3] = exchange(found[z + first], second)
    return [found[at] for at in range(16)]


def reduced(keep, far):
    total = keep + far.astype(F32)
    own = total[0] + exchange(total[1].astype(BF), 8).astype(F32)
    mask = 16
    while mask < lax.axis_size("seq"):
        own = own + exchange(own, mask)
        mask *= 2
    return own.astype(BF)


def per_device(
    text_in,
    layout_in,
    text_cot,
    layout_cot,
    doc_ids,
    span_ids,
    intersection_flags,
    text_qkv,
    text_qv_bias,
    text_out,
    text_out_bias,
    text_gains,
    text_shifts,
    text_up,
    text_up_bias,
    text_down,
    layout_qkv,
    layout_qv_bias,
    layout_out,
    layout_out_bias,
    layout_gains,
    layout_shifts,
    layout_up,
    layout_up_bias,
    layout_down,
):
    rows, wide = text_in.shape
    thin = layout_in.shape[1]
    whole = wide + thin
    width, width_l = text_qkv.shape[2], layout_qkv.shape[2]
    padded = width + LANES
    units, units_l = text_up.shape[1], layout_up.shape[1]
    half = rows // 2
    place = lax.axis_index("seq")
    idx = jnp.stack(
        [place & 1, (place >> 1) & 1, (place >> 2) & 3, lax.axis_index("tensor")]
    ).astype(jnp.int32)

    layout_turned, cot_turned, down_turned = layout_in.T, layout_cot.T, layout_down.T
    own_key = (doc_ids * 65536 + span_ids).astype(F32)[None, :]
    text_other, layout_other = exchange(text_in, 1), exchange(layout_turned, 1)
    keys = jnp.concatenate([own_key, exchange(own_key, 1)], axis=1)
    sent = shape((rows, wide + 2 * LANES), F32)

    cot_rows, keep_rows, pack, quarters = call(
        pack_kernel,
        [
            shape((rows, thin), BF),
            shape((rows, LANES), F32),
            shape((16, units), F32),
            shape((thin, 2 * LANES), BF),
        ],
        idx, cot_turned, intersection_flags[None, :], text_out_bias, text_gains, text_shifts,
        text_up_bias[None, :], layout_out_bias, layout_gains, layout_shifts,
        layout_up_bias[None, :], layout_up, down_turned, smem=1, far=range(1, 13), pin=range(4),
    )
    qkv_weights = (text_qkv, text_qv_bias, layout_qkv, layout_qv_bias)
    q_own, k_own, v_own, layout_rows = call(
        project_kernel,
        [shape((rows, padded), BF)] * 3 + [shape((rows, thin), BF)],
        text_in, layout_turned, *qkv_weights, pin=range(4),
    )
    attended, k_all, v_all = call(
        attend_kernel,
        [sent] + [shape((2 * rows, padded), BF)] * 2,
        q_own, k_own, v_own, text_other, layout_other, *qkv_weights, keys, text_out, layout_out,
        scratch=[pltpu.VMEM((rows, padded), BF)], pin=[1, 2],
    )
    hidden, normed, inverse, low_mine, low = call(
        norm_kernel,
        [
            shape((rows, whole), F32),
            shape((rows, whole), F32),
            shape((rows, 2 * LANES), F32),
            shape((half, wide + 2 * LANES), BF),
            shape((rows, wide + 2 * LANES), BF),
        ],
        idx, text_in, layout_rows, attended, over_cores(attended), pack, smem=1, pin=[0, 1, 2, 4],
    )
    slope_t, slope_l, ffn = call(
        ffn_kernel,
        [shape((rows, units), F32), shape((rows, units_l), F32), sent],
        low, pack, text_up, text_down, layout_up, down_turned, flops=14 * 10**8, room=20, pin=[0, 1],
    )
    ffn_back = over_cores(ffn)
    low_far = [exchange(low_mine, mask) for mask in (1, 2, 3)]
    text_result, layout_result, second, grad_low, grad_mine, sums_two = call(
        second_norm_kernel,
        [
            shape((rows, wide), BF),
            shape((thin, rows), BF),
            shape((rows, whole), F32),
            shape((rows, wide + 2 * LANES), BF),
            shape((half, wide + 2 * LANES), BF),
            shape((3, whole), F32),
        ],
        idx, hidden, ffn, ffn_back, text_cot, cot_rows, keep_rows, pack, smem=1, pin=[2, 3, 5],
    )
    grad_far = [exchange(grad_mine, mask) for mask in (1, 2, 3)]
    low_back = Near(over_cores(jnp.concatenate(low_far, axis=0)))
    hidden_part, bias_t, bias_l = call(
        ffn_back_kernel,
        [sent, shape((1, units), F32), shape((1, units_l), F32)],
        grad_low, slope_t, slope_l, text_up, text_down, layout_up, down_turned, flops=14 * 10**8,
        room=20, pin=[1, 2], after=[low_back],
    )
    first, attended_grad, small = call(
        first_norm_kernel,
        [shape((rows, whole), F32), shape((rows, whole), BF), shape((32, width), F32)],
        second, hidden_part, over_cores(hidden_part), normed, inverse, pack, sums_two, bias_t, bias_l, pin=[0],
    )
    attended_grad_other = exchange(attended_grad, 1)

    grad_cat = jnp.concatenate(grad_far, axis=0)
    low_parts = [low, *low_far, low_back]
    grad_parts = [grad_low, *grad_far, over_cores(tied(grad_cat, small))]
    block = (2, wide // 4 + 16, width)
    up_keep, up_send, down_keep, down_send = call(
        unit_grads_kernel,
        [shape(block, F32), shape(block, BF)] * 2,
        idx, *low_parts, *grad_parts, text_up, text_down, quarters, pack,
        scratch=[
            pltpu.VMEM((4 * rows, wide + 2 * LANES), BF),
            pltpu.VMEM((4 * rows, wide + 2 * LANES), BF),
            pltpu.VMEM((wide, units // 4), BF),
            pltpu.VMEM((units // 4, wide), BF),
            pltpu.VMEM((thin, 2 * LANES), BF),
            pltpu.VMEM((16, units), F32),
            pltpu.VMEM((4,) + block[1:], F32),
            pltpu.SemaphoreType.DMA((14,)),
        ],
        smem=1, anys=range(1, 15), flops=24 * 10**8, room=24,
    )
    up_far, down_far = exchange(up_send, 4), exchange(down_send, 4)
    small_other = exchange(tied(small, up_send), 1)

    dq, dk, dv, context = call(
        attention_back_kernel,
        [shape((2 * rows, padded), BF)] * 4,
        k_all, v_all, text_in, layout_turned, text_other, layout_other, *qkv_weights, keys, text_out,
        layout_out, attended_grad, attended_grad_other,
        scratch=[pltpu.VMEM((2 * rows, padded), BF)] * 2, flops=50 * 10**8, room=24, pin=range(4),
    )
    used = 6 * len(pieces(whole, width)) + len(pieces(units, width)) + len(pieces(units_l, width))
    keep, send = call(
        partial(attention_grads_kernel, used),
        [shape((4,) + block[1:], F32), shape((4,) + block[1:], BF)],
        idx, dq, dk, dv, context, text_in, layout_turned, text_other, layout_other, attended_grad,
        attended_grad_other, small, small_other,
        scratch=[
            pltpu.VMEM((4, thin, LANES), F32),
            pltpu.VMEM((8,) + block[1:], F32),
            pltpu.VMEM(small.shape, F32),
        ],
        smem=1, flops=10**9, room=24,
    )
    send_far = exchange(send, 2)
    up_own = reduced(up_keep, tied(up_far, keep))
    down_own = reduced(down_keep, tied(down_far, keep))
    (input_part,) = call(
        input_part_kernel, [sent], dq, dk, dv, text_qkv, layout_qkv, flops=5 * 10**8
    )
    text_in_grad, layout_in_grad = call(
        input_grad_kernel,
        [shape((rows, wide), BF), shape((thin, rows), BF)],
        first, input_part, over_cores(input_part),
    )
    plane = keep + send_far.astype(F32)
    attention_own = reduced(
        jnp.stack([plane[0], plane[2]]),
        exchange(jnp.stack([plane[1], plane[3]]).astype(BF), 4),
    )

    up_t, up_l, down_t, down_l = call(
        units_result_kernel,
        [shape(a.shape, F32) for a in (text_up, layout_up, text_down, down_turned)],
        idx, *gathered_singly(jnp.stack([up_own, down_own])), scratch=[pltpu.VMEM((4, thin, LANES), F32)] * 2, smem=1,
        room=32,
    )
    one_row = (1, units), (1, units_l)
    kinds = [text_out_bias.shape] * 3 + [one_row[0], text_qv_bias.shape]
    kinds += [layout_out_bias.shape] * 3 + [one_row[1], layout_qv_bias.shape]
    (
        qkv_t, out_t, qkv_l, out_l,
        out_bias_t, gains_t, shifts_t, ub_t, qv_t, out_bias_l, gains_l, shifts_l, ub_l, qv_l,
    ) = call(
        attention_result_kernel,
        [shape(a.shape, F32) for a in (text_qkv, text_out, layout_qkv, layout_out)]
        + [shape(dims, F32) for dims in kinds],
        idx, *gathered(attention_own),
        scratch=[pltpu.VMEM((4, thin, LANES), F32), pltpu.VMEM((2, 8, 8, width), F32)], smem=1,
    )
    return (
        text_result,
        layout_result.T,
        text_in_grad,
        layout_in_grad.T,
        qkv_t,
        qv_t,
        out_t,
        out_bias_t,
        gains_t,
        shifts_t,
        up_t,
        ub_t[0],
        down_t,
        qkv_l,
        qv_l,
        out_l,
        out_bias_l,
        gains_l,
        shifts_l,
        up_l,
        ub_l[0],
        down_l.T,
    )


def solution(mesh):
    rows, both, halves = P("seq", None), P(), P("tensor", None)
    stack, columns, one = P(None, None, "tensor"), P(None, "tensor"), P("tensor")
    weights_in = (stack, columns, halves, both, both, both, columns, one, halves)
    return jax.shard_map(
        per_device,
        mesh=mesh,
        in_specs=(rows,) * 4 + (P("seq"),) * 3 + weights_in * 2,
        out_specs=(rows,) * 4 + weights_in * 2,
        check_vma=False,
    )
```

time: 266 us -> 205 us (0.77)
  local copies, waits for them, and re-layouts: 44.2 us -> 9.64 us
  starting transfers between devices: 60.2 us -> 44.2 us
  other arithmetic: 12.4 us -> 2.68 us
  waiting for transfers between devices: 97.7 us -> 104 us
  Pallas kernels: 48.8 us -> 43.3 us
    unnamed x166 -> x56, local copies, waits for them, and re-layouts: 30.3 us -> 8.33 us
    ppermute x55 -> x47, starting transfers between devices: 60.2 us -> 44.2 us  [exchange(): lax.ppermute(shard, axis, [(i, i ^ mask) for i in range(lax.axis_size(axi...]
    ppermute x4 -> x0, local copies, waits for them, and re-layouts: 6.88 us -> none  [exchange(): lax.ppermute(shard, axis, [(i, i ^ mask) for i in range(lax.axis_size(axi...]
    ppermute x55 -> x47, waiting for transfers between devices: 97.7 us -> 104 us  [exchange(): lax.ppermute(shard, axis, [(i, i ^ mask) for i in range(lax.axis_size(axi...]
    pallas_call x11 -> x15, Pallas kernels: 48.8 us -> 43.3 us  [call(): pl.pallas_call(body, out_shape=tuple((pltpu.VMEM(o.shape, o.dtype) if k i...]
    pallas_call x4 -> x0, local copies, waits for them, and re-layouts: 4.12 us -> none  [call(): pl.pallas_call(kernel, out_shape=tuple(outs), in_specs=specs, out_specs=t...]
    add x8 -> x3, other arithmetic: 3.5 us -> 0.2 us  [reduced(): total = keep + far.astype(F32)]
    convert_element_type x3 -> x0, other arithmetic: 2.99 us -> none  [the longest x1 1.99 us: per_device(): text_in_grad = (first[:, :wide] + input_total[:, :wide]).astype(BF)]
  transfers between devices with their start and end apart: 55 -> 47, of which waited for: 20 -> 21; matrix products, arithmetic and copies ran while one was open for 10% -> 1% of each run, Pallas kernels for 14% -> 15%
where the time goes in v2:
time: 205 us
  waiting for transfers between devices  104 us (51%)
  starting transfers between devices  44.2 us (22%)
  Pallas kernels  43.3 us (21%)
  local copies, waits for them, and re-layouts  9.64 us (5%)
  other arithmetic  2.68 us (1%)
    ppermute x47, waiting for transfers between devices, exchange(): lax.ppermute(shard, axis, [(i, i ^ mask) for i in range(lax.axis_size(axi...  104 us
    ppermute x47, starting transfers between devices, exchange(): lax.ppermute(shard, axis, [(i, i ^ mask) for i in range(lax.axis_size(axi...  44.2 us
    pallas_call x15, Pallas kernels, call(): pl.pallas_call(body, out_shape=tuple((pltpu.VMEM(o.shape, o.dtype) if k i...  43.3 us
    unnamed x56, local copies, waits for them, and re-layouts  8.33 us
  transfers between devices with their start and end apart: 47, of which 21 were waited for; matrix products, arithmetic and copies ran while one was open for 1% of the time, Pallas kernels for 15%

profile of v2, /device:TPU:0, one launch (start us, length us, event | category | flops | bytes accessed | tf_op | source)
XLA Modules:
  0.0 204.6 jit_solution(13241483876957685829)
XLA Ops:
  0.7 3.0 %collective-permute-start = (bf16[256,768]{1,0:T(8,128)(2,1)}, bf16[256,768]{1,0:T(8,128)(2,1)S(1)}, u32[]{:S(2)}, u32[]{:S(2)}) collective-permute-start(bf16[256,768]{1,0:T(8,128)(2,1)} %refs_5_.9), channel_id=1, source_target_pairs={{0,2},{2,0},{4,6},{6,4},{8,10},{10,8},{12,14},{14,12},{16,18},{18,... | collective-permute-start | bytes 1179656 | tf_op jit(solution)/shard_map/ppermute | solution.py:20
  16.3 3.6 %shard_map.409 = (f32[256,1024]{1,0:T(8,128)}, bf16[512,512]{1,0:T(8,128)(2,1)S(1)}, bf16[512,512]{1,0:T(8,128)(2,1)S(1)}) custom-call(bf16[256,512]{1,0:T(8,128)(2,1)S(1)} %get-tuple-element.88.refs_0_, bf16[256,512]{1,0:T(8,128)(2,1)S(1)} %get-tuple-element.89.refs_1_, bf16[256,512]{1,0:T(8,128)(2,1)S(1)} %get-tuple-element.90.refs_2_, ...), custom_call_target="tpu_custom_call" | custom-call | flops 100000000 | bytes 5885824 | tf_op jit(solution)/shard_map/pallas_call | solution.py:85
  22.7 2.8 %shard_map.410 = (bf16[256,192]{1,0:T(8,128)(2,1)S(1)}, f32[256,128]{1,0:T(8,128)S(1)}, f32[16,1536]{1,0:T(8,128)S(1)}, bf16[192,256]{1,0:T(8,128)(2,1)S(1)}) custom-call(s32[4]{0:T(128)S(1)} %pad_add_fusion.refs_0_, bf16[192,256]{1,0:T(8,128)(2,1)} %bitcast.55, s32[1,256]{1,0:T(1,128)} %bitcast.58, bf16[2,768]{1,0:T(2,128)(2,1)} %refs_3_.6, ...), custom_call_target="tpu_custom_call" | custom-call | flops 100000000 | bytes 835600 | tf_op jit(solution)/shard_map/pallas_call | solution.py:85
  33.6 3.2 %collective-permute-done.5.refs_2_ = bf16[128,1024]{1,0:T(8,128)(2,1)S(1)} collective-permute-done((bf16[128,1024]{1,0:T(8,128)(2,1)S(1)}, bf16[128,1024]{1,0:T(8,128)(2,1)S(1)}, u32[]{:S(2)}, u32[]{:S(2)}) %collective-permute-start.5) | collective-permute-done | bytes 262176 | tf_op jit(solution)/shard_map/ppermute | solution.py:20
  36.8 6.7 %collective-permute-done.6.refs_3_ = bf16[128,1024]{1,0:T(8,128)(2,1)S(1)} collective-permute-done((bf16[128,1024]{1,0:T(8,128)(2,1)S(1)}, bf16[128,1024]{1,0:T(8,128)(2,1)S(1)}, u32[]{:S(2)}, u32[]{:S(2)}) %collective-permute-start.6) | collective-permute-done | bytes 262176 | tf_op jit(solution)/shard_map/ppermute | solution.py:20
  52.3 5.7 %collective-permute-done.12.refs_7_ = bf16[128,1024]{1,0:T(8,128)(2,1)S(1)} collective-permute-done((bf16[128,1024]{1,0:T(8,128)(2,1)S(1)}, bf16[128,1024]{1,0:T(8,128)(2,1)S(1)}, u32[]{:S(2)}, u32[]{:S(2)}) %collective-permute-start.12) | collective-permute-done | bytes 262176 | tf_op jit(solution)/shard_map/ppermute | solution.py:20
  58.0 4.1 %collective-permute-done.13.refs_8_ = bf16[128,1024]{1,0:T(8,128)(2,1)S(1)} collective-permute-done((bf16[128,1024]{1,0:T(8,128)(2,1)S(1)}, bf16[128,1024]{1,0:T(8,128)(2,1)S(1)}, u32[]{:S(2)}, u32[]{:S(2)}) %collective-permute-start.13) | collective-permute-done | bytes 262176 | tf_op jit(solution)/shard_map/ppermute | solution.py:20
  67.0 5.6 %shard_map.419 = (f32[2,208,384]{2,1,0:T(8,128)S(1)}, bf16[2,208,384]{2,1,0:T(8,128)(2,1)S(1)}, f32[2,208,384]{2,1,0:T(8,128)S(1)}, bf16[2,208,384]{2,1,0:T(8,128)(2,1)S(1)}) custom-call(s32[4]{0:T(128)S(1)} %pad_add_fusion.refs_0_, bf16[256,1024]{1,0:T(8,128)(2,1)S(1)} %get-tuple-element.94.refs_0_.refs_1_, ...), custom_call_target="tpu_custom_call" | custom-call | flops 2400000000 | bytes 11026448 | tf_op jit(solution)/shard_map/pallas_call | solution.py:85
  75.0 4.4 %collective-permute-done.10.refs_14_.refs_10_ = bf16[256,960]{1,0:T(8,128)(2,1)S(1)} collective-permute-done((bf16[256,960]{1,0:T(8,128)(2,1)S(1)}, bf16[256,960]{1,0:T(8,128)(2,1)S(1)}, u32[]{:S(2)}, u32[]{:S(2)}) %collective-permute-start.10) | collective-permute-done | bytes 491552 | tf_op jit(solution)/shard_map/ppermute | solution.py:20
  79.5 8.6 %shard_map.416 = (bf16[512,512]{1,0:T(8,128)(2,1)S(1)}, bf16[512,512]{1,0:T(8,128)(2,1)S(1)}, bf16[512,512]{1,0:T(8,128)(2,1)S(1)}, bf16[512,512]{1,0:T(8,128)(2,1)S(1)}) custom-call(bf16[512,512]{1,0:T(8,128)(2,1)S(1)} %copy-done.23, bf16[512,512]{1,0:T(8,128)(2,1)S(1)} %copy-done.25, bf16[256,768]{1,0:T(8,128)(2,1)S(1)} %copy-done.6, ...), custom_call_target="tpu_custom_call" | custom-call | flops 5000000000 | bytes 7622528 | tf_op jit(solution)/shard_map/pallas_call | solution.py:85
  93.8 2.7 %collective-permute-start.29 = (bf16[208,384]{1,0:T(8,128)(2,1)S(1)}, bf16[208,384]{1,0:T(8,128)(2,1)S(1)}, u32[]{:S(2)}, u32[]{:S(2)}) collective-permute-start(bf16[208,384]{1,0:T(8,128)(2,1)S(1)} %fusion.8), channel_id=1, source_target_pairs={{0,16},{2,18},{4,20},{6,22},{8,24},{10,26},{12,28},{14,30},{16,0},... | collective-permute-start | bytes 479240 | tf_op jit(solution)/shard_map/ppermute | solution.py:20
  96.5 6.0 %collective-permute-done.30 = bf16[2,208,384]{2,1,0:T(8,128)(2,1)S(1)} collective-permute-done((bf16[2,208,384]{2,1,0:T(8,128)(2,1)S(1)}, bf16[2,208,384]{2,1,0:T(8,128)(2,1)S(1)}, u32[]{:S(2)}, u32[]{:S(2)}) %collective-permute-start.30) | collective-permute-done | bytes 319520 | tf_op jit(solution)/shard_map/ppermute | solution.py:20
  103.6 9.0 %collective-permute-done.31 = bf16[208,384]{1,0:T(8,128)(2,1)S(1)} collective-permute-done((bf16[208,384]{1,0:T(8,128)(2,1)S(1)}, bf16[208,384]{1,0:T(8,128)(2,1)S(1)}, u32[]{:S(2)}, u32[]{:S(2)}) %collective-permute-start.31) | collective-permute-done | bytes 159776 | tf_op jit(solution)/shard_map/ppermute | solution.py:20
  113.0 2.5 %collective-permute-start.39 = (bf16[2,208,384]{2,1,0:T(8,128)(2,1)S(1)}, bf16[2,208,384]{2,1,0:T(8,128)(2,1)S(1)}, u32[]{:S(2)}, u32[]{:S(2)}) collective-permute-start(bf16[2,208,384]{2,1,0:T(8,128)(2,1)S(1)} %pad_maximum_fusion.4.refs_1_), channel_id=1, source_target_pairs={{0,16},{2,18},{4,20},{6,22},{8,24},{10,26},{12,28},{14,30},{16,0},... | collective-permute-start | bytes 958472 | tf_op jit(solution)/shard_map/ppermute | solution.py:20
  115.6 14.6 %collective-permute-done.18 = bf16[2,208,384]{2,1,0:T(8,128)(2,1)S(1)} collective-permute-done((bf16[2,208,384]{2,1,0:T(8,128)(2,1)S(1)}, bf16[2,208,384]{2,1,0:T(8,128)(2,1)S(1)}, u32[]{:S(2)}, u32[]{:S(2)}) %collective-permute-start.18) | collective-permute-done | bytes 319520 | tf_op jit(solution)/shard_map/ppermute | solution.py:20
  134.9 5.5 %collective-permute-done.35.refs_5_ = bf16[2,208,384]{2,1,0:T(8,128)(2,1)S(1)} collective-permute-done((bf16[2,208,384]{2,1,0:T(8,128)(2,1)S(1)}, bf16[2,208,384]{2,1,0:T(8,128)(2,1)S(1)}, u32[]{:S(2)}, u32[]{:S(2)}) %collective-permute-start.35) | collective-permute-done | bytes 319520 | tf_op jit(solution)/shard_map/ppermute | solution.py:20
  143.2 8.6 %collective-permute-done.20 = bf16[208,384]{1,0:T(8,128)(2,1)S(1)} collective-permute-done((bf16[208,384]{1,0:T(8,128)(2,1)S(1)}, bf16[208,384]{1,0:T(8,128)(2,1)S(1)}, u32[]{:S(2)}, u32[]{:S(2)}) %collective-permute-start.20) | collective-permute-done | bytes 159776 | tf_op jit(solution)/shard_map/ppermute | solution.py:20
  156.1 6.1 %collective-permute-done.34.refs_4_ = bf16[2,208,384]{2,1,0:T(8,128)(2,1)S(1)} collective-permute-done((bf16[2,208,384]{2,1,0:T(8,128)(2,1)S(1)}, bf16[2,208,384]{2,1,0:T(8,128)(2,1)S(1)}, u32[]{:S(2)}, u32[]{:S(2)}) %collective-permute-start.34) | collective-permute-done | bytes 319520 | tf_op jit(solution)/shard_map/ppermute | solution.py:20
  164.4 4.7 %collective-permute-done.41.refs_11_ = bf16[2,208,384]{2,1,0:T(8,128)(2,1)S(1)} collective-permute-done((bf16[2,208,384]{2,1,0:T(8,128)(2,1)S(1)}, bf16[2,208,384]{2,1,0:T(8,128)(2,1)S(1)}, u32[]{:S(2)}, u32[]{:S(2)}) %collective-permute-start.41) | collective-permute-done | bytes 319520 | tf_op jit(solution)/shard_map/ppermute | solution.py:20
  169.4 6.6 %collective-permute-done.45.refs_15_ = bf16[2,208,384]{2,1,0:T(8,128)(2,1)S(1)} collective-permute-done((bf16[2,208,384]{2,1,0:T(8,128)(2,1)S(1)}, bf16[2,208,384]{2,1,0:T(8,128)(2,1)S(1)}, u32[]{:S(2)}, u32[]{:S(2)}) %collective-permute-start.45) | collective-permute-done | bytes 319520 | tf_op jit(solution)/shard_map/ppermute | solution.py:20
  178.2 4.5 %collective-permute-done.42.refs_12_ = bf16[2,208,384]{2,1,0:T(8,128)(2,1)S(1)} collective-permute-done((bf16[2,208,384]{2,1,0:T(8,128)(2,1)S(1)}, bf16[2,208,384]{2,1,0:T(8,128)(2,1)S(1)}, u32[]{:S(2)}, u32[]{:S(2)}) %collective-permute-start.42) | collective-permute-done | bytes 319520 | tf_op jit(solution)/shard_map/ppermute | solution.py:20
  186.7 2.9 %collective-permute-done.25.refs_6_ = bf16[2,208,384]{2,1,0:T(8,128)(2,1)S(1)} collective-permute-done((bf16[2,208,384]{2,1,0:T(8,128)(2,1)S(1)}, bf16[2,208,384]{2,1,0:T(8,128)(2,1)S(1)}, u32[]{:S(2)}, u32[]{:S(2)}) %collective-permute-start.25) | collective-permute-done | bytes 319520 | tf_op jit(solution)/shard_map/ppermute | solution.py:20
  193.2 4.9 %shard_map.422 = (f32[768,1536]{1,0:T(8,128)}, f32[192,384]{1,0:T(8,128)}, f32[1536,768]{1,0:T(8,128)}, f32[192,384]{1,0:T(8,128)}) custom-call(s32[4]{0:T(128)S(1)} %pad_add_fusion.refs_0_, bf16[2,208,384]{2,1,0:T(8,128)(2,1)S(1)} %pad_maximum_fusion.4.refs_1_, bf16[2,208,384]{2,1,0:T(8,128)(2,1)S(1)} %collective-permute-done.32.refs_2_, ...), custom_call_target="tpu_custom_call" | custom-call | flops 100000000 | bytes 15138832 | tf_op jit(solution)/shard_map/pallas_call | solution.py:85
  200.2 3.1 %shard_map.421 = (f32[3,768,384]{2,1,0:T(8,128)}, f32[384,768]{1,0:T(8,128)}, f32[3,192,96]{2,1,0:T(8,128)}, f32[96,192]{1,0:T(8,128)}, f32[2,768]{1,0:T(2,128)}...) custom-call(s32[4]{0:T(128)S(1)} %pad_add_fusion.refs_0_, ...), custom_call_target="tpu_custom_call" | custom-call | flops 100000000 | bytes 7603984 | tf_op jit(solution)/shard_map/pallas_call | solution.py:85
  (165 shorter events, 74.3 us)
Async XLA Ops:
  0.7 14.5 %collective-permute-start = (bf16[256,768]{1,0:T(8,128)(2,1)}, bf16[256,768]{1,0:T(8,128)(2,1)S(1)}, u32[]{:S(2)}, u32[]{:S(2)}) collective-permute-start(bf16[256,768]{1,0:T(8,128)(2,1)} %refs_5_.9), channel_id=1, source_target_pairs={{0,2},{2,0},{4,6},{6,4},{8,10},{10,8},{12,14},{14,12},{16,18},{18,... | collective-permute-start | bytes 1179656 | tf_op jit(solution)/shard_map/ppermute | solution.py:20
  29.4 14.1 %collective-permute-start.6 = (bf16[128,1024]{1,0:T(8,128)(2,1)S(1)}, bf16[128,1024]{1,0:T(8,128)(2,1)S(1)}, u32[]{:S(2)}, u32[]{:S(2)}) collective-permute-start(bf16[128,1024]{1,0:T(8,128)(2,1)S(1)} %get-tuple-element.104), channel_id=1, source_target_pairs={{0,4},{2,6},{4,0},{6,2},{8,12},{10,14},{12,8},{14,10},{16,20},{18,... | collective-permute-start | bytes 786440 | tf_op jit(solution)/shard_map/ppermute | solution.py:20
  48.2 15.5 %collective-permute-start.9 = (f32[256,1024]{1,0:T(8,128)S(1)}, f32[256,1024]{1,0:T(8,128)S(1)}, u32[]{:S(2)}, u32[]{:S(2)}) collective-permute-start(f32[256,1024]{1,0:T(8,128)S(1)} %get-tuple-element.105.refs_1_), channel_id=1, source_target_pairs={{0,1},{1,0},{2,3},{3,2},{4,5},{5,4},{6,7},{7,6},{8,9},{9,8},{10,11... | collective-permute-start | bytes 3145736 | tf_op jit(solution)/shard_map/ppermute | solution.py:20
  64.6 14.8 %collective-permute-start.10 = (bf16[256,960]{1,0:T(8,128)(2,1)S(1)}, bf16[256,960]{1,0:T(8,128)(2,1)S(1)}, u32[]{:S(2)}, u32[]{:S(2)}) collective-permute-start(bf16[256,960]{1,0:T(8,128)(2,1)S(1)} %get-tuple-element.114.refs_13_.refs_9_), channel_id=1, source_target_pairs={{0,2},{2,0},{4,6},{6,4},{8,10},{10,8},{12,14},{14,12},{16,18},{18,... | collective-permute-start | bytes 1474568 | tf_op jit(solution)/shard_map/ppermute | solution.py:20
  72.5 21.2 %collective-permute-start.28 = (bf16[2,208,384]{2,1,0:T(8,128)(2,1)S(1)}, bf16[2,208,384]{2,1,0:T(8,128)(2,1)S(1)}, u32[]{:S(2)}, u32[]{:S(2)}) collective-permute-start(bf16[2,208,384]{2,1,0:T(8,128)(2,1)S(1)} %get-tuple-element.125), channel_id=1, source_target_pairs={{0,8},{2,10},{4,12},{6,14},{8,0},{10,2},{12,4},{14,6},{16,24},{18,... | collective-permute-start | bytes 958472 | tf_op jit(solution)/shard_map/ppermute | solution.py:20
  74.2 16.5 %collective-permute-start.16 = (f32[32,384]{1,0:T(8,128)S(1)}, f32[32,384]{1,0:T(8,128)S(1)}, u32[]{:S(2)}, u32[]{:S(2)}) collective-permute-start(f32[32,384]{1,0:T(8,128)S(1)} %get-tuple-element.126.refs_11_), channel_id=1, source_target_pairs={{0,2},{2,0},{4,6},{6,4},{8,10},{10,8},{12,14},{14,12},{16,18},{18,... | collective-permute-start | bytes 147464 | tf_op jit(solution)/shard_map/ppermute | solution.py:20
  89.0 41.6 %collective-permute-start.11 = (f32[256,1024]{1,0:T(8,128)S(1)}, f32[256,1024]{1,0:T(8,128)S(1)}, u32[]{:S(2)}, u32[]{:S(2)}) collective-permute-start(f32[256,1024]{1,0:T(8,128)S(1)} %shard_map.417.refs_1_), channel_id=1, source_target_pairs={{0,1},{1,0},{2,3},{3,2},{4,5},{5,4},{6,7},{7,6},{8,9},{9,8},{10,11... | collective-permute-start | bytes 3145736 | tf_op jit(solution)/shard_map/ppermute | solution.py:20
  92.8 19.8 %collective-permute-start.17 = (bf16[4,208,384]{2,1,0:T(8,128)(2,1)S(1)}, bf16[4,208,384]{2,1,0:T(8,128)(2,1)S(1)}, u32[]{:S(2)}, u32[]{:S(2)}) collective-permute-start(bf16[4,208,384]{2,1,0:T(8,128)(2,1)S(1)} %get-tuple-element.128), channel_id=1, source_target_pairs={{0,4},{2,6},{4,0},{6,2},{8,12},{10,14},{12,8},{14,10},{16,20},{18,... | collective-permute-start | bytes 1916936 | tf_op jit(solution)/shard_map/ppermute | solution.py:20
  112.9 17.2 %collective-permute-start.18 = (bf16[2,208,384]{2,1,0:T(8,128)(2,1)S(1)}, bf16[2,208,384]{2,1,0:T(8,128)(2,1)S(1)}, u32[]{:S(2)}, u32[]{:S(2)}) collective-permute-start(bf16[2,208,384]{2,1,0:T(8,128)(2,1)S(1)} %pad_maximum_fusion.2), channel_id=1, source_target_pairs={{0,8},{2,10},{4,12},{6,14},{8,0},{10,2},{12,4},{14,6},{16,24},{18,... | collective-permute-start | bytes 958472 | tf_op jit(solution)/shard_map/ppermute | solution.py:20
  113.0 19.8 %collective-permute-start.39 = (bf16[2,208,384]{2,1,0:T(8,128)(2,1)S(1)}, bf16[2,208,384]{2,1,0:T(8,128)(2,1)S(1)}, u32[]{:S(2)}, u32[]{:S(2)}) collective-permute-start(bf16[2,208,384]{2,1,0:T(8,128)(2,1)S(1)} %pad_maximum_fusion.4.refs_1_), channel_id=1, source_target_pairs={{0,16},{2,18},{4,20},{6,22},{8,24},{10,26},{12,28},{14,30},{16,0},... | collective-permute-start | bytes 958472 | tf_op jit(solution)/shard_map/ppermute | solution.py:20
  115.5 24.9 %collective-permute-start.35 = (bf16[2,208,384]{2,1,0:T(8,128)(2,1)S(1)}, bf16[2,208,384]{2,1,0:T(8,128)(2,1)S(1)}, u32[]{:S(2)}, u32[]{:S(2)}) collective-permute-start(bf16[2,208,384]{2,1,0:T(8,128)(2,1)S(1)} %pad_maximum_fusion.4.refs_1_), channel_id=1, source_target_pairs={{0,8},{2,10},{4,12},{6,14},{8,0},{10,2},{12,4},{14,6},{16,24},{18,... | collective-permute-start | bytes 958472 | tf_op jit(solution)/shard_map/ppermute | solution.py:20
  130.6 21.5 %collective-permute-start.33 = (bf16[2,208,384]{2,1,0:T(8,128)(2,1)S(1)}, bf16[2,208,384]{2,1,0:T(8,128)(2,1)S(1)}, u32[]{:S(2)}, u32[]{:S(2)}) collective-permute-start(bf16[2,208,384]{2,1,0:T(8,128)(2,1)S(1)} %pad_maximum_fusion.4.refs_1_), channel_id=1, source_target_pairs={{0,4},{2,6},{4,0},{6,2},{8,12},{10,14},{12,8},{14,10},{16,20},{18,... | collective-permute-start | bytes 958472 | tf_op jit(solution)/shard_map/ppermute | solution.py:20
  132.8 21.2 %collective-permute-start.43 = (bf16[2,208,384]{2,1,0:T(8,128)(2,1)S(1)}, bf16[2,208,384]{2,1,0:T(8,128)(2,1)S(1)}, u32[]{:S(2)}, u32[]{:S(2)}) collective-permute-start(bf16[2,208,384]{2,1,0:T(8,128)(2,1)S(1)} %collective-permute-done.39.refs_9_), channel_id=1, source_target_pairs={{0,8},{2,10},{4,12},{6,14},{8,0},{10,2},{12,4},{14,6},{16,24},{18,... | collective-permute-start | bytes 958472 | tf_op jit(solution)/shard_map/ppermute | solution.py:20
  140.4 15.7 %collective-permute-start.40 = (bf16[2,208,384]{2,1,0:T(8,128)(2,1)S(1)}, bf16[2,208,384]{2,1,0:T(8,128)(2,1)S(1)}, u32[]{:S(2)}, u32[]{:S(2)}) collective-permute-start(bf16[2,208,384]{2,1,0:T(8,128)(2,1)S(1)} %collective-permute-done.39.refs_9_), channel_id=1, source_target_pairs={{0,2},{2,0},{4,6},{6,4},{8,10},{10,8},{12,14},{14,12},{16,18},{18,... | collective-permute-start | bytes 958472 | tf_op jit(solution)/shard_map/ppermute | solution.py:20
  154.1 15.0 %collective-permute-start.41 = (bf16[2,208,384]{2,1,0:T(8,128)(2,1)S(1)}, bf16[2,208,384]{2,1,0:T(8,128)(2,1)S(1)}, u32[]{:S(2)}, u32[]{:S(2)}) collective-permute-start(bf16[2,208,384]{2,1,0:T(8,128)(2,1)S(1)} %collective-permute-done.39.refs_9_), channel_id=1, source_target_pairs={{0,4},{2,6},{4,0},{6,2},{8,12},{10,14},{12,8},{14,10},{16,20},{18,... | collective-permute-start | bytes 958472 | tf_op jit(solution)/shard_map/ppermute | solution.py:20
  154.2 21.7 %collective-permute-start.45 = (bf16[2,208,384]{2,1,0:T(8,128)(2,1)S(1)}, bf16[2,208,384]{2,1,0:T(8,128)(2,1)S(1)}, u32[]{:S(2)}, u32[]{:S(2)}) collective-permute-start(bf16[2,208,384]{2,1,0:T(8,128)(2,1)S(1)} %collective-permute-done.43.refs_13_), channel_id=1, source_target_pairs={{0,4},{2,6},{4,0},{6,2},{8,12},{10,14},{12,8},{14,10},{16,20},{18,... | collective-permute-start | bytes 958472 | tf_op jit(solution)/shard_map/ppermute | solution.py:20
  156.1 20.1 %collective-permute-start.21 = (bf16[2,208,384]{2,1,0:T(8,128)(2,1)S(1)}, bf16[2,208,384]{2,1,0:T(8,128)(2,1)S(1)}, u32[]{:S(2)}, u32[]{:S(2)}) collective-permute-start(bf16[2,208,384]{2,1,0:T(8,128)(2,1)S(1)} %pad_maximum_fusion.3.refs_1_), channel_id=1, source_target_pairs={{0,8},{2,10},{4,12},{6,14},{8,0},{10,2},{12,4},{14,6},{16,24},{18,... | collective-permute-start | bytes 958472 | tf_op jit(solution)/shard_map/ppermute | solution.py:20
  162.2 15.9 %collective-permute-start.38 = (bf16[2,208,384]{2,1,0:T(8,128)(2,1)S(1)}, bf16[2,208,384]{2,1,0:T(8,128)(2,1)S(1)}, u32[]{:S(2)}, u32[]{:S(2)}) collective-permute-start(bf16[2,208,384]{2,1,0:T(8,128)(2,1)S(1)} %collective-permute-done.37.refs_7_), channel_id=1, source_target_pairs={{0,2},{2,0},{4,6},{6,4},{8,10},{10,8},{12,14},{14,12},{16,18},{18,... | collective-permute-start | bytes 958472 | tf_op jit(solution)/shard_map/ppermute | solution.py:20
  162.5 20.3 %collective-permute-start.42 = (bf16[2,208,384]{2,1,0:T(8,128)(2,1)S(1)}, bf16[2,208,384]{2,1,0:T(8,128)(2,1)S(1)}, u32[]{:S(2)}, u32[]{:S(2)}) collective-permute-start(bf16[2,208,384]{2,1,0:T(8,128)(2,1)S(1)} %collective-permute-done.40.refs_10_), channel_id=1, source_target_pairs={{0,4},{2,6},{4,0},{6,2},{8,12},{10,14},{12,8},{14,10},{16,20},{18,... | collective-permute-start | bytes 958472 | tf_op jit(solution)/shard_map/ppermute | solution.py:20
  169.1 14.0 %collective-permute-start.44 = (bf16[2,208,384]{2,1,0:T(8,128)(2,1)S(1)}, bf16[2,208,384]{2,1,0:T(8,128)(2,1)S(1)}, u32[]{:S(2)}, u32[]{:S(2)}) collective-permute-start(bf16[2,208,384]{2,1,0:T(8,128)(2,1)S(1)} %collective-permute-done.43.refs_13_), channel_id=1, source_target_pairs={{0,2},{2,0},{4,6},{6,4},{8,10},{10,8},{12,14},{14,12},{16,18},{18,... | collective-permute-start | bytes 958472 | tf_op jit(solution)/shard_map/ppermute | solution.py:20
  176.2 13.4 %collective-permute-start.25 = (bf16[2,208,384]{2,1,0:T(8,128)(2,1)S(1)}, bf16[2,208,384]{2,1,0:T(8,128)(2,1)S(1)}, u32[]{:S(2)}, u32[]{:S(2)}) collective-permute-start(bf16[2,208,384]{2,1,0:T(8,128)(2,1)S(1)} %collective-permute-done.21.refs_2_), channel_id=1, source_target_pairs={{0,4},{2,6},{4,0},{6,2},{8,12},{10,14},{12,8},{14,10},{16,20},{18,... | collective-permute-start | bytes 958472 | tf_op jit(solution)/shard_map/ppermute | solution.py:20
  178.1 15.1 %collective-permute-start.46 = (bf16[2,208,384]{2,1,0:T(8,128)(2,1)S(1)}, bf16[2,208,384]{2,1,0:T(8,128)(2,1)S(1)}, u32[]{:S(2)}, u32[]{:S(2)}) collective-permute-start(bf16[2,208,384]{2,1,0:T(8,128)(2,1)S(1)} %collective-permute-done.45.refs_15_), channel_id=1, source_target_pairs={{0,2},{2,0},{4,6},{6,4},{8,10},{10,8},{12,14},{14,12},{16,18},{18,... | collective-permute-start | bytes 958472 | tf_op jit(solution)/shard_map/ppermute | solution.py:20
  182.8 15.4 %collective-permute-start.24 = (bf16[2,208,384]{2,1,0:T(8,128)(2,1)S(1)}, bf16[2,208,384]{2,1,0:T(8,128)(2,1)S(1)}, u32[]{:S(2)}, u32[]{:S(2)}) collective-permute-start(bf16[2,208,384]{2,1,0:T(8,128)(2,1)S(1)} %pad_maximum_fusion.3.refs_1_), channel_id=1, source_target_pairs={{0,4},{2,6},{4,0},{6,2},{8,12},{10,14},{12,8},{14,10},{16,20},{18,... | collective-permute-start | bytes 958472 | tf_op jit(solution)/shard_map/ppermute | solution.py:20
  183.1 15.1 %collective-permute-start.23 = (bf16[2,208,384]{2,1,0:T(8,128)(2,1)S(1)}, bf16[2,208,384]{2,1,0:T(8,128)(2,1)S(1)}, u32[]{:S(2)}, u32[]{:S(2)}) collective-permute-start(bf16[2,208,384]{2,1,0:T(8,128)(2,1)S(1)} %collective-permute-done.21.refs_2_), channel_id=1, source_target_pairs={{0,2},{2,0},{4,6},{6,4},{8,10},{10,8},{12,14},{14,12},{16,18},{18,... | collective-permute-start | bytes 958472 | tf_op jit(solution)/shard_map/ppermute | solution.py:20
  (51 other events, 417.8 us)

commit v3 on v2

--- a/solution.py
+++ b/solution.py
@@ -141,8 +141,9 @@
     for first, text, layout in ((OB, ob_t, ob_l), (GAIN, g_t, g_l), (SHIFT, s_t, s_l)):
         pack_out[first : first + 2, :wide] = text[...].astype(F32)
         pack_out[first : first + 2, wide : wide + thin] = layout[...].astype(F32)
-    pack_out[UP_T : UP_T + 1, :] = ub_t[...].astype(F32)
-    pack_out[UP_L : UP_L + 1, : ub_l.shape[1]] = ub_l[...].astype(F32)
+    pack_out[UP_T : UP_T + 1, :] = ub_t[...].astype(F32)[None, :]
+    bias_l = ub_l[...].astype(F32)[None, :]
+    pack_out[UP_L : UP_L + 1, : bias_l.shape[1]] = bias_l
     quarter = idx[1] * 2 + idx[0]
     count = up_l.shape[1] // 4
 
@@ -152,7 +153,7 @@
             value = jnp.where(quarter == q, ref[:, count * q : count * (q + 1)].astype(F32), value)
         return value
 
-    pack_out[UP_Q : UP_Q + 1, :count] = cut(ub_l)
+    pack_out[UP_Q : UP_Q + 1, :count] = cut(bias_l)
     quarter_out[:, :count] = cut(up_l).astype(BF)
     quarter_out[:, LANES : LANES + count] = cut(dn_l).astype(BF)
     cl_out[...] = turned(cl[...]).astype(BF)
@@ -347,13 +348,26 @@
         part_out[:, lo:hi] = total
 
 
+def turning_kernel(
+    idx, hidden, part, back, ct, cl, keep, pack, slope_t, slope_l, up_t, dn_t, up_l, dn_l,
+    rt_out, rl_out, second_out, low_out, mine_out, sums_out, part_out, bias_t, bias_l,
+):
+    second_norm_kernel(
+        idx, hidden, part, back, ct, cl, keep, pack,
+        rt_out, rl_out, second_out, low_out, mine_out, sums_out,
+    )
+    ffn_back_kernel(
+        low_out, slope_t, slope_l, up_t, dn_t, up_l, dn_l, part_out, bias_t, bias_l
+    )
+
+
 def pieces(columns, piece):
     return [(at, min(at + piece, columns)) for at in range(0, columns, piece)]
 
 
 def first_norm_kernel(
-    second, part, back, normed_in, inverse_in, pack, sums_two, bias_t, bias_l,
-    first_out, low_out, small_out,
+    idx, second, part, back, normed_in, inverse_in, pack, sums_two, bias_t, bias_l,
+    first_out, low_out, mine_out, small_out,
 ):
     whole, piece = second.shape[1], small_out.shape[1]
     width = whole * 4 // 5
@@ -378,6 +392,8 @@
         sums[0].append(jnp.sum(upstream * normed, axis=0, keepdims=True))
         sums[1].append(jnp.sum(upstream, axis=0, keepdims=True))
         sums[2].append(jnp.sum(low.astype(F32), axis=0, keepdims=True))
+    half = mine_out.shape[0]
+    mine_out[...] = low_out[pl.ds(pl.multiple_of(idx[3] * half, half), half), :]
     for kind in range(3):
         put(jnp.concatenate(sums[kind], axis=1))
         put(sums_two[kind : kind + 1, :])
@@ -388,8 +404,8 @@
 def unit_grads_kernel(idx, *refs):
     (
         low_parts, grad_parts, (up_t, dn_t, quarters, pack_in),
-        (up_keep, up_send, dn_keep, dn_send),
-        (low, grad, w_up, w_dn, w_l, pack, held, sems),
+        (keep, send, act_out, grad),
+        (low, w_up, w_dn, w_l, pack, held, sems),
     ) = refs[:5], refs[5:10], refs[10:14], refs[14:18], refs[18:]
     quarter = idx[1] * 2 + idx[0]
     zz = idx[2]
@@ -412,7 +428,6 @@
         c.wait()
     width = w_up.shape[0]
     piece = width // 4
-    slot_rows = 16
 
     def grads(lo, hi, up, bias, down):
         before = dot(low[:, lo:hi], up) + bias
@@ -434,43 +449,58 @@
         w_l[:, LANES : LANES + count],
     )
 
-    def place_layout(matrix):
-        pad = jnp.zeros((matrix.shape[0], LANES - matrix.shape[1]), F32)
-        padded = jnp.concatenate([matrix, pad], axis=1)
-        for k in range(4):
-            for slot in range(3):
-                first = slot_rows * (3 * k + slot)
-                held[k ^ zz, piece : piece + slot_rows, LANES * slot : LANES * (slot + 1)] = padded[
-                    first : first + slot_rows
-                ]
-
-    def hand_out(keep, send):
-        for at in range(2):
-            keep[at] = held[2 * at]
-            send[at] = held[2 * at + 1].astype(BF)
-
+    act_out[:, :units] = act_t
+    act_out[:, units:] = widened(act_l)
     up_grad = dot_tn(low[:, :width], back_t)
     for k in range(4):
         held[k ^ zz, :piece, :] = up_grad[piece * k : piece * (k + 1)]
-    place_layout(dot_tn(low[:, width:whole], back_l))
-    hand_out(up_keep, up_send)
-    down_grad = dot_tn(act_t, grad[:, :width])
-    part = piece // 2
+    place_layout(held, zz, dot_tn(low[:, width:whole], widened(back_l)))
+    hand_out(held, keep, send)
+
+
+def widened(matrix):
+    pad = jnp.zeros((matrix.shape[0], LANES - matrix.shape[1]), matrix.dtype)
+    return jnp.concatenate([matrix, pad], axis=1)
+
+
+def place_layout(held, zz, matrix):
+    piece = held.shape[1] - 16
+    for k in range(4):
+        for slot in range(3):
+            first = 16 * (3 * k + slot)
+            held[k ^ zz, piece:, LANES * slot : LANES * (slot + 1)] = matrix[first : first + 16]
+
+
+def hand_out(held, keep, send):
+    for k in range(2):
+        keep[k] = held[2 * k]
+        send[k] = held[2 * k + 1].astype(BF)
+
+
+def down_grads_kernel(idx, act, grad, keep, send, held):
+    zz = idx[2]
+    units, width = held.shape[2], 2 * held.shape[2]
+    down_grad = dot_tn(act[:, :units], grad[:, :width])
+    part = (held.shape[1] - 16) // 2
     for k in range(4):
         for side in range(2):
             held[k ^ zz, part * side : part * (side + 1), :] = down_grad[
                 part * k : part * (k + 1), units * side : units * (side + 1)
             ]
-    place_layout(dot_tn(grad[:, width:whole], act_l))
-    hand_out(dn_keep, dn_send)
+    place_layout(held, zz, dot_tn(grad[:, width : width + width // 4], act[:, units:]))
+    hand_out(held, keep, send)
 
 
 def attention_back_kernel(
-    k_all, v_all, xt, xl, xt_p, xl_p, wt, bt, wl, bl, keys, out_t, out_l, ag_own, ag_p,
-    dq, dk, dv, context, q_all, g_all,
+    idx, k_all, v_all, xt, xl, xt_p, xl_p, wt, bt, wl, bl, keys, out_t, out_l, ag_own, ag_far, ag_back,
+    dq, dk, dv, context, ag_p, q_all, g_all,
 ):
     rows, width = xt.shape[0], wt.shape[2]
     wide = out_t.shape[1]
+    half = ag_far.shape[0]
+    core = idx[3]
+    ag_p[pl.ds(pl.multiple_of(core * half, half), half), :] = ag_far[...]
+    ag_p[pl.ds(pl.multiple_of((1 - core) * half, half), half), :] = ag_back[...]
     for at, text_rows, layout_columns in ((0, xt, xl), (rows, xt_p, xl_p)):
 
         def write(text_part, layout_part, at=at):
@@ -598,9 +628,9 @@
             held[(y ^ by) * 4 + (z ^ zz), 4 * thin : 4 * thin + 16, :] = jnp.concatenate(
                 [packed, sums[rest * eighth : rest * (eighth + 1), :]], axis=0
             )
-    for k in range(4):
-        keep_out[k] = held[k]
-        send_out[k] = held[4 + k].astype(BF)
+    for at, k in enumerate((0, 2, 1, 3)):
+        keep_out[at] = held[k]
+        send_out[at] = held[4 + k].astype(BF)
 
 
 def pieces_of(refs, idx):
@@ -688,41 +718,73 @@
             value = take(whole)
             text_out[row : row + 1, :] = value[:, :wide]
             layout_out[row : row + 1, :] = value[:, wide:]
-    ubt[...] = take(ubt.shape[1])
-    ubl[...] = take(ubl.shape[1])
+    ubt[...] = take(ubt.shape[0])[0]
+    ubl[...] = take(ubl.shape[0])[0]
     for row in range(2):
         value = take(qvt.shape[1] + LANES)
         qvt[row : row + 1, :] = value[:, : qvt.shape[1]]
         qvl[row : row + 1, :] = value[:, qvt.shape[1] : qvt.shape[1] + qvl.shape[1]]
 
 
-def gathered(own):
-    even = jnp.stack([own, exchange(own, 8)])
-    odd = exchange(even, 4)
-    even_x, odd_y = exchange(even, 1), exchange(odd, 2)
-    even_y, odd_x = exchange(even, 2), exchange(odd, 1)
-    even_xy, odd_xy = exchange(even_x, 2), exchange(odd_y, 1)
-    return even, odd, even_x, odd_x, even_y, odd_y, even_xy, odd_xy
-
-
-def gathered_singly(own):
-    found = {0: own, 4: exchange(own, 4), 8: exchange(own, 8)}
-    found[12] = exchange(found[8], 4)
-    for z, first, second in ((0, 1, 2), (4, 2, 1), (8, 1, 2), (12, 2, 1)):
-        found[z + first] = exchange(found[z], first)
-        found[z + second] = exchange(found[z], second)
-        found[z + 3] = exchange(found[z + first], second)
-    return [found[at] for at in range(16)]
-
-
-def reduced(keep, far):
-    total = keep + far.astype(F32)
-    own = total[0] + exchange(total[1].astype(BF), 8).astype(F32)
-    mask = 16
-    while mask < lax.axis_size("seq"):
-        own = own + exchange(own, mask)
-        mask *= 2
-    return own.astype(BF)
+ORDER = (
+    "down4", "up8", "down8", "y", 4, 1, 8, "z4", 6, 5, 2, 10, "z8", 9, 3, 12, 7, "even", 11, 13, 14,
+    "odd", "even1", "even2", "odd2", 15, "odd1", "even3", "odd3",
+)
+
+
+def reduced_and_gathered(token, up, up_far, down_keep, down_far, keep, far):
+    last = token
+    coming, found = {"up8": up_far, "down4": down_far, "y": far}, {}
+
+    def send(shard, mask, name):
+        coming[name] = exchange(shard, mask)
+
+    def beyond(own):
+        mask = 16
+        while mask < lax.axis_size("seq"):
+            own = own + exchange(own, mask)
+            mask *= 2
+        return own.astype(BF)
+
+    for name in ORDER:
+        last = found[name] = tied(coming[name], last)
+        if name == "down4":
+            down = down_keep + last.astype(F32)
+            send(down[1].astype(BF), 8, "down8")
+        elif name == "down8":
+            up_own = beyond(up + found["up8"].astype(F32))
+            found[0] = jnp.stack([up_own, beyond(down[0] + last.astype(F32))])
+            for mask in (4, 1, 8, 2):
+                send(found[0], mask, mask)
+        elif name == "y":
+            total = keep + last.astype(F32)
+            send(total[2:].astype(BF), 4, "z4")
+        elif name == "z4":
+            total = total[:2] + last.astype(F32)
+            send(total[1].astype(BF), 8, "z8")
+        elif name == "z8":
+            own = beyond(total[0] + last.astype(F32))
+            send(own, 8, "even")
+        elif name == "even":
+            found["even"] = jnp.stack([own, last])
+            for mask, to in ((4, "odd"), (1, "even1"), (2, "even2")):
+                send(found["even"], mask, to)
+        elif name == "odd":
+            for mask in (1, 2):
+                send(last, mask, f"odd{mask}")
+        elif name == "even1":
+            send(last, 2, "even3")
+        elif name == "odd2":
+            send(last, 1, "odd3")
+        elif name in (4, 8, 12):
+            for mask in (1, 2) if name != 8 else (4, 2, 1):
+                send(last, mask, name + mask)
+        elif name in (1, 9):
+            send(last, 2, name + 2)
+        elif name in (6, 14):
+            send(last, 1, name + 1)
+    names = ("even", "odd", "even1", "odd1", "even2", "odd2", "even3", "odd3")
+    return [found[at] for at in range(16)], [found[name] for name in names]
 
 
 def per_device(
@@ -779,14 +841,14 @@
             shape((thin, 2 * LANES), BF),
         ],
         idx, cot_turned, intersection_flags[None, :], text_out_bias, text_gains, text_shifts,
-        text_up_bias[None, :], layout_out_bias, layout_gains, layout_shifts,
-        layout_up_bias[None, :], layout_up, down_turned, smem=1, far=range(1, 13), pin=range(4),
+        text_up_bias, layout_out_bias, layout_gains, layout_shifts,
+        layout_up_bias, layout_up, down_turned, smem=1, far=range(1, 13), pin=range(4),
     )
     qkv_weights = (text_qkv, text_qv_bias, layout_qkv, layout_qv_bias)
     q_own, k_own, v_own, layout_rows = call(
         project_kernel,
         [shape((rows, padded), BF)] * 3 + [shape((rows, thin), BF)],
-        text_in, layout_turned, *qkv_weights, pin=range(4),
+        text_in, layout_turned, *qkv_weights, pin=range(4), after=[pack], far=range(6),
     )
     attended, k_all, v_all = call(
         attend_kernel,
@@ -811,9 +873,11 @@
         low, pack, text_up, text_down, layout_up, down_turned, flops=14 * 10**8, room=20, pin=[0, 1],
     )
     ffn_back = over_cores(ffn)
-    low_far = [exchange(low_mine, mask) for mask in (1, 2, 3)]
-    text_result, layout_result, second, grad_low, grad_mine, sums_two = call(
-        second_norm_kernel,
+    low_x, low_y = exchange(low_mine, 1), exchange(low_mine, 2)
+    (
+        text_result, layout_result, second, grad_low, grad_mine, sums_two, hidden_part, bias_t, bias_l,
+    ) = call(
+        turning_kernel,
         [
             shape((rows, wide), BF),
             shape((thin, rows), BF),
@@ -821,34 +885,50 @@
             shape((rows, wide + 2 * LANES), BF),
             shape((half, wide + 2 * LANES), BF),
             shape((3, whole), F32),
+            sent,
+            shape((1, units), F32),
+            shape((1, units_l), F32),
         ],
-        idx, hidden, ffn, ffn_back, text_cot, cot_rows, keep_rows, pack, smem=1, pin=[2, 3, 5],
-    )
-    grad_far = [exchange(grad_mine, mask) for mask in (1, 2, 3)]
-    low_back = Near(over_cores(jnp.concatenate(low_far, axis=0)))
-    hidden_part, bias_t, bias_l = call(
-        ffn_back_kernel,
-        [sent, shape((1, units), F32), shape((1, units_l), F32)],
-        grad_low, slope_t, slope_l, text_up, text_down, layout_up, down_turned, flops=14 * 10**8,
-        room=20, pin=[1, 2], after=[low_back],
-    )
-    first, attended_grad, small = call(
+        idx, hidden, ffn, ffn_back, text_cot, cot_rows, keep_rows, pack, slope_t, slope_l, text_up,
+        text_down, layout_up, down_turned, smem=1, pin=[2, 3, 5, 7, 8], flops=14 * 10**8, room=20,
+    )
+    grad_x, grad_y = exchange(grad_mine, 1), exchange(grad_mine, 2)
+    low_x, low_y = tied(low_x, grad_mine), tied(low_y, grad_mine)
+    low_xy = exchange(low_x, 2)
+    hidden_back = over_cores(tied(tied(hidden_part, low_x), low_y))
+    low_far = [low_x, low_y, tied(low_xy, hidden_part)]
+    low_back = over_cores(jnp.concatenate(low_far, axis=0))
+    grad_x = tied(grad_x, low_far[2])
+    grad_xy = exchange(grad_x, 2)
+    first, attended_grad, attended_mine, small = call(
         first_norm_kernel,
-        [shape((rows, whole), F32), shape((rows, whole), BF), shape((32, width), F32)],
-        second, hidden_part, over_cores(hidden_part), normed, inverse, pack, sums_two, bias_t, bias_l, pin=[0],
-    )
-    attended_grad_other = exchange(attended_grad, 1)
-
-    grad_cat = jnp.concatenate(grad_far, axis=0)
+        [
+            shape((rows, whole), F32),
+            shape((rows, whole), BF),
+            shape((half, whole), BF),
+            shape((32, width), F32),
+        ],
+        idx, second, hidden_part, hidden_back, normed, inverse, pack, sums_two, bias_t, bias_l, smem=1, pin=[0, 1],
+        after=[grad_x],
+    )
+    attended_far = exchange(attended_mine, 1)
+    grad_y = tied(grad_y, small)
+    attended_far = tied(attended_far, grad_y)
+    attended_back = over_cores(attended_far)
+    grad_far = [grad_x, grad_y, tied(grad_xy, attended_far)]
     low_parts = [low, *low_far, low_back]
-    grad_parts = [grad_low, *grad_far, over_cores(tied(grad_cat, small))]
+    grad_parts = [grad_low, *grad_far, over_cores(jnp.concatenate(grad_far, axis=0))]
     block = (2, wide // 4 + 16, width)
-    up_keep, up_send, down_keep, down_send = call(
+    up_keep, up_send, activated, grad_rows = call(
         unit_grads_kernel,
-        [shape(block, F32), shape(block, BF)] * 2,
+        [
+            shape(block, F32),
+            shape(block, BF),
+            shape((4 * rows, units // 4 + LANES), BF),
+            shape((4 * rows, wide + 2 * LANES), BF),
+        ],
         idx, *low_parts, *grad_parts, text_up, text_down, quarters, pack,
         scratch=[
-            pltpu.VMEM((4 * rows, wide + 2 * LANES), BF),
             pltpu.VMEM((4 * rows, wide + 2 * LANES), BF),
             pltpu.VMEM((wide, units // 4), BF),
             pltpu.VMEM((units // 4, wide), BF),
@@ -857,22 +937,33 @@
             pltpu.VMEM((4,) + block[1:], F32),
             pltpu.SemaphoreType.DMA((14,)),
         ],
-        smem=1, anys=range(1, 15), flops=24 * 10**8, room=24,
-    )
-    up_far, down_far = exchange(up_send, 4), exchange(down_send, 4)
+        smem=1, anys=range(1, 15), flops=18 * 10**8, room=24, pin=[2, 3],
+    )
+    up_far = exchange(up_send, 4)
+    down_keep, down_send = call(
+        down_grads_kernel,
+        [shape(block, F32), shape(block, BF)],
+        idx, activated, grad_rows, scratch=[pltpu.VMEM((4,) + block[1:], F32)], smem=1,
+        flops=7 * 10**8, after=[up_send],
+    )
+    down_far = exchange(down_send, 4)
     small_other = exchange(tied(small, up_send), 1)
 
-    dq, dk, dv, context = call(
+    dq, dk, dv, context, attended_grad_other = call(
         attention_back_kernel,
-        [shape((2 * rows, padded), BF)] * 4,
-        k_all, v_all, text_in, layout_turned, text_other, layout_other, *qkv_weights, keys, text_out,
-        layout_out, attended_grad, attended_grad_other,
-        scratch=[pltpu.VMEM((2 * rows, padded), BF)] * 2, flops=50 * 10**8, room=24, pin=range(4),
-    )
+        [shape((2 * rows, padded), BF)] * 4 + [shape((rows, whole), BF)],
+        idx, k_all, v_all, text_in, layout_turned, text_other, layout_other, *qkv_weights, keys,
+        text_out, layout_out, attended_grad, attended_far, attended_back,
+        scratch=[pltpu.VMEM((2 * rows, padded), BF)] * 2, smem=1, flops=50 * 10**8, room=24,
+        pin=[0, 1, 2, 4], after=[down_send],
+    )
+    up_total = up_keep + tied(up_far, context).astype(F32)
+    up_part = up_total[1].astype(BF)
     used = 6 * len(pieces(whole, width)) + len(pieces(units, width)) + len(pieces(units_l, width))
+    block = (4,) + block[1:]
     keep, send = call(
         partial(attention_grads_kernel, used),
-        [shape((4,) + block[1:], F32), shape((4,) + block[1:], BF)],
+        [shape(block, F32), shape(block, BF)],
         idx, dq, dk, dv, context, text_in, layout_turned, text_other, layout_other, attended_grad,
         attended_grad_other, small, small_other,
         scratch=[
@@ -880,32 +971,28 @@
             pltpu.VMEM((8,) + block[1:], F32),
             pltpu.VMEM(small.shape, F32),
         ],
-        smem=1, flops=10**9, room=24,
+        smem=1, flops=10**9, room=24, after=[up_part],
     )
     send_far = exchange(send, 2)
-    up_own = reduced(up_keep, tied(up_far, keep))
-    down_own = reduced(down_keep, tied(down_far, keep))
     (input_part,) = call(
-        input_part_kernel, [sent], dq, dk, dv, text_qkv, layout_qkv, flops=5 * 10**8
+        input_part_kernel, [sent], dq, dk, dv, text_qkv, layout_qkv, flops=5 * 10**8, after=[send],
     )
     text_in_grad, layout_in_grad = call(
         input_grad_kernel,
         [shape((rows, wide), BF), shape((thin, rows), BF)],
         first, input_part, over_cores(input_part),
     )
-    plane = keep + send_far.astype(F32)
-    attention_own = reduced(
-        jnp.stack([plane[0], plane[2]]),
-        exchange(jnp.stack([plane[1], plane[3]]).astype(BF), 4),
+    units_pieces, attention_pieces = reduced_and_gathered(
+        keep, up_total[0], exchange(up_part, 8), down_keep, down_far, keep, send_far
     )
 
     up_t, up_l, down_t, down_l = call(
         units_result_kernel,
         [shape(a.shape, F32) for a in (text_up, layout_up, text_down, down_turned)],
-        idx, *gathered_singly(jnp.stack([up_own, down_own])), scratch=[pltpu.VMEM((4, thin, LANES), F32)] * 2, smem=1,
+        idx, *units_pieces, scratch=[pltpu.VMEM((4, thin, LANES), F32)] * 2, smem=1,
         room=32,
     )
-    one_row = (1, units), (1, units_l)
+    one_row = (units,), (units_l,)
     kinds = [text_out_bias.shape] * 3 + [one_row[0], text_qv_bias.shape]
     kinds += [layout_out_bias.shape] * 3 + [one_row[1], layout_qv_bias.shape]
     (
@@ -915,7 +1002,7 @@
         attention_result_kernel,
         [shape(a.shape, F32) for a in (text_qkv, text_out, layout_qkv, layout_out)]
         + [shape(dims, F32) for dims in kinds],
-        idx, *gathered(attention_own),
+        idx, *attention_pieces, after=[up_l],
         scratch=[pltpu.VMEM((4, thin, LANES), F32), pltpu.VMEM((2, 8, 8, width), F32)], smem=1,
     )
     return (
@@ -930,7 +1017,7 @@
         gains_t,
         shifts_t,
         up_t,
-        ub_t[0],
+        ub_t,
         down_t,
         qkv_l,
         qv_l,
@@ -939,7 +1026,7 @@
         gains_l,
         shifts_l,
         up_l,
-        ub_l[0],
+        ub_l,
         down_l.T,
     )
 

time: 205 us -> 178 us (0.87)
  waiting for transfers between devices: 104 us -> 81.7 us
  local copies, waits for them, and re-layouts: 9.64 us -> 1.14 us
  starting transfers between devices: 44.2 us -> 47.5 us
    ppermute x47 -> x48, waiting for transfers between devices: 104 us -> 81.7 us  [exchange(): lax.ppermute(shard, axis, [(i, i ^ mask) for i in range(lax.axis_size(axi...]
    unnamed x56 -> x28, local copies, waits for them, and re-layouts: 8.33 us -> 1.04 us
    ppermute x47 -> x48, starting transfers between devices: 44.2 us -> 47.5 us  [exchange(): lax.ppermute(shard, axis, [(i, i ^ mask) for i in range(lax.axis_size(axi...]
  transfers between devices with their start and end apart: 47 -> 48, of which waited for: 21 -> 25; matrix products, arithmetic and copies ran while one was open for 1% -> 1% of each run, Pallas kernels for 15% -> 20%
where the time goes in v3:
time: 178 us
  waiting for transfers between devices  81.7 us (46%)
  starting transfers between devices  47.5 us (27%)
  Pallas kernels  44.3 us (25%)
    ppermute x48, waiting for transfers between devices, exchange(): lax.ppermute(shard, axis, [(i, i ^ mask) for i in range(lax.axis_size(axi...  81.7 us
    ppermute x48, starting transfers between devices, exchange(): lax.ppermute(shard, axis, [(i, i ^ mask) for i in range(lax.axis_size(axi...  47.5 us
    pallas_call x15, Pallas kernels, call(): pl.pallas_call(body, out_shape=tuple((pltpu.VMEM(o.shape, o.dtype) if k i...  44.3 us
  transfers between devices with their start and end apart: 48, of which 25 were waited for; matrix products, arithmetic and copies ran while one was open for 1% of the time, Pallas kernels for 20%

profile of v3, /device:TPU:0, one launch (start us, length us, event | category | flops | bytes accessed | tf_op | source)
XLA Modules:
  0.0 177.5 jit_solution(6342010486757208555)
XLA Ops:
  0.7 3.0 %collective-permute-start = (bf16[256,768]{1,0:T(8,128)(2,1)}, bf16[256,768]{1,0:T(8,128)(2,1)S(1)}, u32[]{:S(2)}, u32[]{:S(2)}) collective-permute-start(bf16[256,768]{1,0:T(8,128)(2,1)} %refs_5_.7), channel_id=1, source_target_pairs={{0,2},{2,0},{4,6},{6,4},{8,10},{10,8},{12,14},{14,12},{16,18},{18,... | collective-permute-start | bytes 1179656 | tf_op jit(solution)/shard_map/ppermute | solution.py:20
  6.5 2.7 %shard_map.408 = (bf16[256,192]{1,0:T(8,128)(2,1)S(1)}, f32[256,128]{1,0:T(8,128)S(1)}, f32[16,1536]{1,0:T(8,128)S(1)}, bf16[192,256]{1,0:T(8,128)(2,1)S(1)}) custom-call(s32[4]{0:T(128)S(1)} %pad_add_fusion.refs_0_, bf16[192,256]{1,0:T(8,128)(2,1)} %bitcast.55, s32[1,256]{1,0:T(1,128)} %bitcast.58, bf16[2,768]{1,0:T(2,128)(2,1)} %refs_3_.5, ...), custom_call_target="tpu_custom_call" | custom-call | flops 100000000 | bytes 835600 | tf_op jit(solution)/shard_map/pallas_call | solution.py:85
  9.3 2.6 %shard_map.409 = (bf16[256,512]{1,0:T(8,128)(2,1)S(1)}, bf16[256,512]{1,0:T(8,128)(2,1)S(1)}, bf16[256,512]{1,0:T(8,128)(2,1)S(1)}, bf16[256,192]{1,0:T(8,128)(2,1)S(1)}) custom-call(bf16[256,768]{1,0:T(8,128)(2,1)} %refs_5_.7, bf16[192,256]{1,0:T(8,128)(2,1)} %bitcast.50, bf16[3,768,384]{2,1,0:T(8,128)(2,1)} %refs_3_.9, bf16[2,384]{1,0:T(2,128)(2,1)} %refs_8_.5, ...), custom_call_target="tpu_custom_call" | custom-call | flops 100000000 | bytes 3356544 | tf_op jit(solution)/shard_map/pallas_call | solution.py:85
  15.3 2.6 %shard_map.410 = (f32[256,1024]{1,0:T(8,128)S(1)}, bf16[512,512]{1,0:T(8,128)(2,1)S(1)}, bf16[512,512]{1,0:T(8,128)(2,1)S(1)}) custom-call(bf16[256,512]{1,0:T(8,128)(2,1)S(1)} %get-tuple-element.129.refs_0_, bf16[256,512]{1,0:T(8,128)(2,1)S(1)} %get-tuple-element.130.refs_1_, bf16[256,512]{1,0:T(8,128)(2,1)S(1)} %get-tuple-element.131.refs_2_, ...), custom_call_target="tpu_custom_call" | custom-call | flops 100000000 | bytes 5885824 | tf_op jit(solution)/shard_map/pallas_call | solution.py:85
  18.0 2.6 %collective-permute-done.3.refs_4_ = f32[256,1024]{1,0:T(8,128)S(1)} collective-permute-done((f32[256,1024]{1,0:T(8,128)S(1)}, f32[256,1024]{1,0:T(8,128)S(1)}, u32[]{:S(2)}, u32[]{:S(2)}) %collective-permute-start.3) | collective-permute-done | bytes 1048608 | tf_op jit(solution)/shard_map/ppermute | solution.py:20
  27.6 4.4 %shard_map.413 = (bf16[256,768]{1,0:T(8,128)(2,1)}, bf16[192,256]{1,0:T(8,128)(2,1)}, f32[256,960]{1,0:T(8,128)S(1)}, bf16[256,1024]{1,0:T(8,128)(2,1)S(1)}, bf1...) custom-call(s32[4]{0:T(128)S(1)} %pad_add_fusion.refs_0_, ...), custom_call_target="tpu_custom_call" | custom-call | flops 1400000000 | bytes 14109456 | tf_op jit(solution)/shard_map/pallas_call | solution.py:85
  37.9 5.6 %collective-permute-done.9.refs_4_ = bf16[128,1024]{1,0:T(8,128)(2,1)S(1)} collective-permute-done((bf16[128,1024]{1,0:T(8,128)(2,1)S(1)}, bf16[128,1024]{1,0:T(8,128)(2,1)S(1)}, u32[]{:S(2)}, u32[]{:S(2)}) %collective-permute-start.9) | collective-permute-done | bytes 262176 | tf_op jit(solution)/shard_map/ppermute | solution.py:20
  49.1 4.5 %collective-permute-done.10.refs_15_ = bf16[128,960]{1,0:T(8,128)(2,1)S(1)} collective-permute-done((bf16[128,960]{1,0:T(8,128)(2,1)S(1)}, bf16[128,960]{1,0:T(8,128)(2,1)S(1)}, u32[]{:S(2)}, u32[]{:S(2)}) %collective-permute-start.10) | collective-permute-done | bytes 245792 | tf_op jit(solution)/shard_map/ppermute | solution.py:20
  56.8 4.7 %shard_map.415 = (f32[2,208,384]{2,1,0:T(8,128)S(1)}, bf16[2,208,384]{2,1,0:T(8,128)(2,1)S(1)}, bf16[1024,512]{1,0:T(8,128)(2,1)S(1)}, bf16[1024,1024]{1,0:T(8,128)(2,1)S(1)}) custom-call(s32[4]{0:T(128)S(1)} %pad_add_fusion.refs_0_, bf16[256,1024]{1,0:T(8,128)(2,1)S(1)} %get-tuple-element.134.refs_0_.refs_1_, ...), custom_call_target="tpu_custom_call" | custom-call | flops 1800000000 | bytes 13213712 | tf_op jit(solution)/shard_map/pallas_call | solution.py:85
  66.7 8.8 %shard_map.417 = (bf16[512,512]{1,0:T(8,128)(2,1)S(1)}, bf16[512,512]{1,0:T(8,128)(2,1)S(1)}, bf16[512,512]{1,0:T(8,128)(2,1)S(1)}, bf16[512,512]{1,0:T(8,128)(2,1)S(1)}, bf16[256,960]{1,0:T(8,128)(2,1)S(1)}) custom-call(s32[4]{0:T(128)S(1)} %pad_add_fusion.refs_0_, bf16[512,512]{1,0:T(8,128)(2,1)S(1)} %get-tuple-element.158.refs_1_, ...), custom_call_target="tpu_custom_call" | custom-call | flops 5000000000 | bytes 8433552 | tf_op jit(solution)/shard_map/pallas_call | solution.py:85
  75.8 2.7 %collective-permute-start.22 = (bf16[208,384]{1,0:T(8,128)(2,1)S(1)}, bf16[208,384]{1,0:T(8,128)(2,1)S(1)}, u32[]{:S(2)}, u32[]{:S(2)}) collective-permute-start(bf16[208,384]{1,0:T(8,128)(2,1)S(1)} %fusion.6.refs_13_), channel_id=1, source_target_pairs={{0,16},{2,18},{4,20},{6,22},{8,24},{10,26},{12,28},{14,30},{16,0},... | collective-permute-start | bytes 479240 | tf_op jit(solution)/shard_map/ppermute | solution.py:20
  81.7 8.7 %collective-permute-done.22 = bf16[208,384]{1,0:T(8,128)(2,1)S(1)} collective-permute-done((bf16[208,384]{1,0:T(8,128)(2,1)S(1)}, bf16[208,384]{1,0:T(8,128)(2,1)S(1)}, u32[]{:S(2)}, u32[]{:S(2)}) %collective-permute-start.22) | collective-permute-done | bytes 159776 | tf_op jit(solution)/shard_map/ppermute | solution.py:20
  93.9 3.4 %collective-permute-start.24 = (bf16[2,208,384]{2,1,0:T(8,128)(2,1)S(1)}, bf16[2,208,384]{2,1,0:T(8,128)(2,1)S(1)}, u32[]{:S(2)}, u32[]{:S(2)}) collective-permute-start(bf16[2,208,384]{2,1,0:T(8,128)(2,1)S(1)} %pad_maximum_fusion.2.refs_1_), channel_id=1, source_target_pairs={{0,16},{2,18},{4,20},{6,22},{8,24},{10,26},{12,28},{14,30},{16,0},... | collective-permute-start | bytes 958472 | tf_op jit(solution)/shard_map/ppermute | solution.py:20
  98.3 11.1 %collective-permute-done.26.refs_5_ = bf16[2,208,384]{2,1,0:T(8,128)(2,1)S(1)} collective-permute-done((bf16[2,208,384]{2,1,0:T(8,128)(2,1)S(1)}, bf16[2,208,384]{2,1,0:T(8,128)(2,1)S(1)}, u32[]{:S(2)}, u32[]{:S(2)}) %collective-permute-start.26) | collective-permute-done | bytes 319520 | tf_op jit(solution)/shard_map/ppermute | solution.py:20
  111.8 2.9 %collective-permute-done.23 = bf16[2,208,384]{2,1,0:T(8,128)(2,1)S(1)} collective-permute-done((bf16[2,208,384]{2,1,0:T(8,128)(2,1)S(1)}, bf16[2,208,384]{2,1,0:T(8,128)(2,1)S(1)}, u32[]{:S(2)}, u32[]{:S(2)}) %collective-permute-start.23) | collective-permute-done | bytes 319520 | tf_op jit(solution)/shard_map/ppermute | solution.py:20
  114.8 3.5 %collective-permute-start.27 = (bf16[208,384]{1,0:T(8,128)(2,1)S(1)}, bf16[208,384]{1,0:T(8,128)(2,1)S(1)}, u32[]{:S(2)}, u32[]{:S(2)}) collective-permute-start(bf16[208,384]{1,0:T(8,128)(2,1)S(1)} %fusion.10), channel_id=1, source_target_pairs={{0,16},{2,18},{4,20},{6,22},{8,24},{10,26},{12,28},{14,30},{16,0},... | collective-permute-start | bytes 479240 | tf_op jit(solution)/shard_map/ppermute | solution.py:20
  122.9 2.6 %collective-permute-done.27 = bf16[208,384]{1,0:T(8,128)(2,1)S(1)} collective-permute-done((bf16[208,384]{1,0:T(8,128)(2,1)S(1)}, bf16[208,384]{1,0:T(8,128)(2,1)S(1)}, u32[]{:S(2)}, u32[]{:S(2)}) %collective-permute-start.27) | collective-permute-done | bytes 159776 | tf_op jit(solution)/shard_map/ppermute | solution.py:20
  128.8 2.6 %collective-permute-done.34.refs_13_ = bf16[2,208,384]{2,1,0:T(8,128)(2,1)S(1)} collective-permute-done((bf16[2,208,384]{2,1,0:T(8,128)(2,1)S(1)}, bf16[2,208,384]{2,1,0:T(8,128)(2,1)S(1)}, u32[]{:S(2)}, u32[]{:S(2)}) %collective-permute-start.34) | collective-permute-done | bytes 319520 | tf_op jit(solution)/shard_map/ppermute | solution.py:20
  136.9 3.7 %collective-permute-done.39.refs_14_ = bf16[2,208,384]{2,1,0:T(8,128)(2,1)S(1)} collective-permute-done((bf16[2,208,384]{2,1,0:T(8,128)(2,1)S(1)}, bf16[2,208,384]{2,1,0:T(8,128)(2,1)S(1)}, u32[]{:S(2)}, u32[]{:S(2)}) %collective-permute-start.39) | collective-permute-done | bytes 319520 | tf_op jit(solution)/shard_map/ppermute | solution.py:20
  141.3 6.6 %collective-permute-done.40.refs_12_ = bf16[2,208,384]{2,1,0:T(8,128)(2,1)S(1)} collective-permute-done((bf16[2,208,384]{2,1,0:T(8,128)(2,1)S(1)}, bf16[2,208,384]{2,1,0:T(8,128)(2,1)S(1)}, u32[]{:S(2)}, u32[]{:S(2)}) %collective-permute-start.40) | collective-permute-done | bytes 319520 | tf_op jit(solution)/shard_map/ppermute | solution.py:20
  151.9 6.4 %collective-permute-done.45.refs_5_ = bf16[2,208,384]{2,1,0:T(8,128)(2,1)S(1)} collective-permute-done((bf16[2,208,384]{2,1,0:T(8,128)(2,1)S(1)}, bf16[2,208,384]{2,1,0:T(8,128)(2,1)S(1)}, u32[]{:S(2)}, u32[]{:S(2)}) %collective-permute-start.45) | collective-permute-done | bytes 319520 | tf_op jit(solution)/shard_map/ppermute | solution.py:20
  158.6 6.4 %collective-permute-done.44.refs_6_ = bf16[2,208,384]{2,1,0:T(8,128)(2,1)S(1)} collective-permute-done((bf16[2,208,384]{2,1,0:T(8,128)(2,1)S(1)}, bf16[2,208,384]{2,1,0:T(8,128)(2,1)S(1)}, u32[]{:S(2)}, u32[]{:S(2)}) %collective-permute-start.44) | collective-permute-done | bytes 319520 | tf_op jit(solution)/shard_map/ppermute | solution.py:20
  168.4 4.9 %shard_map.421 = (f32[768,1536]{1,0:T(8,128)}, f32[192,384]{1,0:T(8,128)}, f32[1536,768]{1,0:T(8,128)}, f32[192,384]{1,0:T(8,128)}) custom-call(s32[4]{0:T(128)S(1)} %pad_add_fusion.refs_0_, bf16[2,208,384]{2,1,0:T(8,128)(2,1)S(1)} %pad_maximum_fusion.2.refs_1_, bf16[2,208,384]{2,1,0:T(8,128)(2,1)S(1)} %collective-permute-done.25.refs_2_, ...), custom_call_target="tpu_custom_call" | custom-call | flops 100000000 | bytes 15138832 | tf_op jit(solution)/shard_map/pallas_call | solution.py:85
  174.2 3.1 %shard_map.422 = (f32[3,768,384]{2,1,0:T(8,128)}, f32[384,768]{1,0:T(8,128)}, f32[3,192,96]{2,1,0:T(8,128)}, f32[96,192]{1,0:T(8,128)}, f32[2,768]{1,0:T(2,128)}...) custom-call(s32[4]{0:T(128)S(1)} %pad_add_fusion.refs_0_, ...), custom_call_target="tpu_custom_call" | custom-call | flops 100000000 | bytes 7898896 | tf_op jit(solution)/shard_map/pallas_call | solution.py:85
  (132 shorter events, 66.2 us)
Async XLA Ops:
  0.7 14.5 %collective-permute-start = (bf16[256,768]{1,0:T(8,128)(2,1)}, bf16[256,768]{1,0:T(8,128)(2,1)S(1)}, u32[]{:S(2)}, u32[]{:S(2)}) collective-permute-start(bf16[256,768]{1,0:T(8,128)(2,1)} %refs_5_.7), channel_id=1, source_target_pairs={{0,2},{2,0},{4,6},{6,4},{8,10},{10,8},{12,14},{14,12},{16,18},{18,... | collective-permute-start | bytes 1179656 | tf_op jit(solution)/shard_map/ppermute | solution.py:20
  36.4 12.7 %collective-permute-start.11 = (bf16[128,1024]{1,0:T(8,128)(2,1)S(1)}, bf16[128,1024]{1,0:T(8,128)(2,1)S(1)}, u32[]{:S(2)}, u32[]{:S(2)}) collective-permute-start(bf16[128,1024]{1,0:T(8,128)(2,1)S(1)} %get-tuple-element.145), channel_id=1, source_target_pairs={{0,4},{2,6},{4,0},{6,2},{8,12},{10,14},{12,8},{14,10},{16,20},{18,... | collective-permute-start | bytes 786440 | tf_op jit(solution)/shard_map/ppermute | solution.py:20
  43.5 10.8 %collective-permute-start.14 = (bf16[128,1024]{1,0:T(8,128)(2,1)S(1)}, bf16[128,1024]{1,0:T(8,128)(2,1)S(1)}, u32[]{:S(2)}, u32[]{:S(2)}) collective-permute-start(bf16[128,1024]{1,0:T(8,128)(2,1)S(1)} %collective-permute-done.8.refs_10_.refs_7_), channel_id=1, source_target_pairs={{0,4},{2,6},{4,0},{6,2},{8,12},{10,14},{12,8},{14,10},{16,20},{18,... | collective-permute-start | bytes 786440 | tf_op jit(solution)/shard_map/ppermute | solution.py:20
  54.5 12.2 %collective-permute-start.12 = (bf16[128,960]{1,0:T(8,128)(2,1)S(1)}, bf16[128,960]{1,0:T(8,128)(2,1)S(1)}, u32[]{:S(2)}, u32[]{:S(2)}) collective-permute-start(bf16[128,960]{1,0:T(8,128)(2,1)S(1)} %collective-permute-done.10.refs_15_), channel_id=1, source_target_pairs={{0,1},{1,0},{2,3},{3,2},{4,5},{5,4},{6,7},{7,6},{8,9},{9,8},{10,11... | collective-permute-start | bytes 737288 | tf_op jit(solution)/shard_map/ppermute | solution.py:20
  61.5 14.0 %collective-permute-start.17 = (bf16[2,208,384]{2,1,0:T(8,128)(2,1)S(1)}, bf16[2,208,384]{2,1,0:T(8,128)(2,1)S(1)}, u32[]{:S(2)}, u32[]{:S(2)}) collective-permute-start(bf16[2,208,384]{2,1,0:T(8,128)(2,1)S(1)} %get-tuple-element.170.refs_3_), channel_id=1, source_target_pairs={{0,8},{2,10},{4,12},{6,14},{8,0},{10,2},{12,4},{14,6},{16,24},{18,... | collective-permute-start | bytes 958472 | tf_op jit(solution)/shard_map/ppermute | solution.py:20
  63.1 15.4 %collective-permute-start.16 = (f32[32,384]{1,0:T(8,128)S(1)}, f32[32,384]{1,0:T(8,128)S(1)}, u32[]{:S(2)}, u32[]{:S(2)}) collective-permute-start(f32[32,384]{1,0:T(8,128)S(1)} %get-tuple-element.177.refs_11_), channel_id=1, source_target_pairs={{0,2},{2,0},{4,6},{6,4},{8,10},{10,8},{12,14},{14,12},{16,18},{18,... | collective-permute-start | bytes 147464 | tf_op jit(solution)/shard_map/ppermute | solution.py:20
  66.2 14.4 %collective-permute-start.20 = (bf16[2,208,384]{2,1,0:T(8,128)(2,1)S(1)}, bf16[2,208,384]{2,1,0:T(8,128)(2,1)S(1)}, u32[]{:S(2)}, u32[]{:S(2)}) collective-permute-start(bf16[2,208,384]{2,1,0:T(8,128)(2,1)S(1)} %get-tuple-element.171.refs_17_), channel_id=1, source_target_pairs={{0,8},{2,10},{4,12},{6,14},{8,0},{10,2},{12,4},{14,6},{16,24},{18,... | collective-permute-start | bytes 958472 | tf_op jit(solution)/shard_map/ppermute | solution.py:20
  75.8 14.6 %collective-permute-start.22 = (bf16[208,384]{1,0:T(8,128)(2,1)S(1)}, bf16[208,384]{1,0:T(8,128)(2,1)S(1)}, u32[]{:S(2)}, u32[]{:S(2)}) collective-permute-start(bf16[208,384]{1,0:T(8,128)(2,1)S(1)} %fusion.6.refs_13_), channel_id=1, source_target_pairs={{0,16},{2,18},{4,20},{6,22},{8,24},{10,26},{12,28},{14,30},{16,0},... | collective-permute-start | bytes 479240 | tf_op jit(solution)/shard_map/ppermute | solution.py:20
  80.6 16.6 %collective-permute-start.19 = (bf16[4,208,384]{2,1,0:T(8,128)(2,1)S(1)}, bf16[4,208,384]{2,1,0:T(8,128)(2,1)S(1)}, u32[]{:S(2)}, u32[]{:S(2)}) collective-permute-start(bf16[4,208,384]{2,1,0:T(8,128)(2,1)S(1)} %get-tuple-element.180.refs_5_), channel_id=1, source_target_pairs={{0,4},{2,6},{4,0},{6,2},{8,12},{10,14},{12,8},{14,10},{16,20},{18,... | collective-permute-start | bytes 1916936 | tf_op jit(solution)/shard_map/ppermute | solution.py:20
  81.3 11.1 %collective-permute-start.21 = (bf16[208,384]{1,0:T(8,128)(2,1)S(1)}, bf16[208,384]{1,0:T(8,128)(2,1)S(1)}, u32[]{:S(2)}, u32[]{:S(2)}) collective-permute-start(bf16[208,384]{1,0:T(8,128)(2,1)S(1)} %fusion.7), channel_id=1, source_target_pairs={{0,16},{2,18},{4,20},{6,22},{8,24},{10,26},{12,28},{14,30},{16,0},... | collective-permute-start | bytes 479240 | tf_op jit(solution)/shard_map/ppermute | solution.py:20
  92.5 16.8 %collective-permute-start.26 = (bf16[2,208,384]{2,1,0:T(8,128)(2,1)S(1)}, bf16[2,208,384]{2,1,0:T(8,128)(2,1)S(1)}, u32[]{:S(2)}, u32[]{:S(2)}) collective-permute-start(bf16[2,208,384]{2,1,0:T(8,128)(2,1)S(1)} %pad_maximum_fusion.2.refs_1_), channel_id=1, source_target_pairs={{0,8},{2,10},{4,12},{6,14},{8,0},{10,2},{12,4},{14,6},{16,24},{18,... | collective-permute-start | bytes 958472 | tf_op jit(solution)/shard_map/ppermute | solution.py:20
  93.3 16.6 %collective-permute-start.25 = (bf16[2,208,384]{2,1,0:T(8,128)(2,1)S(1)}, bf16[2,208,384]{2,1,0:T(8,128)(2,1)S(1)}, u32[]{:S(2)}, u32[]{:S(2)}) collective-permute-start(bf16[2,208,384]{2,1,0:T(8,128)(2,1)S(1)} %pad_maximum_fusion.2.refs_1_), channel_id=1, source_target_pairs={{0,2},{2,0},{4,6},{6,4},{8,10},{10,8},{12,14},{14,12},{16,18},{18,... | collective-permute-start | bytes 958472 | tf_op jit(solution)/shard_map/ppermute | solution.py:20
  93.9 17.4 %collective-permute-start.24 = (bf16[2,208,384]{2,1,0:T(8,128)(2,1)S(1)}, bf16[2,208,384]{2,1,0:T(8,128)(2,1)S(1)}, u32[]{:S(2)}, u32[]{:S(2)}) collective-permute-start(bf16[2,208,384]{2,1,0:T(8,128)(2,1)S(1)} %pad_maximum_fusion.2.refs_1_), channel_id=1, source_target_pairs={{0,16},{2,18},{4,20},{6,22},{8,24},{10,26},{12,28},{14,30},{16,0},... | collective-permute-start | bytes 958472 | tf_op jit(solution)/shard_map/ppermute | solution.py:20
  97.4 17.2 %collective-permute-start.23 = (bf16[2,208,384]{2,1,0:T(8,128)(2,1)S(1)}, bf16[2,208,384]{2,1,0:T(8,128)(2,1)S(1)}, u32[]{:S(2)}, u32[]{:S(2)}) collective-permute-start(bf16[2,208,384]{2,1,0:T(8,128)(2,1)S(1)} %slice.74), channel_id=1, source_target_pairs={{0,8},{2,10},{4,12},{6,14},{8,0},{10,2},{12,4},{14,6},{16,24},{18,... | collective-permute-start | bytes 958472 | tf_op jit(solution)/shard_map/ppermute | solution.py:20
  97.8 22.8 %collective-permute-start.29 = (bf16[2,208,384]{2,1,0:T(8,128)(2,1)S(1)}, bf16[2,208,384]{2,1,0:T(8,128)(2,1)S(1)}, u32[]{:S(2)}, u32[]{:S(2)}) collective-permute-start(bf16[2,208,384]{2,1,0:T(8,128)(2,1)S(1)} %pad_maximum_fusion.2.refs_1_), channel_id=1, source_target_pairs={{0,4},{2,6},{4,0},{6,2},{8,12},{10,14},{12,8},{14,10},{16,20},{18,... | collective-permute-start | bytes 958472 | tf_op jit(solution)/shard_map/ppermute | solution.py:20
  118.9 12.5 %collective-permute-start.34 = (bf16[2,208,384]{2,1,0:T(8,128)(2,1)S(1)}, bf16[2,208,384]{2,1,0:T(8,128)(2,1)S(1)}, u32[]{:S(2)}, u32[]{:S(2)}) collective-permute-start(bf16[2,208,384]{2,1,0:T(8,128)(2,1)S(1)} %collective-permute-done.24.refs_9_), channel_id=1, source_target_pairs={{0,8},{2,10},{4,12},{6,14},{8,0},{10,2},{12,4},{14,6},{16,24},{18,... | collective-permute-start | bytes 958472 | tf_op jit(solution)/shard_map/ppermute | solution.py:20
  121.7 13.1 %collective-permute-start.33 = (bf16[2,208,384]{2,1,0:T(8,128)(2,1)S(1)}, bf16[2,208,384]{2,1,0:T(8,128)(2,1)S(1)}, u32[]{:S(2)}, u32[]{:S(2)}) collective-permute-start(bf16[2,208,384]{2,1,0:T(8,128)(2,1)S(1)} %collective-permute-done.31.refs_7_), channel_id=1, source_target_pairs={{0,2},{2,0},{4,6},{6,4},{8,10},{10,8},{12,14},{14,12},{16,18},{18,... | collective-permute-start | bytes 958472 | tf_op jit(solution)/shard_map/ppermute | solution.py:20
  128.7 36.6 %collective-permute-start.18 = (f32[256,1024]{1,0:T(8,128)S(1)}, f32[256,1024]{1,0:T(8,128)S(1)}, u32[]{:S(2)}, u32[]{:S(2)}) collective-permute-start(f32[256,1024]{1,0:T(8,128)S(1)} %shard_map.419.refs_1_), channel_id=1, source_target_pairs={{0,1},{1,0},{2,3},{3,2},{4,5},{5,4},{6,7},{7,6},{8,9},{9,8},{10,11... | collective-permute-start | bytes 3145736 | tf_op jit(solution)/shard_map/ppermute | solution.py:20
  133.2 14.9 %collective-permute-start.38 = (bf16[2,208,384]{2,1,0:T(8,128)(2,1)S(1)}, bf16[2,208,384]{2,1,0:T(8,128)(2,1)S(1)}, u32[]{:S(2)}, u32[]{:S(2)}) collective-permute-start(bf16[2,208,384]{2,1,0:T(8,128)(2,1)S(1)} %collective-permute-done.34.refs_13_), channel_id=1, source_target_pairs={{0,4},{2,6},{4,0},{6,2},{8,12},{10,14},{12,8},{14,10},{16,20},{18,... | collective-permute-start | bytes 958472 | tf_op jit(solution)/shard_map/ppermute | solution.py:20
  134.8 13.0 %collective-permute-start.40 = (bf16[2,208,384]{2,1,0:T(8,128)(2,1)S(1)}, bf16[2,208,384]{2,1,0:T(8,128)(2,1)S(1)}, u32[]{:S(2)}, u32[]{:S(2)}) collective-permute-start(bf16[2,208,384]{2,1,0:T(8,128)(2,1)S(1)} %collective-permute-done.36.refs_10_), channel_id=1, source_target_pairs={{0,4},{2,6},{4,0},{6,2},{8,12},{10,14},{12,8},{14,10},{16,20},{18,... | collective-permute-start | bytes 958472 | tf_op jit(solution)/shard_map/ppermute | solution.py:20
  135.6 12.5 %collective-permute-start.37 = (bf16[2,208,384]{2,1,0:T(8,128)(2,1)S(1)}, bf16[2,208,384]{2,1,0:T(8,128)(2,1)S(1)}, u32[]{:S(2)}, u32[]{:S(2)}) collective-permute-start(bf16[2,208,384]{2,1,0:T(8,128)(2,1)S(1)} %pad_maximum_fusion.3.refs_1_), channel_id=1, source_target_pairs={{0,8},{2,10},{4,12},{6,14},{8,0},{10,2},{12,4},{14,6},{16,24},{18,... | collective-permute-start | bytes 958472 | tf_op jit(solution)/shard_map/ppermute | solution.py:20
  148.1 16.8 %collective-permute-start.44 = (bf16[2,208,384]{2,1,0:T(8,128)(2,1)S(1)}, bf16[2,208,384]{2,1,0:T(8,128)(2,1)S(1)}, u32[]{:S(2)}, u32[]{:S(2)}) collective-permute-start(bf16[2,208,384]{2,1,0:T(8,128)(2,1)S(1)} %collective-permute-done.37.refs_2_), channel_id=1, source_target_pairs={{0,4},{2,6},{4,0},{6,2},{8,12},{10,14},{12,8},{14,10},{16,20},{18,... | collective-permute-start | bytes 958472 | tf_op jit(solution)/shard_map/ppermute | solution.py:20
  149.9 16.5 %collective-permute-start.43 = (bf16[2,208,384]{2,1,0:T(8,128)(2,1)S(1)}, bf16[2,208,384]{2,1,0:T(8,128)(2,1)S(1)}, u32[]{:S(2)}, u32[]{:S(2)}) collective-permute-start(bf16[2,208,384]{2,1,0:T(8,128)(2,1)S(1)} %collective-permute-done.38.refs_15_), channel_id=1, source_target_pairs={{0,2},{2,0},{4,6},{6,4},{8,10},{10,8},{12,14},{14,12},{16,18},{18,... | collective-permute-start | bytes 958472 | tf_op jit(solution)/shard_map/ppermute | solution.py:20
  150.1 16.2 %collective-permute-start.42 = (bf16[2,208,384]{2,1,0:T(8,128)(2,1)S(1)}, bf16[2,208,384]{2,1,0:T(8,128)(2,1)S(1)}, u32[]{:S(2)}, u32[]{:S(2)}) collective-permute-start(bf16[2,208,384]{2,1,0:T(8,128)(2,1)S(1)} %collective-permute-done.37.refs_2_), channel_id=1, source_target_pairs={{0,2},{2,0},{4,6},{6,4},{8,10},{10,8},{12,14},{14,12},{16,18},{18,... | collective-permute-start | bytes 958472 | tf_op jit(solution)/shard_map/ppermute | solution.py:20
  (38 other events, 323.5 us)

commit v4 on v3

--- a/solution.py
+++ b/solution.py
@@ -649,7 +649,8 @@
 
 
 def units_result_kernel(idx, *refs):
-    parts, (up_t, up_l, dn_t, dn_l), (up_table, dn_table) = refs[:16], refs[16:20], refs[20:]
+    parts, (up_t, up_l, dn_t, dn_l, token), (up_table, dn_table) = refs[:16], refs[16:21], refs[21:]
+    token[...] = jnp.zeros_like(token)
     rows, columns = up_t.shape[0] // 4, up_t.shape[1] // 4
     thin = up_l.shape[1] // 4
     half = rows // 2
@@ -727,17 +728,17 @@
 
 
 ORDER = (
-    "down4", "up8", "down8", "y", 4, 1, 8, "z4", 6, 5, 2, 10, "z8", 9, 3, 12, 7, "even", 11, 13, 14,
-    "odd", "even1", "even2", "odd2", 15, "odd1", "even3", "odd3",
+    ("down4", None, 0), ("up8", None, 0), ("down8", None, 0), (4, 0, 4), (1, 0, 1), (2, 0, 2), ("y", None, 0),
+    (6, 4, 2), (8, 0, 8), ("z4", None, 0), (5, 4, 1), (3, 1, 2), (12, 8, 4), ("z8", None, 0), (10, 8, 2),
+    (9, 8, 1), ("even", None, 0), (13, 9, 4), (11, 9, 2), (7, 6, 1), ("odd", "even", 4), (15, 11, 4),
+    ("even2", "even", 2), ("even1", "even", 1), ("odd2", "odd", 2), ("odd1", "odd", 1), (14, 10, 4),
+    ("even3", "even1", 2), ("odd3", "odd2", 1),
 )
 
 
 def reduced_and_gathered(token, up, up_far, down_keep, down_far, keep, far):
     last = token
     coming, found = {"up8": up_far, "down4": down_far, "y": far}, {}
-
-    def send(shard, mask, name):
-        coming[name] = exchange(shard, mask)
 
     def beyond(own):
         mask = 16
@@ -746,43 +747,33 @@
             mask *= 2
         return own.astype(BF)
 
-    for name in ORDER:
-        last = found[name] = tied(coming[name], last)
+    def have(name, value):
+        found[name] = value
+        for other, source, mask in ORDER:
+            if source == name and source is not None:
+                coming[other] = exchange(value, mask)
+
+    for name, _, _ in ORDER:
+        last = tied(coming[name], last)
+        if name == "even":
+            have("even", jnp.stack([own, last]))
+        else:
+            have(name, last)
         if name == "down4":
             down = down_keep + last.astype(F32)
-            send(down[1].astype(BF), 8, "down8")
-        elif name == "down8":
-            up_own = beyond(up + found["up8"].astype(F32))
-            found[0] = jnp.stack([up_own, beyond(down[0] + last.astype(F32))])
-            for mask in (4, 1, 8, 2):
-                send(found[0], mask, mask)
+            coming["down8"] = exchange(down[1].astype(BF), 8)
         elif name == "y":
             total = keep + last.astype(F32)
-            send(total[2:].astype(BF), 4, "z4")
+            coming["z4"] = exchange(total[2:].astype(BF), 4)
         elif name == "z4":
             total = total[:2] + last.astype(F32)
-            send(total[1].astype(BF), 8, "z8")
+            coming["z8"] = exchange(total[1].astype(BF), 8)
         elif name == "z8":
             own = beyond(total[0] + last.astype(F32))
-            send(own, 8, "even")
-        elif name == "even":
-            found["even"] = jnp.stack([own, last])
-            for mask, to in ((4, "odd"), (1, "even1"), (2, "even2")):
-                send(found["even"], mask, to)
-        elif name == "odd":
-            for mask in (1, 2):
-                send(last, mask, f"odd{mask}")
-        elif name == "even1":
-            send(last, 2, "even3")
-        elif name == "odd2":
-            send(last, 1, "odd3")
-        elif name in (4, 8, 12):
-            for mask in (1, 2) if name != 8 else (4, 2, 1):
-                send(last, mask, name + mask)
-        elif name in (1, 9):
-            send(last, 2, name + 2)
-        elif name in (6, 14):
-            send(last, 1, name + 1)
+            coming["even"] = exchange(own, 8)
+        if name in ("up8", "down8") and {"up8", "down8"} <= found.keys():
+            sums = up + found["up8"].astype(F32), down[0] + found["down8"].astype(F32)
+            have(0, jnp.stack([beyond(piece) for piece in sums]))
     names = ("even", "odd", "even1", "odd1", "even2", "odd2", "even3", "odd3")
     return [found[at] for at in range(16)], [found[name] for name in names]
 
@@ -896,10 +887,8 @@
     low_x, low_y = tied(low_x, grad_mine), tied(low_y, grad_mine)
     low_xy = exchange(low_x, 2)
     hidden_back = over_cores(tied(tied(hidden_part, low_x), low_y))
-    low_far = [low_x, low_y, tied(low_xy, hidden_part)]
-    low_back = over_cores(jnp.concatenate(low_far, axis=0))
-    grad_x = tied(grad_x, low_far[2])
-    grad_xy = exchange(grad_x, 2)
+    grad_y = tied(grad_y, hidden_part)
+    grad_xy = exchange(grad_y, 1)
     first, attended_grad, attended_mine, small = call(
         first_norm_kernel,
         [
@@ -909,13 +898,14 @@
             shape((32, width), F32),
         ],
         idx, second, hidden_part, hidden_back, normed, inverse, pack, sums_two, bias_t, bias_l, smem=1, pin=[0, 1],
-        after=[grad_x],
-    )
-    attended_far = exchange(attended_mine, 1)
-    grad_y = tied(grad_y, small)
-    attended_far = tied(attended_far, grad_y)
-    attended_back = over_cores(attended_far)
-    grad_far = [grad_x, grad_y, tied(grad_xy, attended_far)]
+        after=[grad_y],
+    )
+    attended_far, small_other = exchange(attended_mine, 1), exchange(small, 1)
+    low_far = [low_x, low_y, tied(low_xy, small)]
+    low_back = over_cores(jnp.concatenate(low_far, axis=0))
+    small_other = tied(small_other, low_far[2])
+    grad_x = tied(grad_x, small_other)
+    grad_far = [grad_x, grad_y, tied(grad_xy, grad_x)]
     low_parts = [low, *low_far, low_back]
     grad_parts = [grad_low, *grad_far, over_cores(jnp.concatenate(grad_far, axis=0))]
     block = (2, wide // 4 + 16, width)
@@ -940,14 +930,15 @@
         smem=1, anys=range(1, 15), flops=18 * 10**8, room=24, pin=[2, 3],
     )
     up_far = exchange(up_send, 4)
+    attended_far = tied(attended_far, up_send)
+    attended_back = over_cores(attended_far)
     down_keep, down_send = call(
         down_grads_kernel,
         [shape(block, F32), shape(block, BF)],
         idx, activated, grad_rows, scratch=[pltpu.VMEM((4,) + block[1:], F32)], smem=1,
-        flops=7 * 10**8, after=[up_send],
+        flops=7 * 10**8, after=[attended_far],
     )
     down_far = exchange(down_send, 4)
-    small_other = exchange(tied(small, up_send), 1)
 
     dq, dk, dv, context, attended_grad_other = call(
         attention_back_kernel,
@@ -986,11 +977,12 @@
         keep, up_total[0], exchange(up_part, 8), down_keep, down_far, keep, send_far
     )
 
-    up_t, up_l, down_t, down_l = call(
+    up_t, up_l, down_t, down_l, token = call(
         units_result_kernel,
-        [shape(a.shape, F32) for a in (text_up, layout_up, text_down, down_turned)],
+        [shape(a.shape, F32) for a in (text_up, layout_up, text_down, down_turned)]
+        + [shape((8, LANES), F32)],
         idx, *units_pieces, scratch=[pltpu.VMEM((4, thin, LANES), F32)] * 2, smem=1,
-        room=32,
+        pin=[4], room=32,
     )
     one_row = (units,), (units_l,)
     kinds = [text_out_bias.shape] * 3 + [one_row[0], text_qv_bias.shape]
@@ -1002,7 +994,7 @@
         attention_result_kernel,
         [shape(a.shape, F32) for a in (text_qkv, text_out, layout_qkv, layout_out)]
         + [shape(dims, F32) for dims in kinds],
-        idx, *attention_pieces, after=[up_l],
+        idx, *attention_pieces, after=[token],
         scratch=[pltpu.VMEM((4, thin, LANES), F32), pltpu.VMEM((2, 8, 8, width), F32)], smem=1,
     )
     return (

time: 178 us -> 173 us (0.972)
  waiting for transfers between devices: 81.7 us -> 70.5 us
  starting transfers between devices: 47.5 us -> 55.2 us
    ppermute x48, waiting for transfers between devices: 81.7 us -> 70.5 us  [exchange(): lax.ppermute(shard, axis, [(i, i ^ mask) for i in range(lax.axis_size(axi...]
    ppermute x48, starting transfers between devices: 47.5 us -> 55.2 us  [exchange(): lax.ppermute(shard, axis, [(i, i ^ mask) for i in range(lax.axis_size(axi...]
  transfers between devices with their start and end apart: 48 -> 48, of which waited for: 25 -> 22; matrix products, arithmetic and copies ran while one was open for 1% -> 1% of each run, Pallas kernels for 20% -> 20%
where the time goes in v4:
time: 173 us
  waiting for transfers between devices  70.5 us (41%)
  starting transfers between devices  55.2 us (32%)
  Pallas kernels  44.3 us (26%)
    ppermute x48, waiting for transfers between devices, exchange(): lax.ppermute(shard, axis, [(i, i ^ mask) for i in range(lax.axis_size(axi...  70.5 us
    ppermute x48, starting transfers between devices, exchange(): lax.ppermute(shard, axis, [(i, i ^ mask) for i in range(lax.axis_size(axi...  55.2 us
    pallas_call x15, Pallas kernels, call(): pl.pallas_call(body, out_shape=tuple((pltpu.VMEM(o.shape, o.dtype) if k i...  44.3 us
  transfers between devices with their start and end apart: 48, of which 22 were waited for; matrix products, arithmetic and copies ran while one was open for 1% of the time, Pallas kernels for 20%

profile of v4, /device:TPU:0, one launch (start us, length us, event | category | flops | bytes accessed | tf_op | source)
XLA Modules:
  0.0 173.1 jit_solution(821901223897952281)
XLA Ops:
  0.7 3.0 %collective-permute-start = (bf16[256,768]{1,0:T(8,128)(2,1)}, bf16[256,768]{1,0:T(8,128)(2,1)S(1)}, u32[]{:S(2)}, u32[]{:S(2)}) collective-permute-start(bf16[256,768]{1,0:T(8,128)(2,1)} %refs_5_.7), channel_id=1, source_target_pairs={{0,2},{2,0},{4,6},{6,4},{8,10},{10,8},{12,14},{14,12},{16,18},{18,... | collective-permute-start | bytes 1179656 | tf_op jit(solution)/shard_map/ppermute | solution.py:20
  6.5 2.7 %shard_map.408 = (bf16[256,192]{1,0:T(8,128)(2,1)S(1)}, f32[256,128]{1,0:T(8,128)S(1)}, f32[16,1536]{1,0:T(8,128)S(1)}, bf16[192,256]{1,0:T(8,128)(2,1)S(1)}) custom-call(s32[4]{0:T(128)S(1)} %pad_add_fusion.refs_0_, bf16[192,256]{1,0:T(8,128)(2,1)} %bitcast.55, s32[1,256]{1,0:T(1,128)} %bitcast.58, bf16[2,768]{1,0:T(2,128)(2,1)} %refs_3_.5, ...), custom_call_target="tpu_custom_call" | custom-call | flops 100000000 | bytes 835600 | tf_op jit(solution)/shard_map/pallas_call | solution.py:85
  9.3 2.6 %shard_map.409 = (bf16[256,512]{1,0:T(8,128)(2,1)S(1)}, bf16[256,512]{1,0:T(8,128)(2,1)S(1)}, bf16[256,512]{1,0:T(8,128)(2,1)S(1)}, bf16[256,192]{1,0:T(8,128)(2,1)S(1)}) custom-call(bf16[256,768]{1,0:T(8,128)(2,1)} %refs_5_.7, bf16[192,256]{1,0:T(8,128)(2,1)} %bitcast.50, bf16[3,768,384]{2,1,0:T(8,128)(2,1)} %refs_3_.9, bf16[2,384]{1,0:T(2,128)(2,1)} %refs_8_.5, ...), custom_call_target="tpu_custom_call" | custom-call | flops 100000000 | bytes 3356544 | tf_op jit(solution)/shard_map/pallas_call | solution.py:85
  15.3 2.7 %shard_map.410 = (f32[256,1024]{1,0:T(8,128)S(1)}, bf16[512,512]{1,0:T(8,128)(2,1)S(1)}, bf16[512,512]{1,0:T(8,128)(2,1)S(1)}) custom-call(bf16[256,512]{1,0:T(8,128)(2,1)S(1)} %get-tuple-element.130.refs_0_, bf16[256,512]{1,0:T(8,128)(2,1)S(1)} %get-tuple-element.131.refs_1_, bf16[256,512]{1,0:T(8,128)(2,1)S(1)} %get-tuple-element.132.refs_2_, ...), custom_call_target="tpu_custom_call" | custom-call | flops 100000000 | bytes 5885824 | tf_op jit(solution)/shard_map/pallas_call | solution.py:85
  18.0 2.6 %collective-permute-done.3.refs_4_ = f32[256,1024]{1,0:T(8,128)S(1)} collective-permute-done((f32[256,1024]{1,0:T(8,128)S(1)}, f32[256,1024]{1,0:T(8,128)S(1)}, u32[]{:S(2)}, u32[]{:S(2)}) %collective-permute-start.3) | collective-permute-done | bytes 1048608 | tf_op jit(solution)/shard_map/ppermute | solution.py:20
  27.6 4.4 %shard_map.413 = (bf16[256,768]{1,0:T(8,128)(2,1)}, bf16[192,256]{1,0:T(8,128)(2,1)}, f32[256,960]{1,0:T(8,128)S(1)}, bf16[256,1024]{1,0:T(8,128)(2,1)S(1)}, bf1...) custom-call(s32[4]{0:T(128)S(1)} %pad_add_fusion.refs_0_, ...), custom_call_target="tpu_custom_call" | custom-call | flops 1400000000 | bytes 14109456 | tf_op jit(solution)/shard_map/pallas_call | solution.py:85
  37.9 5.6 %collective-permute-done.8.refs_10_.refs_8_ = bf16[128,1024]{1,0:T(8,128)(2,1)S(1)} collective-permute-done((bf16[128,1024]{1,0:T(8,128)(2,1)S(1)}, bf16[128,1024]{1,0:T(8,128)(2,1)S(1)}, u32[]{:S(2)}, u32[]{:S(2)}) %collective-permute-start.8) | collective-permute-done | bytes 262176 | tf_op jit(solution)/shard_map/ppermute | solution.py:20
  48.9 3.2 %collective-permute-done.13.refs_12_ = f32[32,384]{1,0:T(8,128)S(1)} collective-permute-done((f32[32,384]{1,0:T(8,128)S(1)}, f32[32,384]{1,0:T(8,128)S(1)}, u32[]{:S(2)}, u32[]{:S(2)}) %collective-permute-start.13) | collective-permute-done | bytes 49184 | tf_op jit(solution)/shard_map/ppermute | solution.py:20
  54.5 4.7 %shard_map.415 = (f32[2,208,384]{2,1,0:T(8,128)S(1)}, bf16[2,208,384]{2,1,0:T(8,128)(2,1)S(1)}, bf16[1024,512]{1,0:T(8,128)(2,1)S(1)}, bf16[1024,1024]{1,0:T(8,128)(2,1)S(1)}) custom-call(s32[4]{0:T(128)S(1)} %pad_add_fusion.refs_0_, bf16[256,1024]{1,0:T(8,128)(2,1)S(1)} %get-tuple-element.135.refs_0_.refs_1_, ...), custom_call_target="tpu_custom_call" | custom-call | flops 1800000000 | bytes 13213712 | tf_op jit(solution)/shard_map/pallas_call | solution.py:85
  64.7 8.8 %shard_map.417 = (bf16[512,512]{1,0:T(8,128)(2,1)S(1)}, bf16[512,512]{1,0:T(8,128)(2,1)S(1)}, bf16[512,512]{1,0:T(8,128)(2,1)S(1)}, bf16[512,512]{1,0:T(8,128)(2,1)S(1)}, bf16[256,960]{1,0:T(8,128)(2,1)S(1)}) custom-call(s32[4]{0:T(128)S(1)} %pad_add_fusion.refs_0_, bf16[512,512]{1,0:T(8,128)(2,1)S(1)} %get-tuple-element.158.refs_1_, ...), custom_call_target="tpu_custom_call" | custom-call | flops 5000000000 | bytes 8433552 | tf_op jit(solution)/shard_map/pallas_call | solution.py:85
  73.8 2.7 %collective-permute-start.20 = (bf16[208,384]{1,0:T(8,128)(2,1)S(1)}, bf16[208,384]{1,0:T(8,128)(2,1)S(1)}, u32[]{:S(2)}, u32[]{:S(2)}) collective-permute-start(bf16[208,384]{1,0:T(8,128)(2,1)S(1)} %fusion.6.refs_13_), channel_id=1, source_target_pairs={{0,16},{2,18},{4,20},{6,22},{8,24},{10,26},{12,28},{14,30},{16,0},... | collective-permute-start | bytes 479240 | tf_op jit(solution)/shard_map/ppermute | solution.py:20
  81.4 7.0 %collective-permute-done.20 = bf16[208,384]{1,0:T(8,128)(2,1)S(1)} collective-permute-done((bf16[208,384]{1,0:T(8,128)(2,1)S(1)}, bf16[208,384]{1,0:T(8,128)(2,1)S(1)}, u32[]{:S(2)}, u32[]{:S(2)}) %collective-permute-start.20) | collective-permute-done | bytes 159776 | tf_op jit(solution)/shard_map/ppermute | solution.py:20
  88.4 2.6 %collective-permute-done.22 = bf16[208,384]{1,0:T(8,128)(2,1)S(1)} collective-permute-done((bf16[208,384]{1,0:T(8,128)(2,1)S(1)}, bf16[208,384]{1,0:T(8,128)(2,1)S(1)}, u32[]{:S(2)}, u32[]{:S(2)}) %collective-permute-start.22) | collective-permute-done | bytes 159776 | tf_op jit(solution)/shard_map/ppermute | solution.py:20
  93.9 3.4 %collective-permute-start.27 = (bf16[2,208,384]{2,1,0:T(8,128)(2,1)S(1)}, bf16[2,208,384]{2,1,0:T(8,128)(2,1)S(1)}, u32[]{:S(2)}, u32[]{:S(2)}) collective-permute-start(bf16[2,208,384]{2,1,0:T(8,128)(2,1)S(1)} %pad_maximum_fusion.2.refs_1_), channel_id=1, source_target_pairs={{0,16},{2,18},{4,20},{6,22},{8,24},{10,26},{12,28},{14,30},{16,0},... | collective-permute-start | bytes 958472 | tf_op jit(solution)/shard_map/ppermute | solution.py:20
  97.3 7.8 %collective-permute-done.25.refs_5_ = bf16[2,208,384]{2,1,0:T(8,128)(2,1)S(1)} collective-permute-done((bf16[2,208,384]{2,1,0:T(8,128)(2,1)S(1)}, bf16[2,208,384]{2,1,0:T(8,128)(2,1)S(1)}, u32[]{:S(2)}, u32[]{:S(2)}) %collective-permute-start.25) | collective-permute-done | bytes 319520 | tf_op jit(solution)/shard_map/ppermute | solution.py:20
  110.0 5.7 %collective-permute-done.28.refs_7_ = bf16[2,208,384]{2,1,0:T(8,128)(2,1)S(1)} collective-permute-done((bf16[2,208,384]{2,1,0:T(8,128)(2,1)S(1)}, bf16[2,208,384]{2,1,0:T(8,128)(2,1)S(1)}, u32[]{:S(2)}, u32[]{:S(2)}) %collective-permute-start.28) | collective-permute-done | bytes 319520 | tf_op jit(solution)/shard_map/ppermute | solution.py:20
  121.1 4.2 %collective-permute-done.30.refs_13_ = bf16[2,208,384]{2,1,0:T(8,128)(2,1)S(1)} collective-permute-done((bf16[2,208,384]{2,1,0:T(8,128)(2,1)S(1)}, bf16[2,208,384]{2,1,0:T(8,128)(2,1)S(1)}, u32[]{:S(2)}, u32[]{:S(2)}) %collective-permute-start.30) | collective-permute-done | bytes 319520 | tf_op jit(solution)/shard_map/ppermute | solution.py:20
  130.6 3.5 %collective-permute-start.39 = (bf16[2,208,384]{2,1,0:T(8,128)(2,1)S(1)}, bf16[2,208,384]{2,1,0:T(8,128)(2,1)S(1)}, u32[]{:S(2)}, u32[]{:S(2)}) collective-permute-start(bf16[2,208,384]{2,1,0:T(8,128)(2,1)S(1)} %collective-permute-done.34.refs_10_), channel_id=1, source_target_pairs={{0,8},{2,10},{4,12},{6,14},{8,0},{10,2},{12,4},{14,6},{16,24},{18,... | collective-permute-start | bytes 958472 | tf_op jit(solution)/shard_map/ppermute | solution.py:20
  134.5 8.0 %collective-permute-done.39.refs_14_ = bf16[2,208,384]{2,1,0:T(8,128)(2,1)S(1)} collective-permute-done((bf16[2,208,384]{2,1,0:T(8,128)(2,1)S(1)}, bf16[2,208,384]{2,1,0:T(8,128)(2,1)S(1)}, u32[]{:S(2)}, u32[]{:S(2)}) %collective-permute-start.39) | collective-permute-done | bytes 319520 | tf_op jit(solution)/shard_map/ppermute | solution.py:20
  146.0 3.3 %collective-permute-done.36.refs_2_ = bf16[2,208,384]{2,1,0:T(8,128)(2,1)S(1)} collective-permute-done((bf16[2,208,384]{2,1,0:T(8,128)(2,1)S(1)}, bf16[2,208,384]{2,1,0:T(8,128)(2,1)S(1)}, u32[]{:S(2)}, u32[]{:S(2)}) %collective-permute-start.36) | collective-permute-done | bytes 319520 | tf_op jit(solution)/shard_map/ppermute | solution.py:20
  152.8 3.0 %collective-permute-done.42.refs_16_ = bf16[2,208,384]{2,1,0:T(8,128)(2,1)S(1)} collective-permute-done((bf16[2,208,384]{2,1,0:T(8,128)(2,1)S(1)}, bf16[2,208,384]{2,1,0:T(8,128)(2,1)S(1)}, u32[]{:S(2)}, u32[]{:S(2)}) %collective-permute-start.42) | collective-permute-done | bytes 319520 | tf_op jit(solution)/shard_map/ppermute | solution.py:20
  160.7 4.1 %collective-permute-done.46.refs_15_ = bf16[2,208,384]{2,1,0:T(8,128)(2,1)S(1)} collective-permute-done((bf16[2,208,384]{2,1,0:T(8,128)(2,1)S(1)}, bf16[2,208,384]{2,1,0:T(8,128)(2,1)S(1)}, u32[]{:S(2)}, u32[]{:S(2)}) %collective-permute-start.46) | collective-permute-done | bytes 319520 | tf_op jit(solution)/shard_map/ppermute | solution.py:20
  164.8 4.9 %shard_map.421 = (f32[768,1536]{1,0:T(8,128)}, f32[192,384]{1,0:T(8,128)}, f32[1536,768]{1,0:T(8,128)}, f32[192,384]{1,0:T(8,128)}, f32[8,128]{1,0:T(8,128)S(1)}) custom-call(s32[4]{0:T(128)S(1)} %pad_add_fusion.refs_0_, bf16[2,208,384]{2,1,0:T(8,128)(2,1)S(1)} %pad_maximum_fusion.2.refs_1_, bf16[2,208,384]{2,1,0:T(8,128)(2,1)S(1)} %collective-permute-done.24.refs_2_, ...), custom_call_target="tpu_custom_call" | custom-call | flops 100000000 | bytes 15142928 | tf_op jit(solution)/shard_map/pallas_call | solution.py:85
  169.7 3.2 %shard_map.422 = (f32[3,768,384]{2,1,0:T(8,128)}, f32[384,768]{1,0:T(8,128)}, f32[3,192,96]{2,1,0:T(8,128)}, f32[96,192]{1,0:T(8,128)}, f32[2,768]{1,0:T(2,128)}...) custom-call(s32[4]{0:T(128)S(1)} %pad_add_fusion.refs_0_, ...), custom_call_target="tpu_custom_call" | custom-call | flops 100000000 | bytes 7608080 | tf_op jit(solution)/shard_map/pallas_call | solution.py:85
  (130 shorter events, 68.1 us)
Async XLA Ops:
  0.7 14.5 %collective-permute-start = (bf16[256,768]{1,0:T(8,128)(2,1)}, bf16[256,768]{1,0:T(8,128)(2,1)S(1)}, u32[]{:S(2)}, u32[]{:S(2)}) collective-permute-start(bf16[256,768]{1,0:T(8,128)(2,1)} %refs_5_.7), channel_id=1, source_target_pairs={{0,2},{2,0},{4,6},{6,4},{8,10},{10,8},{12,14},{14,12},{16,18},{18,... | collective-permute-start | bytes 1179656 | tf_op jit(solution)/shard_map/ppermute | solution.py:20
  34.7 14.1 %collective-permute-start.10 = (bf16[128,1024]{1,0:T(8,128)(2,1)S(1)}, bf16[128,1024]{1,0:T(8,128)(2,1)S(1)}, u32[]{:S(2)}, u32[]{:S(2)}) collective-permute-start(bf16[128,1024]{1,0:T(8,128)(2,1)S(1)} %collective-permute-done.5.refs_2_), channel_id=1, source_target_pairs={{0,4},{2,6},{4,0},{6,2},{8,12},{10,14},{12,8},{14,10},{16,20},{18,... | collective-permute-start | bytes 786440 | tf_op jit(solution)/shard_map/ppermute | solution.py:20
  36.4 15.7 %collective-permute-start.12 = (bf16[128,1024]{1,0:T(8,128)(2,1)S(1)}, bf16[128,1024]{1,0:T(8,128)(2,1)S(1)}, u32[]{:S(2)}, u32[]{:S(2)}) collective-permute-start(bf16[128,1024]{1,0:T(8,128)(2,1)S(1)} %get-tuple-element.146), channel_id=1, source_target_pairs={{0,2},{2,0},{4,6},{6,4},{8,10},{10,8},{12,14},{14,12},{16,18},{18,... | collective-permute-start | bytes 786440 | tf_op jit(solution)/shard_map/ppermute | solution.py:20
  61.0 12.5 %collective-permute-start.17 = (bf16[2,208,384]{2,1,0:T(8,128)(2,1)S(1)}, bf16[2,208,384]{2,1,0:T(8,128)(2,1)S(1)}, u32[]{:S(2)}, u32[]{:S(2)}) collective-permute-start(bf16[2,208,384]{2,1,0:T(8,128)(2,1)S(1)} %get-tuple-element.169), channel_id=1, source_target_pairs={{0,8},{2,10},{4,12},{6,14},{8,0},{10,2},{12,4},{14,6},{16,24},{18,... | collective-permute-start | bytes 958472 | tf_op jit(solution)/shard_map/ppermute | solution.py:20
  64.2 16.2 %collective-permute-start.21 = (bf16[2,208,384]{2,1,0:T(8,128)(2,1)S(1)}, bf16[2,208,384]{2,1,0:T(8,128)(2,1)S(1)}, u32[]{:S(2)}, u32[]{:S(2)}) collective-permute-start(bf16[2,208,384]{2,1,0:T(8,128)(2,1)S(1)} %get-tuple-element.173.refs_17_), channel_id=1, source_target_pairs={{0,8},{2,10},{4,12},{6,14},{8,0},{10,2},{12,4},{14,6},{16,24},{18,... | collective-permute-start | bytes 958472 | tf_op jit(solution)/shard_map/ppermute | solution.py:20
  73.8 14.6 %collective-permute-start.20 = (bf16[208,384]{1,0:T(8,128)(2,1)S(1)}, bf16[208,384]{1,0:T(8,128)(2,1)S(1)}, u32[]{:S(2)}, u32[]{:S(2)}) collective-permute-start(bf16[208,384]{1,0:T(8,128)(2,1)S(1)} %fusion.6.refs_13_), channel_id=1, source_target_pairs={{0,16},{2,18},{4,20},{6,22},{8,24},{10,26},{12,28},{14,30},{16,0},... | collective-permute-start | bytes 479240 | tf_op jit(solution)/shard_map/ppermute | solution.py:20
  80.9 24.3 %collective-permute-start.19 = (bf16[4,208,384]{2,1,0:T(8,128)(2,1)S(1)}, bf16[4,208,384]{2,1,0:T(8,128)(2,1)S(1)}, u32[]{:S(2)}, u32[]{:S(2)}) collective-permute-start(bf16[4,208,384]{2,1,0:T(8,128)(2,1)S(1)} %get-tuple-element.181.refs_5_), channel_id=1, source_target_pairs={{0,4},{2,6},{4,0},{6,2},{8,12},{10,14},{12,8},{14,10},{16,20},{18,... | collective-permute-start | bytes 1916936 | tf_op jit(solution)/shard_map/ppermute | solution.py:20
  91.2 14.0 %collective-permute-start.25 = (bf16[2,208,384]{2,1,0:T(8,128)(2,1)S(1)}, bf16[2,208,384]{2,1,0:T(8,128)(2,1)S(1)}, u32[]{:S(2)}, u32[]{:S(2)}) collective-permute-start(bf16[2,208,384]{2,1,0:T(8,128)(2,1)S(1)} %pad_maximum_fusion.2.refs_1_), channel_id=1, source_target_pairs={{0,8},{2,10},{4,12},{6,14},{8,0},{10,2},{12,4},{14,6},{16,24},{18,... | collective-permute-start | bytes 958472 | tf_op jit(solution)/shard_map/ppermute | solution.py:20
  91.9 13.2 %collective-permute-start.24 = (bf16[2,208,384]{2,1,0:T(8,128)(2,1)S(1)}, bf16[2,208,384]{2,1,0:T(8,128)(2,1)S(1)}, u32[]{:S(2)}, u32[]{:S(2)}) collective-permute-start(bf16[2,208,384]{2,1,0:T(8,128)(2,1)S(1)} %pad_maximum_fusion.2.refs_1_), channel_id=1, source_target_pairs={{0,2},{2,0},{4,6},{6,4},{8,10},{10,8},{12,14},{14,12},{16,18},{18,... | collective-permute-start | bytes 958472 | tf_op jit(solution)/shard_map/ppermute | solution.py:20
  93.4 11.8 %collective-permute-start.23 = (bf16[2,208,384]{2,1,0:T(8,128)(2,1)S(1)}, bf16[2,208,384]{2,1,0:T(8,128)(2,1)S(1)}, u32[]{:S(2)}, u32[]{:S(2)}) collective-permute-start(bf16[2,208,384]{2,1,0:T(8,128)(2,1)S(1)} %pad_maximum_fusion.2.refs_1_), channel_id=1, source_target_pairs={{0,4},{2,6},{4,0},{6,2},{8,12},{10,14},{12,8},{14,10},{16,20},{18,... | collective-permute-start | bytes 958472 | tf_op jit(solution)/shard_map/ppermute | solution.py:20
  93.9 21.7 %collective-permute-start.27 = (bf16[2,208,384]{2,1,0:T(8,128)(2,1)S(1)}, bf16[2,208,384]{2,1,0:T(8,128)(2,1)S(1)}, u32[]{:S(2)}, u32[]{:S(2)}) collective-permute-start(bf16[2,208,384]{2,1,0:T(8,128)(2,1)S(1)} %pad_maximum_fusion.2.refs_1_), channel_id=1, source_target_pairs={{0,16},{2,18},{4,20},{6,22},{8,24},{10,26},{12,28},{14,30},{16,0},... | collective-permute-start | bytes 958472 | tf_op jit(solution)/shard_map/ppermute | solution.py:20
  105.4 11.4 %collective-permute-start.26 = (bf16[2,208,384]{2,1,0:T(8,128)(2,1)S(1)}, bf16[2,208,384]{2,1,0:T(8,128)(2,1)S(1)}, u32[]{:S(2)}, u32[]{:S(2)}) collective-permute-start(bf16[2,208,384]{2,1,0:T(8,128)(2,1)S(1)} %slice.74), channel_id=1, source_target_pairs={{0,8},{2,10},{4,12},{6,14},{8,0},{10,2},{12,4},{14,6},{16,24},{18,... | collective-permute-start | bytes 958472 | tf_op jit(solution)/shard_map/ppermute | solution.py:20
  105.5 14.5 %collective-permute-start.32 = (bf16[2,208,384]{2,1,0:T(8,128)(2,1)S(1)}, bf16[2,208,384]{2,1,0:T(8,128)(2,1)S(1)}, u32[]{:S(2)}, u32[]{:S(2)}) collective-permute-start(bf16[2,208,384]{2,1,0:T(8,128)(2,1)S(1)} %collective-permute-done.25.refs_5_), channel_id=1, source_target_pairs={{0,2},{2,0},{4,6},{6,4},{8,10},{10,8},{12,14},{14,12},{16,18},{18,... | collective-permute-start | bytes 958472 | tf_op jit(solution)/shard_map/ppermute | solution.py:20
  108.0 13.1 %collective-permute-start.31 = (bf16[2,208,384]{2,1,0:T(8,128)(2,1)S(1)}, bf16[2,208,384]{2,1,0:T(8,128)(2,1)S(1)}, u32[]{:S(2)}, u32[]{:S(2)}) collective-permute-start(bf16[2,208,384]{2,1,0:T(8,128)(2,1)S(1)} %collective-permute-done.24.refs_2_), channel_id=1, source_target_pairs={{0,4},{2,6},{4,0},{6,2},{8,12},{10,14},{12,8},{14,10},{16,20},{18,... | collective-permute-start | bytes 958472 | tf_op jit(solution)/shard_map/ppermute | solution.py:20
  118.6 12.0 %collective-permute-start.35 = (bf16[2,208,384]{2,1,0:T(8,128)(2,1)S(1)}, bf16[2,208,384]{2,1,0:T(8,128)(2,1)S(1)}, u32[]{:S(2)}, u32[]{:S(2)}) collective-permute-start(bf16[2,208,384]{2,1,0:T(8,128)(2,1)S(1)} %collective-permute-done.27.refs_9_), channel_id=1, source_target_pairs={{0,4},{2,6},{4,0},{6,2},{8,12},{10,14},{12,8},{14,10},{16,20},{18,... | collective-permute-start | bytes 958472 | tf_op jit(solution)/shard_map/ppermute | solution.py:20
  120.0 10.7 %collective-permute-start.34 = (bf16[2,208,384]{2,1,0:T(8,128)(2,1)S(1)}, bf16[2,208,384]{2,1,0:T(8,128)(2,1)S(1)}, u32[]{:S(2)}, u32[]{:S(2)}) collective-permute-start(bf16[2,208,384]{2,1,0:T(8,128)(2,1)S(1)} %collective-permute-done.27.refs_9_), channel_id=1, source_target_pairs={{0,2},{2,0},{4,6},{6,4},{8,10},{10,8},{12,14},{14,12},{16,18},{18,... | collective-permute-start | bytes 958472 | tf_op jit(solution)/shard_map/ppermute | solution.py:20
  128.5 31.1 %collective-permute-start.18 = (f32[256,1024]{1,0:T(8,128)S(1)}, f32[256,1024]{1,0:T(8,128)S(1)}, u32[]{:S(2)}, u32[]{:S(2)}) collective-permute-start(f32[256,1024]{1,0:T(8,128)S(1)} %shard_map.419.refs_1_), channel_id=1, source_target_pairs={{0,1},{1,0},{2,3},{3,2},{4,5},{5,4},{6,7},{7,6},{8,9},{9,8},{10,11... | collective-permute-start | bytes 3145736 | tf_op jit(solution)/shard_map/ppermute | solution.py:20
  128.6 16.0 %collective-permute-start.37 = (bf16[2,208,384]{2,1,0:T(8,128)(2,1)S(1)}, bf16[2,208,384]{2,1,0:T(8,128)(2,1)S(1)}, u32[]{:S(2)}, u32[]{:S(2)}) collective-permute-start(bf16[2,208,384]{2,1,0:T(8,128)(2,1)S(1)} %collective-permute-done.28.refs_7_), channel_id=1, source_target_pairs={{0,2},{2,0},{4,6},{6,4},{8,10},{10,8},{12,14},{14,12},{16,18},{18,... | collective-permute-start | bytes 958472 | tf_op jit(solution)/shard_map/ppermute | solution.py:20
  130.6 11.8 %collective-permute-start.39 = (bf16[2,208,384]{2,1,0:T(8,128)(2,1)S(1)}, bf16[2,208,384]{2,1,0:T(8,128)(2,1)S(1)}, u32[]{:S(2)}, u32[]{:S(2)}) collective-permute-start(bf16[2,208,384]{2,1,0:T(8,128)(2,1)S(1)} %collective-permute-done.34.refs_10_), channel_id=1, source_target_pairs={{0,8},{2,10},{4,12},{6,14},{8,0},{10,2},{12,4},{14,6},{16,24},{18,... | collective-permute-start | bytes 958472 | tf_op jit(solution)/shard_map/ppermute | solution.py:20
  134.2 15.1 %collective-permute-start.36 = (bf16[2,208,384]{2,1,0:T(8,128)(2,1)S(1)}, bf16[2,208,384]{2,1,0:T(8,128)(2,1)S(1)}, u32[]{:S(2)}, u32[]{:S(2)}) collective-permute-start(bf16[2,208,384]{2,1,0:T(8,128)(2,1)S(1)} %pad_maximum_fusion.3.refs_1_), channel_id=1, source_target_pairs={{0,8},{2,10},{4,12},{6,14},{8,0},{10,2},{12,4},{14,6},{16,24},{18,... | collective-permute-start | bytes 958472 | tf_op jit(solution)/shard_map/ppermute | solution.py:20
  144.3 11.4 %collective-permute-start.42 = (bf16[2,208,384]{2,1,0:T(8,128)(2,1)S(1)}, bf16[2,208,384]{2,1,0:T(8,128)(2,1)S(1)}, u32[]{:S(2)}, u32[]{:S(2)}) collective-permute-start(bf16[2,208,384]{2,1,0:T(8,128)(2,1)S(1)} %collective-permute-done.38.refs_12_), channel_id=1, source_target_pairs={{0,8},{2,10},{4,12},{6,14},{8,0},{10,2},{12,4},{14,6},{16,24},{18,... | collective-permute-start | bytes 958472 | tf_op jit(solution)/shard_map/ppermute | solution.py:20
  144.6 12.9 %collective-permute-start.40 = (bf16[2,208,384]{2,1,0:T(8,128)(2,1)S(1)}, bf16[2,208,384]{2,1,0:T(8,128)(2,1)S(1)}, u32[]{:S(2)}, u32[]{:S(2)}) collective-permute-start(bf16[2,208,384]{2,1,0:T(8,128)(2,1)S(1)} %pad_maximum_fusion.3.refs_1_), channel_id=1, source_target_pairs={{0,2},{2,0},{4,6},{6,4},{8,10},{10,8},{12,14},{14,12},{16,18},{18,... | collective-permute-start | bytes 958472 | tf_op jit(solution)/shard_map/ppermute | solution.py:20
  157.5 12.2 %collective-permute-start.45 = (bf16[2,208,384]{2,1,0:T(8,128)(2,1)S(1)}, bf16[2,208,384]{2,1,0:T(8,128)(2,1)S(1)}, u32[]{:S(2)}, u32[]{:S(2)}) collective-permute-start(bf16[2,208,384]{2,1,0:T(8,128)(2,1)S(1)} %collective-permute-done.40.refs_3_), channel_id=1, source_target_pairs={{0,4},{2,6},{4,0},{6,2},{8,12},{10,14},{12,8},{14,10},{16,20},{18,... | collective-permute-start | bytes 958472 | tf_op jit(solution)/shard_map/ppermute | solution.py:20
  158.0 11.7 %collective-permute-start.47 = (bf16[2,208,384]{2,1,0:T(8,128)(2,1)S(1)}, bf16[2,208,384]{2,1,0:T(8,128)(2,1)S(1)}, u32[]{:S(2)}, u32[]{:S(2)}) collective-permute-start(bf16[2,208,384]{2,1,0:T(8,128)(2,1)S(1)} %collective-permute-done.44.refs_6_), channel_id=1, source_target_pairs={{0,2},{2,0},{4,6},{6,4},{8,10},{10,8},{12,14},{14,12},{16,18},{18,... | collective-permute-start | bytes 958472 | tf_op jit(solution)/shard_map/ppermute | solution.py:20
  (37 other events, 309.7 us)

commit v5 on v4

--- a/solution.py
+++ b/solution.py
@@ -473,8 +473,8 @@
 
 def hand_out(held, keep, send):
     for k in range(2):
-        keep[k] = held[2 * k]
-        send[k] = held[2 * k + 1].astype(BF)
+        keep[k] = held[3 * k]
+        send[k] = held[1 + k].astype(BF)
 
 
 def down_grads_kernel(idx, act, grad, keep, send, held):
@@ -628,7 +628,7 @@
             held[(y ^ by) * 4 + (z ^ zz), 4 * thin : 4 * thin + 16, :] = jnp.concatenate(
                 [packed, sums[rest * eighth : rest * (eighth + 1), :]], axis=0
             )
-    for at, k in enumerate((0, 2, 1, 3)):
+    for at, k in enumerate((0, 3, 1, 2)):
         keep_out[at] = held[k]
         send_out[at] = held[4 + k].astype(BF)
 
@@ -637,7 +637,7 @@
     for at in range(4):
         for group in range(2):
             for k in range(2):
-                yield refs[2 * at + group], k, (idx[1] * 2 + idx[0]) ^ at, (2 * k + group) ^ idx[2]
+                yield refs[2 * at + group], k, (idx[1] * 2 + idx[0]) ^ at, (3 * k) ^ group ^ idx[2]
 
 
 def unpack_layout(piece, k, lowest, table, quarter, place):
@@ -728,11 +728,11 @@
 
 
 ORDER = (
-    ("down4", None, 0), ("up8", None, 0), ("down8", None, 0), (4, 0, 4), (1, 0, 1), (2, 0, 2), ("y", None, 0),
-    (6, 4, 2), (8, 0, 8), ("z4", None, 0), (5, 4, 1), (3, 1, 2), (12, 8, 4), ("z8", None, 0), (10, 8, 2),
-    (9, 8, 1), ("even", None, 0), (13, 9, 4), (11, 9, 2), (7, 6, 1), ("odd", "even", 4), (15, 11, 4),
-    ("even2", "even", 2), ("even1", "even", 1), ("odd2", "odd", 2), ("odd1", "odd", 1), (14, 10, 4),
-    ("even3", "even1", 2), ("odd3", "odd2", 1),
+    ("down4", None, 0), ("up8", None, 0), ("down8", None, 0), (4, 0, 4), (1, 0, 1), (2, 0, 2),
+    ("y", None, 0), (6, 4, 2), (12, 0, 12), ("z4", None, 0), (5, 4, 1), (3, 1, 2), (8, 12, 4),
+    ("z8", None, 0), (14, 12, 2), (13, 12, 1), ("even", None, 0), (9, 13, 4), (15, 13, 2), (7, 6, 1),
+    ("odd", "even", 4), (11, 15, 4), ("even2", "even", 2), ("even1", "even", 1), ("odd2", "odd", 2),
+    ("odd1", "odd", 1), (10, 14, 4), ("even3", "even1", 2), ("odd3", "odd2", 1),
 )
 
 
@@ -761,16 +761,16 @@
             have(name, last)
         if name == "down4":
             down = down_keep + last.astype(F32)
-            coming["down8"] = exchange(down[1].astype(BF), 8)
+            coming["down8"] = exchange(down[1].astype(BF), 12)
         elif name == "y":
             total = keep + last.astype(F32)
             coming["z4"] = exchange(total[2:].astype(BF), 4)
         elif name == "z4":
             total = total[:2] + last.astype(F32)
-            coming["z8"] = exchange(total[1].astype(BF), 8)
+            coming["z8"] = exchange(total[1].astype(BF), 12)
         elif name == "z8":
             own = beyond(total[0] + last.astype(F32))
-            coming["even"] = exchange(own, 8)
+            coming["even"] = exchange(own, 12)
         if name in ("up8", "down8") and {"up8", "down8"} <= found.keys():
             sums = up + found["up8"].astype(F32), down[0] + found["down8"].astype(F32)
             have(0, jnp.stack([beyond(piece) for piece in sums]))
@@ -974,7 +974,7 @@
         first, input_part, over_cores(input_part),
     )
     units_pieces, attention_pieces = reduced_and_gathered(
-        keep, up_total[0], exchange(up_part, 8), down_keep, down_far, keep, send_far
+        keep, up_total[0], exchange(up_part, 12), down_keep, down_far, keep, send_far
     )
 
     up_t, up_l, down_t, down_l, token = call(

time: 173 us -> 170 us (0.983)
  starting transfers between devices: 55.2 us -> 50.4 us
  waiting for transfers between devices: 70.5 us -> 72.4 us
    ppermute x48, starting transfers between devices: 55.2 us -> 50.4 us  [exchange(): lax.ppermute(shard, axis, [(i, i ^ mask) for i in range(lax.axis_size(axi...]
    ppermute x48, waiting for transfers between devices: 70.5 us -> 72.4 us  [exchange(): lax.ppermute(shard, axis, [(i, i ^ mask) for i in range(lax.axis_size(axi...]
  transfers between devices with their start and end apart: 48 -> 48, of which waited for: 22 -> 25; matrix products, arithmetic and copies ran while one was open for 1% -> 1% of each run, Pallas kernels for 20% -> 21%
where the time goes in v5:
time: 170 us
  waiting for transfers between devices  72.4 us (43%)
  starting transfers between devices  50.4 us (30%)
  Pallas kernels  44.3 us (26%)
    ppermute x48, waiting for transfers between devices, exchange(): lax.ppermute(shard, axis, [(i, i ^ mask) for i in range(lax.axis_size(axi...  72.4 us
    ppermute x48, starting transfers between devices, exchange(): lax.ppermute(shard, axis, [(i, i ^ mask) for i in range(lax.axis_size(axi...  50.4 us
    pallas_call x15, Pallas kernels, call(): pl.pallas_call(body, out_shape=tuple((pltpu.VMEM(o.shape, o.dtype) if k i...  44.3 us
  transfers between devices with their start and end apart: 48, of which 25 were waited for; matrix products, arithmetic and copies ran while one was open for 1% of the time, Pallas kernels for 21%

profile of v5, /device:TPU:0, one launch (start us, length us, event | category | flops | bytes accessed | tf_op | source)
XLA Modules:
  0.0 170.2 jit_solution(7990742389449494562)
XLA Ops:
  0.7 3.0 %collective-permute-start = (bf16[256,768]{1,0:T(8,128)(2,1)}, bf16[256,768]{1,0:T(8,128)(2,1)S(1)}, u32[]{:S(2)}, u32[]{:S(2)}) collective-permute-start(bf16[256,768]{1,0:T(8,128)(2,1)} %refs_5_.7), channel_id=1, source_target_pairs={{0,2},{2,0},{4,6},{6,4},{8,10},{10,8},{12,14},{14,12},{16,18},{18,... | collective-permute-start | bytes 1179656 | tf_op jit(solution)/shard_map/ppermute | solution.py:20
  6.5 2.7 %shard_map.408 = (bf16[256,192]{1,0:T(8,128)(2,1)S(1)}, f32[256,128]{1,0:T(8,128)S(1)}, f32[16,1536]{1,0:T(8,128)S(1)}, bf16[192,256]{1,0:T(8,128)(2,1)S(1)}) custom-call(s32[4]{0:T(128)S(1)} %pad_add_fusion.refs_0_, bf16[192,256]{1,0:T(8,128)(2,1)} %bitcast.55, s32[1,256]{1,0:T(1,128)} %bitcast.58, bf16[2,768]{1,0:T(2,128)(2,1)} %refs_3_.5, ...), custom_call_target="tpu_custom_call" | custom-call | flops 100000000 | bytes 835600 | tf_op jit(solution)/shard_map/pallas_call | solution.py:85
  9.3 2.6 %shard_map.409 = (bf16[256,512]{1,0:T(8,128)(2,1)S(1)}, bf16[256,512]{1,0:T(8,128)(2,1)S(1)}, bf16[256,512]{1,0:T(8,128)(2,1)S(1)}, bf16[256,192]{1,0:T(8,128)(2,1)S(1)}) custom-call(bf16[256,768]{1,0:T(8,128)(2,1)} %refs_5_.7, bf16[192,256]{1,0:T(8,128)(2,1)} %bitcast.50, bf16[3,768,384]{2,1,0:T(8,128)(2,1)} %refs_3_.9, bf16[2,384]{1,0:T(2,128)(2,1)} %refs_8_.5, ...), custom_call_target="tpu_custom_call" | custom-call | flops 100000000 | bytes 3356544 | tf_op jit(solution)/shard_map/pallas_call | solution.py:85
  15.3 2.7 %shard_map.410 = (f32[256,1024]{1,0:T(8,128)S(1)}, bf16[512,512]{1,0:T(8,128)(2,1)S(1)}, bf16[512,512]{1,0:T(8,128)(2,1)S(1)}) custom-call(bf16[256,512]{1,0:T(8,128)(2,1)S(1)} %get-tuple-element.130.refs_0_, bf16[256,512]{1,0:T(8,128)(2,1)S(1)} %get-tuple-element.131.refs_1_, bf16[256,512]{1,0:T(8,128)(2,1)S(1)} %get-tuple-element.132.refs_2_, ...), custom_call_target="tpu_custom_call" | custom-call | flops 100000000 | bytes 5885824 | tf_op jit(solution)/shard_map/pallas_call | solution.py:85
  18.0 2.6 %collective-permute-done.3.refs_4_ = f32[256,1024]{1,0:T(8,128)S(1)} collective-permute-done((f32[256,1024]{1,0:T(8,128)S(1)}, f32[256,1024]{1,0:T(8,128)S(1)}, u32[]{:S(2)}, u32[]{:S(2)}) %collective-permute-start.3) | collective-permute-done | bytes 1048608 | tf_op jit(solution)/shard_map/ppermute | solution.py:20
  27.6 4.4 %shard_map.413 = (bf16[256,768]{1,0:T(8,128)(2,1)}, bf16[192,256]{1,0:T(8,128)(2,1)}, f32[256,960]{1,0:T(8,128)S(1)}, bf16[256,1024]{1,0:T(8,128)(2,1)S(1)}, bf1...) custom-call(s32[4]{0:T(128)S(1)} %pad_add_fusion.refs_0_, ...), custom_call_target="tpu_custom_call" | custom-call | flops 1400000000 | bytes 14109456 | tf_op jit(solution)/shard_map/pallas_call | solution.py:85
  37.9 5.6 %collective-permute-done.8.refs_10_.refs_8_ = bf16[128,1024]{1,0:T(8,128)(2,1)S(1)} collective-permute-done((bf16[128,1024]{1,0:T(8,128)(2,1)S(1)}, bf16[128,1024]{1,0:T(8,128)(2,1)S(1)}, u32[]{:S(2)}, u32[]{:S(2)}) %collective-permute-start.8) | collective-permute-done | bytes 262176 | tf_op jit(solution)/shard_map/ppermute | solution.py:20
  48.9 3.2 %collective-permute-done.13.refs_12_ = f32[32,384]{1,0:T(8,128)S(1)} collective-permute-done((f32[32,384]{1,0:T(8,128)S(1)}, f32[32,384]{1,0:T(8,128)S(1)}, u32[]{:S(2)}, u32[]{:S(2)}) %collective-permute-start.13) | collective-permute-done | bytes 49184 | tf_op jit(solution)/shard_map/ppermute | solution.py:20
  54.5 4.7 %shard_map.415 = (f32[2,208,384]{2,1,0:T(8,128)S(1)}, bf16[2,208,384]{2,1,0:T(8,128)(2,1)S(1)}, bf16[1024,512]{1,0:T(8,128)(2,1)S(1)}, bf16[1024,1024]{1,0:T(8,128)(2,1)S(1)}) custom-call(s32[4]{0:T(128)S(1)} %pad_add_fusion.refs_0_, bf16[256,1024]{1,0:T(8,128)(2,1)S(1)} %get-tuple-element.135.refs_0_.refs_1_, ...), custom_call_target="tpu_custom_call" | custom-call | flops 1800000000 | bytes 13213712 | tf_op jit(solution)/shard_map/pallas_call | solution.py:85
  64.7 8.8 %shard_map.417 = (bf16[512,512]{1,0:T(8,128)(2,1)S(1)}, bf16[512,512]{1,0:T(8,128)(2,1)S(1)}, bf16[512,512]{1,0:T(8,128)(2,1)S(1)}, bf16[512,512]{1,0:T(8,128)(2,1)S(1)}, bf16[256,960]{1,0:T(8,128)(2,1)S(1)}) custom-call(s32[4]{0:T(128)S(1)} %pad_add_fusion.refs_0_, bf16[512,512]{1,0:T(8,128)(2,1)S(1)} %get-tuple-element.158.refs_1_, ...), custom_call_target="tpu_custom_call" | custom-call | flops 5000000000 | bytes 8433552 | tf_op jit(solution)/shard_map/pallas_call | solution.py:85
  73.8 3.7 %collective-permute-start.20 = (bf16[208,384]{1,0:T(8,128)(2,1)S(1)}, bf16[208,384]{1,0:T(8,128)(2,1)S(1)}, u32[]{:S(2)}, u32[]{:S(2)}) collective-permute-start(bf16[208,384]{1,0:T(8,128)(2,1)S(1)} %fusion.6.refs_13_), channel_id=1, source_target_pairs={{0,24},{2,26},{4,28},{6,30},{8,16},{10,18},{12,20},{14,22},{16,8},... | collective-permute-start | bytes 479240 | tf_op jit(solution)/shard_map/ppermute | solution.py:20
  83.3 4.0 %collective-permute-done.22 = bf16[208,384]{1,0:T(8,128)(2,1)S(1)} collective-permute-done((bf16[208,384]{1,0:T(8,128)(2,1)S(1)}, bf16[208,384]{1,0:T(8,128)(2,1)S(1)}, u32[]{:S(2)}, u32[]{:S(2)}) %collective-permute-start.22) | collective-permute-done | bytes 159776 | tf_op jit(solution)/shard_map/ppermute | solution.py:20
  87.5 4.4 %collective-permute-start.25 = (bf16[2,208,384]{2,1,0:T(8,128)(2,1)S(1)}, bf16[2,208,384]{2,1,0:T(8,128)(2,1)S(1)}, u32[]{:S(2)}, u32[]{:S(2)}) collective-permute-start(bf16[2,208,384]{2,1,0:T(8,128)(2,1)S(1)} %pad_maximum_fusion.2.refs_1_), channel_id=1, source_target_pairs={{0,8},{2,10},{4,12},{6,14},{8,0},{10,2},{12,4},{14,6},{16,24},{18,... | collective-permute-start | bytes 958472 | tf_op jit(solution)/shard_map/ppermute | solution.py:20
  96.3 3.5 %collective-permute-done.25.refs_5_ = bf16[2,208,384]{2,1,0:T(8,128)(2,1)S(1)} collective-permute-done((bf16[2,208,384]{2,1,0:T(8,128)(2,1)S(1)}, bf16[2,208,384]{2,1,0:T(8,128)(2,1)S(1)}, u32[]{:S(2)}, u32[]{:S(2)}) %collective-permute-start.25) | collective-permute-done | bytes 319520 | tf_op jit(solution)/shard_map/ppermute | solution.py:20
  100.4 5.4 %collective-permute-done.23.refs_3_ = bf16[2,208,384]{2,1,0:T(8,128)(2,1)S(1)} collective-permute-done((bf16[2,208,384]{2,1,0:T(8,128)(2,1)S(1)}, bf16[2,208,384]{2,1,0:T(8,128)(2,1)S(1)}, u32[]{:S(2)}, u32[]{:S(2)}) %collective-permute-start.23) | collective-permute-done | bytes 319520 | tf_op jit(solution)/shard_map/ppermute | solution.py:20
  108.0 4.5 %collective-permute-done.28.refs_7_ = bf16[2,208,384]{2,1,0:T(8,128)(2,1)S(1)} collective-permute-done((bf16[2,208,384]{2,1,0:T(8,128)(2,1)S(1)}, bf16[2,208,384]{2,1,0:T(8,128)(2,1)S(1)}, u32[]{:S(2)}, u32[]{:S(2)}) %collective-permute-start.28) | collective-permute-done | bytes 319520 | tf_op jit(solution)/shard_map/ppermute | solution.py:20
  112.6 3.9 %collective-permute-done.26 = bf16[2,208,384]{2,1,0:T(8,128)(2,1)S(1)} collective-permute-done((bf16[2,208,384]{2,1,0:T(8,128)(2,1)S(1)}, bf16[2,208,384]{2,1,0:T(8,128)(2,1)S(1)}, u32[]{:S(2)}, u32[]{:S(2)}) %collective-permute-start.26) | collective-permute-done | bytes 319520 | tf_op jit(solution)/shard_map/ppermute | solution.py:20
  120.4 2.8 %collective-permute-done.30.refs_9_ = bf16[2,208,384]{2,1,0:T(8,128)(2,1)S(1)} collective-permute-done((bf16[2,208,384]{2,1,0:T(8,128)(2,1)S(1)}, bf16[2,208,384]{2,1,0:T(8,128)(2,1)S(1)}, u32[]{:S(2)}, u32[]{:S(2)}) %collective-permute-start.30) | collective-permute-done | bytes 319520 | tf_op jit(solution)/shard_map/ppermute | solution.py:20
  133.0 6.4 %collective-permute-done.39.refs_10_ = bf16[2,208,384]{2,1,0:T(8,128)(2,1)S(1)} collective-permute-done((bf16[2,208,384]{2,1,0:T(8,128)(2,1)S(1)}, bf16[2,208,384]{2,1,0:T(8,128)(2,1)S(1)}, u32[]{:S(2)}, u32[]{:S(2)}) %collective-permute-start.39) | collective-permute-done | bytes 319520 | tf_op jit(solution)/shard_map/ppermute | solution.py:20
  141.4 5.0 %collective-permute-done.36.refs_2_ = bf16[2,208,384]{2,1,0:T(8,128)(2,1)S(1)} collective-permute-done((bf16[2,208,384]{2,1,0:T(8,128)(2,1)S(1)}, bf16[2,208,384]{2,1,0:T(8,128)(2,1)S(1)}, u32[]{:S(2)}, u32[]{:S(2)}) %collective-permute-start.36) | collective-permute-done | bytes 319520 | tf_op jit(solution)/shard_map/ppermute | solution.py:20
  150.0 2.8 %collective-permute-done.42.refs_12_ = bf16[2,208,384]{2,1,0:T(8,128)(2,1)S(1)} collective-permute-done((bf16[2,208,384]{2,1,0:T(8,128)(2,1)S(1)}, bf16[2,208,384]{2,1,0:T(8,128)(2,1)S(1)}, u32[]{:S(2)}, u32[]{:S(2)}) %collective-permute-start.42) | collective-permute-done | bytes 319520 | tf_op jit(solution)/shard_map/ppermute | solution.py:20
  157.9 4.0 %collective-permute-done.46.refs_11_ = bf16[2,208,384]{2,1,0:T(8,128)(2,1)S(1)} collective-permute-done((bf16[2,208,384]{2,1,0:T(8,128)(2,1)S(1)}, bf16[2,208,384]{2,1,0:T(8,128)(2,1)S(1)}, u32[]{:S(2)}, u32[]{:S(2)}) %collective-permute-start.46) | collective-permute-done | bytes 319520 | tf_op jit(solution)/shard_map/ppermute | solution.py:20
  161.9 4.9 %shard_map.421 = (f32[768,1536]{1,0:T(8,128)}, f32[192,384]{1,0:T(8,128)}, f32[1536,768]{1,0:T(8,128)}, f32[192,384]{1,0:T(8,128)}, f32[8,128]{1,0:T(8,128)S(1)}) custom-call(s32[4]{0:T(128)S(1)} %pad_add_fusion.refs_0_, bf16[2,208,384]{2,1,0:T(8,128)(2,1)S(1)} %pad_maximum_fusion.2.refs_1_, bf16[2,208,384]{2,1,0:T(8,128)(2,1)S(1)} %collective-permute-done.24.refs_2_, ...), custom_call_target="tpu_custom_call" | custom-call | flops 100000000 | bytes 15142928 | tf_op jit(solution)/shard_map/pallas_call | solution.py:85
  166.8 3.2 %shard_map.422 = (f32[3,768,384]{2,1,0:T(8,128)}, f32[384,768]{1,0:T(8,128)}, f32[3,192,96]{2,1,0:T(8,128)}, f32[96,192]{1,0:T(8,128)}, f32[2,768]{1,0:T(2,128)}...) custom-call(s32[4]{0:T(128)S(1)} %pad_add_fusion.refs_0_, ...), custom_call_target="tpu_custom_call" | custom-call | flops 100000000 | bytes 7608080 | tf_op jit(solution)/shard_map/pallas_call | solution.py:85
  (130 shorter events, 70.1 us)
Async XLA Ops:
  0.7 14.5 %collective-permute-start = (bf16[256,768]{1,0:T(8,128)(2,1)}, bf16[256,768]{1,0:T(8,128)(2,1)S(1)}, u32[]{:S(2)}, u32[]{:S(2)}) collective-permute-start(bf16[256,768]{1,0:T(8,128)(2,1)} %refs_5_.7), channel_id=1, source_target_pairs={{0,2},{2,0},{4,6},{6,4},{8,10},{10,8},{12,14},{14,12},{16,18},{18,... | collective-permute-start | bytes 1179656 | tf_op jit(solution)/shard_map/ppermute | solution.py:20
  34.4 10.6 %collective-permute-start.7 = (f32[256,1024]{1,0:T(8,128)S(1)}, f32[256,1024]{1,0:T(8,128)S(1)}, u32[]{:S(2)}, u32[]{:S(2)}) collective-permute-start(f32[256,1024]{1,0:T(8,128)S(1)} %get-tuple-element.150.refs_2_), channel_id=1, source_target_pairs={{0,1},{1,0},{2,3},{3,2},{4,5},{5,4},{6,7},{7,6},{8,9},{9,8},{10,11... | collective-permute-start | bytes 3145736 | tf_op jit(solution)/shard_map/ppermute | solution.py:20
  34.7 14.1 %collective-permute-start.10 = (bf16[128,1024]{1,0:T(8,128)(2,1)S(1)}, bf16[128,1024]{1,0:T(8,128)(2,1)S(1)}, u32[]{:S(2)}, u32[]{:S(2)}) collective-permute-start(bf16[128,1024]{1,0:T(8,128)(2,1)S(1)} %collective-permute-done.5.refs_2_), channel_id=1, source_target_pairs={{0,4},{2,6},{4,0},{6,2},{8,12},{10,14},{12,8},{14,10},{16,20},{18,... | collective-permute-start | bytes 786440 | tf_op jit(solution)/shard_map/ppermute | solution.py:20
  36.4 15.7 %collective-permute-start.12 = (bf16[128,1024]{1,0:T(8,128)(2,1)S(1)}, bf16[128,1024]{1,0:T(8,128)(2,1)S(1)}, u32[]{:S(2)}, u32[]{:S(2)}) collective-permute-start(bf16[128,1024]{1,0:T(8,128)(2,1)S(1)} %get-tuple-element.146), channel_id=1, source_target_pairs={{0,2},{2,0},{4,6},{6,4},{8,10},{10,8},{12,14},{14,12},{16,18},{18,... | collective-permute-start | bytes 786440 | tf_op jit(solution)/shard_map/ppermute | solution.py:20
  61.0 12.5 %collective-permute-start.17 = (bf16[2,208,384]{2,1,0:T(8,128)(2,1)S(1)}, bf16[2,208,384]{2,1,0:T(8,128)(2,1)S(1)}, u32[]{:S(2)}, u32[]{:S(2)}) collective-permute-start(bf16[2,208,384]{2,1,0:T(8,128)(2,1)S(1)} %get-tuple-element.169), channel_id=1, source_target_pairs={{0,8},{2,10},{4,12},{6,14},{8,0},{10,2},{12,4},{14,6},{16,24},{18,... | collective-permute-start | bytes 958472 | tf_op jit(solution)/shard_map/ppermute | solution.py:20
  64.2 15.4 %collective-permute-start.21 = (bf16[2,208,384]{2,1,0:T(8,128)(2,1)S(1)}, bf16[2,208,384]{2,1,0:T(8,128)(2,1)S(1)}, u32[]{:S(2)}, u32[]{:S(2)}) collective-permute-start(bf16[2,208,384]{2,1,0:T(8,128)(2,1)S(1)} %get-tuple-element.173.refs_17_), channel_id=1, source_target_pairs={{0,8},{2,10},{4,12},{6,14},{8,0},{10,2},{12,4},{14,6},{16,24},{18,... | collective-permute-start | bytes 958472 | tf_op jit(solution)/shard_map/ppermute | solution.py:20
  81.6 24.2 %collective-permute-start.19 = (bf16[4,208,384]{2,1,0:T(8,128)(2,1)S(1)}, bf16[4,208,384]{2,1,0:T(8,128)(2,1)S(1)}, u32[]{:S(2)}, u32[]{:S(2)}) collective-permute-start(bf16[4,208,384]{2,1,0:T(8,128)(2,1)S(1)} %get-tuple-element.181.refs_5_), channel_id=1, source_target_pairs={{0,4},{2,6},{4,0},{6,2},{8,12},{10,14},{12,8},{14,10},{16,20},{18,... | collective-permute-start | bytes 1916936 | tf_op jit(solution)/shard_map/ppermute | solution.py:20
  87.5 12.4 %collective-permute-start.25 = (bf16[2,208,384]{2,1,0:T(8,128)(2,1)S(1)}, bf16[2,208,384]{2,1,0:T(8,128)(2,1)S(1)}, u32[]{:S(2)}, u32[]{:S(2)}) collective-permute-start(bf16[2,208,384]{2,1,0:T(8,128)(2,1)S(1)} %pad_maximum_fusion.2.refs_1_), channel_id=1, source_target_pairs={{0,8},{2,10},{4,12},{6,14},{8,0},{10,2},{12,4},{14,6},{16,24},{18,... | collective-permute-start | bytes 958472 | tf_op jit(solution)/shard_map/ppermute | solution.py:20
  93.3 12.4 %collective-permute-start.23 = (bf16[2,208,384]{2,1,0:T(8,128)(2,1)S(1)}, bf16[2,208,384]{2,1,0:T(8,128)(2,1)S(1)}, u32[]{:S(2)}, u32[]{:S(2)}) collective-permute-start(bf16[2,208,384]{2,1,0:T(8,128)(2,1)S(1)} %pad_maximum_fusion.2.refs_1_), channel_id=1, source_target_pairs={{0,4},{2,6},{4,0},{6,2},{8,12},{10,14},{12,8},{14,10},{16,20},{18,... | collective-permute-start | bytes 958472 | tf_op jit(solution)/shard_map/ppermute | solution.py:20
  93.8 18.7 %collective-permute-start.27 = (bf16[2,208,384]{2,1,0:T(8,128)(2,1)S(1)}, bf16[2,208,384]{2,1,0:T(8,128)(2,1)S(1)}, u32[]{:S(2)}, u32[]{:S(2)}) collective-permute-start(bf16[2,208,384]{2,1,0:T(8,128)(2,1)S(1)} %pad_maximum_fusion.2.refs_1_), channel_id=1, source_target_pairs={{0,24},{2,26},{4,28},{6,30},{8,16},{10,18},{12,20},{14,22},{16,8},... | collective-permute-start | bytes 958472 | tf_op jit(solution)/shard_map/ppermute | solution.py:20
  99.8 12.7 %collective-permute-start.28 = (bf16[2,208,384]{2,1,0:T(8,128)(2,1)S(1)}, bf16[2,208,384]{2,1,0:T(8,128)(2,1)S(1)}, u32[]{:S(2)}, u32[]{:S(2)}) collective-permute-start(bf16[2,208,384]{2,1,0:T(8,128)(2,1)S(1)} %collective-permute-done.25.refs_5_), channel_id=1, source_target_pairs={{0,4},{2,6},{4,0},{6,2},{8,12},{10,14},{12,8},{14,10},{16,20},{18,... | collective-permute-start | bytes 958472 | tf_op jit(solution)/shard_map/ppermute | solution.py:20
  105.9 10.6 %collective-permute-start.26 = (bf16[2,208,384]{2,1,0:T(8,128)(2,1)S(1)}, bf16[2,208,384]{2,1,0:T(8,128)(2,1)S(1)}, u32[]{:S(2)}, u32[]{:S(2)}) collective-permute-start(bf16[2,208,384]{2,1,0:T(8,128)(2,1)S(1)} %slice.74), channel_id=1, source_target_pairs={{0,8},{2,10},{4,12},{6,14},{8,0},{10,2},{12,4},{14,6},{16,24},{18,... | collective-permute-start | bytes 958472 | tf_op jit(solution)/shard_map/ppermute | solution.py:20
  106.0 12.9 %collective-permute-start.32 = (bf16[2,208,384]{2,1,0:T(8,128)(2,1)S(1)}, bf16[2,208,384]{2,1,0:T(8,128)(2,1)S(1)}, u32[]{:S(2)}, u32[]{:S(2)}) collective-permute-start(bf16[2,208,384]{2,1,0:T(8,128)(2,1)S(1)} %collective-permute-done.25.refs_5_), channel_id=1, source_target_pairs={{0,2},{2,0},{4,6},{6,4},{8,10},{10,8},{12,14},{14,12},{16,18},{18,... | collective-permute-start | bytes 958472 | tf_op jit(solution)/shard_map/ppermute | solution.py:20
  107.5 12.9 %collective-permute-start.31 = (bf16[2,208,384]{2,1,0:T(8,128)(2,1)S(1)}, bf16[2,208,384]{2,1,0:T(8,128)(2,1)S(1)}, u32[]{:S(2)}, u32[]{:S(2)}) collective-permute-start(bf16[2,208,384]{2,1,0:T(8,128)(2,1)S(1)} %collective-permute-done.24.refs_2_), channel_id=1, source_target_pairs={{0,4},{2,6},{4,0},{6,2},{8,12},{10,14},{12,8},{14,10},{16,20},{18,... | collective-permute-start | bytes 958472 | tf_op jit(solution)/shard_map/ppermute | solution.py:20
  112.6 10.6 %collective-permute-start.30 = (bf16[2,208,384]{2,1,0:T(8,128)(2,1)S(1)}, bf16[2,208,384]{2,1,0:T(8,128)(2,1)S(1)}, u32[]{:S(2)}, u32[]{:S(2)}) collective-permute-start(bf16[2,208,384]{2,1,0:T(8,128)(2,1)S(1)} %collective-permute-done.27.refs_13_), channel_id=1, source_target_pairs={{0,8},{2,10},{4,12},{6,14},{8,0},{10,2},{12,4},{14,6},{16,24},{18,... | collective-permute-start | bytes 958472 | tf_op jit(solution)/shard_map/ppermute | solution.py:20
  118.4 10.7 %collective-permute-start.35 = (bf16[2,208,384]{2,1,0:T(8,128)(2,1)S(1)}, bf16[2,208,384]{2,1,0:T(8,128)(2,1)S(1)}, u32[]{:S(2)}, u32[]{:S(2)}) collective-permute-start(bf16[2,208,384]{2,1,0:T(8,128)(2,1)S(1)} %collective-permute-done.27.refs_13_), channel_id=1, source_target_pairs={{0,4},{2,6},{4,0},{6,2},{8,12},{10,14},{12,8},{14,10},{16,20},{18,... | collective-permute-start | bytes 958472 | tf_op jit(solution)/shard_map/ppermute | solution.py:20
  127.5 29.4 %collective-permute-start.18 = (f32[256,1024]{1,0:T(8,128)S(1)}, f32[256,1024]{1,0:T(8,128)S(1)}, u32[]{:S(2)}, u32[]{:S(2)}) collective-permute-start(f32[256,1024]{1,0:T(8,128)S(1)} %shard_map.419.refs_1_), channel_id=1, source_target_pairs={{0,1},{1,0},{2,3},{3,2},{4,5},{5,4},{6,7},{7,6},{8,9},{9,8},{10,11... | collective-permute-start | bytes 3145736 | tf_op jit(solution)/shard_map/ppermute | solution.py:20
  127.6 12.9 %collective-permute-start.37 = (bf16[2,208,384]{2,1,0:T(8,128)(2,1)S(1)}, bf16[2,208,384]{2,1,0:T(8,128)(2,1)S(1)}, u32[]{:S(2)}, u32[]{:S(2)}) collective-permute-start(bf16[2,208,384]{2,1,0:T(8,128)(2,1)S(1)} %collective-permute-done.28.refs_7_), channel_id=1, source_target_pairs={{0,2},{2,0},{4,6},{6,4},{8,10},{10,8},{12,14},{14,12},{16,18},{18,... | collective-permute-start | bytes 958472 | tf_op jit(solution)/shard_map/ppermute | solution.py:20
  129.3 10.7 %collective-permute-start.38 = (bf16[2,208,384]{2,1,0:T(8,128)(2,1)S(1)}, bf16[2,208,384]{2,1,0:T(8,128)(2,1)S(1)}, u32[]{:S(2)}, u32[]{:S(2)}) collective-permute-start(bf16[2,208,384]{2,1,0:T(8,128)(2,1)S(1)} %collective-permute-done.34.refs_14_), channel_id=1, source_target_pairs={{0,4},{2,6},{4,0},{6,2},{8,12},{10,14},{12,8},{14,10},{16,20},{18,... | collective-permute-start | bytes 958472 | tf_op jit(solution)/shard_map/ppermute | solution.py:20
  132.3 14.0 %collective-permute-start.36 = (bf16[2,208,384]{2,1,0:T(8,128)(2,1)S(1)}, bf16[2,208,384]{2,1,0:T(8,128)(2,1)S(1)}, u32[]{:S(2)}, u32[]{:S(2)}) collective-permute-start(bf16[2,208,384]{2,1,0:T(8,128)(2,1)S(1)} %pad_maximum_fusion.3.refs_1_), channel_id=1, source_target_pairs={{0,8},{2,10},{4,12},{6,14},{8,0},{10,2},{12,4},{14,6},{16,24},{18,... | collective-permute-start | bytes 958472 | tf_op jit(solution)/shard_map/ppermute | solution.py:20
  140.0 12.8 %collective-permute-start.42 = (bf16[2,208,384]{2,1,0:T(8,128)(2,1)S(1)}, bf16[2,208,384]{2,1,0:T(8,128)(2,1)S(1)}, u32[]{:S(2)}, u32[]{:S(2)}) collective-permute-start(bf16[2,208,384]{2,1,0:T(8,128)(2,1)S(1)} %collective-permute-done.38.refs_16_), channel_id=1, source_target_pairs={{0,8},{2,10},{4,12},{6,14},{8,0},{10,2},{12,4},{14,6},{16,24},{18,... | collective-permute-start | bytes 958472 | tf_op jit(solution)/shard_map/ppermute | solution.py:20
  140.5 12.3 %collective-permute-start.40 = (bf16[2,208,384]{2,1,0:T(8,128)(2,1)S(1)}, bf16[2,208,384]{2,1,0:T(8,128)(2,1)S(1)}, u32[]{:S(2)}, u32[]{:S(2)}) collective-permute-start(bf16[2,208,384]{2,1,0:T(8,128)(2,1)S(1)} %pad_maximum_fusion.3.refs_1_), channel_id=1, source_target_pairs={{0,2},{2,0},{4,6},{6,4},{8,10},{10,8},{12,14},{14,12},{16,18},{18,... | collective-permute-start | bytes 958472 | tf_op jit(solution)/shard_map/ppermute | solution.py:20
  152.8 14.0 %collective-permute-start.45 = (bf16[2,208,384]{2,1,0:T(8,128)(2,1)S(1)}, bf16[2,208,384]{2,1,0:T(8,128)(2,1)S(1)}, u32[]{:S(2)}, u32[]{:S(2)}) collective-permute-start(bf16[2,208,384]{2,1,0:T(8,128)(2,1)S(1)} %collective-permute-done.40.refs_3_), channel_id=1, source_target_pairs={{0,4},{2,6},{4,0},{6,2},{8,12},{10,14},{12,8},{14,10},{16,20},{18,... | collective-permute-start | bytes 958472 | tf_op jit(solution)/shard_map/ppermute | solution.py:20
  155.1 11.7 %collective-permute-start.47 = (bf16[2,208,384]{2,1,0:T(8,128)(2,1)S(1)}, bf16[2,208,384]{2,1,0:T(8,128)(2,1)S(1)}, u32[]{:S(2)}, u32[]{:S(2)}) collective-permute-start(bf16[2,208,384]{2,1,0:T(8,128)(2,1)S(1)} %collective-permute-done.44.refs_6_), channel_id=1, source_target_pairs={{0,2},{2,0},{4,6},{6,4},{8,10},{10,8},{12,14},{14,12},{16,18},{18,... | collective-permute-start | bytes 958472 | tf_op jit(solution)/shard_map/ppermute | solution.py:20
  (37 other events, 303.3 us)

commit v6 on v5

--- a/solution.py
+++ b/solution.py
@@ -728,11 +728,11 @@
 
 
 ORDER = (
-    ("down4", None, 0), ("up8", None, 0), ("down8", None, 0), (4, 0, 4), (1, 0, 1), (2, 0, 2),
-    ("y", None, 0), (6, 4, 2), (12, 0, 12), ("z4", None, 0), (5, 4, 1), (3, 1, 2), (8, 12, 4),
-    ("z8", None, 0), (14, 12, 2), (13, 12, 1), ("even", None, 0), (9, 13, 4), (15, 13, 2), (7, 6, 1),
+    ("down4", None, 0), ("up8", None, 0), ("down8", None, 0), (4, 0, 4), ("y", None, 0), (1, 0, 1),
+    (12, 0, 12), (2, 0, 2), ("z4", None, 0), (5, 4, 1), (6, 4, 2), (13, 12, 1), (8, 12, 4), (7, 6, 1),
+    (14, 12, 2), ("z8", None, 0), (3, 2, 1), (9, 8, 1), ("even", None, 0), (15, 13, 2), (10, 14, 4),
     ("odd", "even", 4), (11, 15, 4), ("even2", "even", 2), ("even1", "even", 1), ("odd2", "odd", 2),
-    ("odd1", "odd", 1), (10, 14, 4), ("even3", "even1", 2), ("odd3", "odd2", 1),
+    ("odd1", "even1", 4), ("even3", "even1", 2), ("odd3", "odd2", 1),
 )
 
 

time: 170 us -> 169 us (level)
  waiting for transfers between devices: 72.4 us -> 62 us
  starting transfers between devices: 50.4 us -> 59.3 us
    ppermute x48, waiting for transfers between devices: 72.4 us -> 62 us  [exchange(): lax.ppermute(shard, axis, [(i, i ^ mask) for i in range(lax.axis_size(axi...]
    ppermute x48, starting transfers between devices: 50.4 us -> 59.3 us  [exchange(): lax.ppermute(shard, axis, [(i, i ^ mask) for i in range(lax.axis_size(axi...]
  transfers between devices with their start and end apart: 48 -> 48, of which waited for: 25 -> 24; matrix products, arithmetic and copies ran while one was open for 1% -> 1% of each run, Pallas kernels for 21% -> 21%
where the time goes in v6:
time: 169 us
  waiting for transfers between devices  62 us (37%)
  starting transfers between devices  59.3 us (35%)
  Pallas kernels  44.3 us (26%)
    ppermute x48, waiting for transfers between devices, exchange(): lax.ppermute(shard, axis, [(i, i ^ mask) for i in range(lax.axis_size(axi...  62 us
    ppermute x48, starting transfers between devices, exchange(): lax.ppermute(shard, axis, [(i, i ^ mask) for i in range(lax.axis_size(axi...  59.3 us
    pallas_call x15, Pallas kernels, call(): pl.pallas_call(body, out_shape=tuple((pltpu.VMEM(o.shape, o.dtype) if k i...  44.3 us
  transfers between devices with their start and end apart: 48, of which 24 were waited for; matrix products, arithmetic and copies ran while one was open for 1% of the time, Pallas kernels for 21%

profile of v6, /device:TPU:0, one launch (start us, length us, event | category | flops | bytes accessed | tf_op | source)
XLA Modules:
  0.0 168.7 jit_solution(556938620191699889)
XLA Ops:
  0.7 3.0 %collective-permute-start = (bf16[256,768]{1,0:T(8,128)(2,1)}, bf16[256,768]{1,0:T(8,128)(2,1)S(1)}, u32[]{:S(2)}, u32[]{:S(2)}) collective-permute-start(bf16[256,768]{1,0:T(8,128)(2,1)} %refs_5_.7), channel_id=1, source_target_pairs={{0,2},{2,0},{4,6},{6,4},{8,10},{10,8},{12,14},{14,12},{16,18},{18,... | collective-permute-start | bytes 1179656 | tf_op jit(solution)/shard_map/ppermute | solution.py:20
  6.5 2.7 %shard_map.408 = (bf16[256,192]{1,0:T(8,128)(2,1)S(1)}, f32[256,128]{1,0:T(8,128)S(1)}, f32[16,1536]{1,0:T(8,128)S(1)}, bf16[192,256]{1,0:T(8,128)(2,1)S(1)}) custom-call(s32[4]{0:T(128)S(1)} %pad_add_fusion.refs_0_, bf16[192,256]{1,0:T(8,128)(2,1)} %bitcast.55, s32[1,256]{1,0:T(1,128)} %bitcast.58, bf16[2,768]{1,0:T(2,128)(2,1)} %refs_3_.5, ...), custom_call_target="tpu_custom_call" | custom-call | flops 100000000 | bytes 835600 | tf_op jit(solution)/shard_map/pallas_call | solution.py:85
  9.3 2.6 %shard_map.409 = (bf16[256,512]{1,0:T(8,128)(2,1)S(1)}, bf16[256,512]{1,0:T(8,128)(2,1)S(1)}, bf16[256,512]{1,0:T(8,128)(2,1)S(1)}, bf16[256,192]{1,0:T(8,128)(2,1)S(1)}) custom-call(bf16[256,768]{1,0:T(8,128)(2,1)} %refs_5_.7, bf16[192,256]{1,0:T(8,128)(2,1)} %bitcast.50, bf16[3,768,384]{2,1,0:T(8,128)(2,1)} %refs_3_.9, bf16[2,384]{1,0:T(2,128)(2,1)} %refs_8_.5, ...), custom_call_target="tpu_custom_call" | custom-call | flops 100000000 | bytes 3356544 | tf_op jit(solution)/shard_map/pallas_call | solution.py:85
  15.3 2.7 %shard_map.410 = (f32[256,1024]{1,0:T(8,128)S(1)}, bf16[512,512]{1,0:T(8,128)(2,1)S(1)}, bf16[512,512]{1,0:T(8,128)(2,1)S(1)}) custom-call(bf16[256,512]{1,0:T(8,128)(2,1)S(1)} %get-tuple-element.130.refs_0_, bf16[256,512]{1,0:T(8,128)(2,1)S(1)} %get-tuple-element.131.refs_1_, bf16[256,512]{1,0:T(8,128)(2,1)S(1)} %get-tuple-element.132.refs_2_, ...), custom_call_target="tpu_custom_call" | custom-call | flops 100000000 | bytes 5885824 | tf_op jit(solution)/shard_map/pallas_call | solution.py:85
  18.0 2.6 %collective-permute-done.3.refs_4_ = f32[256,1024]{1,0:T(8,128)S(1)} collective-permute-done((f32[256,1024]{1,0:T(8,128)S(1)}, f32[256,1024]{1,0:T(8,128)S(1)}, u32[]{:S(2)}, u32[]{:S(2)}) %collective-permute-start.3) | collective-permute-done | bytes 1048608 | tf_op jit(solution)/shard_map/ppermute | solution.py:20
  27.6 4.4 %shard_map.413 = (bf16[256,768]{1,0:T(8,128)(2,1)}, bf16[192,256]{1,0:T(8,128)(2,1)}, f32[256,960]{1,0:T(8,128)S(1)}, bf16[256,1024]{1,0:T(8,128)(2,1)S(1)}, bf1...) custom-call(s32[4]{0:T(128)S(1)} %pad_add_fusion.refs_0_, ...), custom_call_target="tpu_custom_call" | custom-call | flops 1400000000 | bytes 14109456 | tf_op jit(solution)/shard_map/pallas_call | solution.py:85
  37.9 5.6 %collective-permute-done.8.refs_10_.refs_8_ = bf16[128,1024]{1,0:T(8,128)(2,1)S(1)} collective-permute-done((bf16[128,1024]{1,0:T(8,128)(2,1)S(1)}, bf16[128,1024]{1,0:T(8,128)(2,1)S(1)}, u32[]{:S(2)}, u32[]{:S(2)}) %collective-permute-start.8) | collective-permute-done | bytes 262176 | tf_op jit(solution)/shard_map/ppermute | solution.py:20
  48.9 3.2 %collective-permute-done.13.refs_12_ = f32[32,384]{1,0:T(8,128)S(1)} collective-permute-done((f32[32,384]{1,0:T(8,128)S(1)}, f32[32,384]{1,0:T(8,128)S(1)}, u32[]{:S(2)}, u32[]{:S(2)}) %collective-permute-start.13) | collective-permute-done | bytes 49184 | tf_op jit(solution)/shard_map/ppermute | solution.py:20
  54.5 4.7 %shard_map.415 = (f32[2,208,384]{2,1,0:T(8,128)S(1)}, bf16[2,208,384]{2,1,0:T(8,128)(2,1)S(1)}, bf16[1024,512]{1,0:T(8,128)(2,1)S(1)}, bf16[1024,1024]{1,0:T(8,128)(2,1)S(1)}) custom-call(s32[4]{0:T(128)S(1)} %pad_add_fusion.refs_0_, bf16[256,1024]{1,0:T(8,128)(2,1)S(1)} %get-tuple-element.135.refs_0_.refs_1_, ...), custom_call_target="tpu_custom_call" | custom-call | flops 1800000000 | bytes 13213712 | tf_op jit(solution)/shard_map/pallas_call | solution.py:85
  64.7 8.8 %shard_map.417 = (bf16[512,512]{1,0:T(8,128)(2,1)S(1)}, bf16[512,512]{1,0:T(8,128)(2,1)S(1)}, bf16[512,512]{1,0:T(8,128)(2,1)S(1)}, bf16[512,512]{1,0:T(8,128)(2,1)S(1)}, bf16[256,960]{1,0:T(8,128)(2,1)S(1)}) custom-call(s32[4]{0:T(128)S(1)} %pad_add_fusion.refs_0_, bf16[512,512]{1,0:T(8,128)(2,1)S(1)} %get-tuple-element.158.refs_1_, ...), custom_call_target="tpu_custom_call" | custom-call | flops 5000000000 | bytes 8433552 | tf_op jit(solution)/shard_map/pallas_call | solution.py:85
  73.8 3.7 %collective-permute-start.20 = (bf16[208,384]{1,0:T(8,128)(2,1)S(1)}, bf16[208,384]{1,0:T(8,128)(2,1)S(1)}, u32[]{:S(2)}, u32[]{:S(2)}) collective-permute-start(bf16[208,384]{1,0:T(8,128)(2,1)S(1)} %fusion.6.refs_13_), channel_id=1, source_target_pairs={{0,24},{2,26},{4,28},{6,30},{8,16},{10,18},{12,20},{14,22},{16,8},... | collective-permute-start | bytes 479240 | tf_op jit(solution)/shard_map/ppermute | solution.py:20
  83.3 4.0 %collective-permute-done.22 = bf16[208,384]{1,0:T(8,128)(2,1)S(1)} collective-permute-done((bf16[208,384]{1,0:T(8,128)(2,1)S(1)}, bf16[208,384]{1,0:T(8,128)(2,1)S(1)}, u32[]{:S(2)}, u32[]{:S(2)}) %collective-permute-start.22) | collective-permute-done | bytes 159776 | tf_op jit(solution)/shard_map/ppermute | solution.py:20
  87.5 4.4 %collective-permute-start.23 = (bf16[2,208,384]{2,1,0:T(8,128)(2,1)S(1)}, bf16[2,208,384]{2,1,0:T(8,128)(2,1)S(1)}, u32[]{:S(2)}, u32[]{:S(2)}) collective-permute-start(bf16[2,208,384]{2,1,0:T(8,128)(2,1)S(1)} %pad_maximum_fusion.2.refs_1_), channel_id=1, source_target_pairs={{0,8},{2,10},{4,12},{6,14},{8,0},{10,2},{12,4},{14,6},{16,24},{18,... | collective-permute-start | bytes 958472 | tf_op jit(solution)/shard_map/ppermute | solution.py:20
  96.3 3.5 %collective-permute-done.23.refs_5_ = bf16[2,208,384]{2,1,0:T(8,128)(2,1)S(1)} collective-permute-done((bf16[2,208,384]{2,1,0:T(8,128)(2,1)S(1)}, bf16[2,208,384]{2,1,0:T(8,128)(2,1)S(1)}, u32[]{:S(2)}, u32[]{:S(2)}) %collective-permute-start.23) | collective-permute-done | bytes 319520 | tf_op jit(solution)/shard_map/ppermute | solution.py:20
  100.0 2.5 %collective-permute-start.24 = (bf16[2,208,384]{2,1,0:T(8,128)(2,1)S(1)}, bf16[2,208,384]{2,1,0:T(8,128)(2,1)S(1)}, u32[]{:S(2)}, u32[]{:S(2)}) collective-permute-start(bf16[2,208,384]{2,1,0:T(8,128)(2,1)S(1)} %slice.74), channel_id=1, source_target_pairs={{0,8},{2,10},{4,12},{6,14},{8,0},{10,2},{12,4},{14,6},{16,24},{18,... | collective-permute-start | bytes 958472 | tf_op jit(solution)/shard_map/ppermute | solution.py:20
  104.6 5.1 %collective-permute-done.26.refs_13_ = bf16[2,208,384]{2,1,0:T(8,128)(2,1)S(1)} collective-permute-done((bf16[2,208,384]{2,1,0:T(8,128)(2,1)S(1)}, bf16[2,208,384]{2,1,0:T(8,128)(2,1)S(1)}, u32[]{:S(2)}, u32[]{:S(2)}) %collective-permute-start.26) | collective-permute-done | bytes 319520 | tf_op jit(solution)/shard_map/ppermute | solution.py:20
  111.1 3.6 %collective-permute-done.24 = bf16[2,208,384]{2,1,0:T(8,128)(2,1)S(1)} collective-permute-done((bf16[2,208,384]{2,1,0:T(8,128)(2,1)S(1)}, bf16[2,208,384]{2,1,0:T(8,128)(2,1)S(1)}, u32[]{:S(2)}, u32[]{:S(2)}) %collective-permute-start.24) | collective-permute-done | bytes 319520 | tf_op jit(solution)/shard_map/ppermute | solution.py:20
  122.3 3.6 %collective-permute-done.32.refs_8_ = bf16[2,208,384]{2,1,0:T(8,128)(2,1)S(1)} collective-permute-done((bf16[2,208,384]{2,1,0:T(8,128)(2,1)S(1)}, bf16[2,208,384]{2,1,0:T(8,128)(2,1)S(1)}, u32[]{:S(2)}, u32[]{:S(2)}) %collective-permute-start.32) | collective-permute-done | bytes 319520 | tf_op jit(solution)/shard_map/ppermute | solution.py:20
  130.1 2.7 %collective-permute-done.37.refs_4_ = bf16[2,208,384]{2,1,0:T(8,128)(2,1)S(1)} collective-permute-done((bf16[2,208,384]{2,1,0:T(8,128)(2,1)S(1)}, bf16[2,208,384]{2,1,0:T(8,128)(2,1)S(1)}, u32[]{:S(2)}, u32[]{:S(2)}) %collective-permute-start.37) | collective-permute-done | bytes 319520 | tf_op jit(solution)/shard_map/ppermute | solution.py:20
  132.8 4.4 %collective-permute-done.36.refs_10_ = bf16[2,208,384]{2,1,0:T(8,128)(2,1)S(1)} collective-permute-done((bf16[2,208,384]{2,1,0:T(8,128)(2,1)S(1)}, bf16[2,208,384]{2,1,0:T(8,128)(2,1)S(1)}, u32[]{:S(2)}, u32[]{:S(2)}) %collective-permute-start.36) | collective-permute-done | bytes 319520 | tf_op jit(solution)/shard_map/ppermute | solution.py:20
  143.8 6.2 %collective-permute-done.38.refs_2_ = bf16[2,208,384]{2,1,0:T(8,128)(2,1)S(1)} collective-permute-done((bf16[2,208,384]{2,1,0:T(8,128)(2,1)S(1)}, bf16[2,208,384]{2,1,0:T(8,128)(2,1)S(1)}, u32[]{:S(2)}, u32[]{:S(2)}) %collective-permute-start.38) | collective-permute-done | bytes 319520 | tf_op jit(solution)/shard_map/ppermute | solution.py:20
  151.6 2.7 %collective-permute-done.43.refs_12_ = bf16[2,208,384]{2,1,0:T(8,128)(2,1)S(1)} collective-permute-done((bf16[2,208,384]{2,1,0:T(8,128)(2,1)S(1)}, bf16[2,208,384]{2,1,0:T(8,128)(2,1)S(1)}, u32[]{:S(2)}, u32[]{:S(2)}) %collective-permute-start.43) | collective-permute-done | bytes 319520 | tf_op jit(solution)/shard_map/ppermute | solution.py:20
  160.5 4.9 %shard_map.421 = (f32[768,1536]{1,0:T(8,128)}, f32[192,384]{1,0:T(8,128)}, f32[1536,768]{1,0:T(8,128)}, f32[192,384]{1,0:T(8,128)}, f32[8,128]{1,0:T(8,128)S(1)}) custom-call(s32[4]{0:T(128)S(1)} %pad_add_fusion.refs_0_, bf16[2,208,384]{2,1,0:T(8,128)(2,1)S(1)} %pad_maximum_fusion.2.refs_1_, bf16[2,208,384]{2,1,0:T(8,128)(2,1)S(1)} %collective-permute-done.27.refs_2_, ...), custom_call_target="tpu_custom_call" | custom-call | flops 100000000 | bytes 15142928 | tf_op jit(solution)/shard_map/pallas_call | solution.py:85
  165.4 3.2 %shard_map.422 = (f32[3,768,384]{2,1,0:T(8,128)}, f32[384,768]{1,0:T(8,128)}, f32[3,192,96]{2,1,0:T(8,128)}, f32[96,192]{1,0:T(8,128)}, f32[2,768]{1,0:T(2,128)}...) custom-call(s32[4]{0:T(128)S(1)} %pad_add_fusion.refs_0_, ...), custom_call_target="tpu_custom_call" | custom-call | flops 100000000 | bytes 7608080 | tf_op jit(solution)/shard_map/pallas_call | solution.py:85
  (130 shorter events, 72.7 us)
Async XLA Ops:
  0.7 14.5 %collective-permute-start = (bf16[256,768]{1,0:T(8,128)(2,1)}, bf16[256,768]{1,0:T(8,128)(2,1)S(1)}, u32[]{:S(2)}, u32[]{:S(2)}) collective-permute-start(bf16[256,768]{1,0:T(8,128)(2,1)} %refs_5_.7), channel_id=1, source_target_pairs={{0,2},{2,0},{4,6},{6,4},{8,10},{10,8},{12,14},{14,12},{16,18},{18,... | collective-permute-start | bytes 1179656 | tf_op jit(solution)/shard_map/ppermute | solution.py:20
  34.4 10.6 %collective-permute-start.7 = (f32[256,1024]{1,0:T(8,128)S(1)}, f32[256,1024]{1,0:T(8,128)S(1)}, u32[]{:S(2)}, u32[]{:S(2)}) collective-permute-start(f32[256,1024]{1,0:T(8,128)S(1)} %get-tuple-element.150.refs_2_), channel_id=1, source_target_pairs={{0,1},{1,0},{2,3},{3,2},{4,5},{5,4},{6,7},{7,6},{8,9},{9,8},{10,11... | collective-permute-start | bytes 3145736 | tf_op jit(solution)/shard_map/ppermute | solution.py:20
  34.7 14.1 %collective-permute-start.10 = (bf16[128,1024]{1,0:T(8,128)(2,1)S(1)}, bf16[128,1024]{1,0:T(8,128)(2,1)S(1)}, u32[]{:S(2)}, u32[]{:S(2)}) collective-permute-start(bf16[128,1024]{1,0:T(8,128)(2,1)S(1)} %collective-permute-done.5.refs_2_), channel_id=1, source_target_pairs={{0,4},{2,6},{4,0},{6,2},{8,12},{10,14},{12,8},{14,10},{16,20},{18,... | collective-permute-start | bytes 786440 | tf_op jit(solution)/shard_map/ppermute | solution.py:20
  36.4 15.7 %collective-permute-start.12 = (bf16[128,1024]{1,0:T(8,128)(2,1)S(1)}, bf16[128,1024]{1,0:T(8,128)(2,1)S(1)}, u32[]{:S(2)}, u32[]{:S(2)}) collective-permute-start(bf16[128,1024]{1,0:T(8,128)(2,1)S(1)} %get-tuple-element.146), channel_id=1, source_target_pairs={{0,2},{2,0},{4,6},{6,4},{8,10},{10,8},{12,14},{14,12},{16,18},{18,... | collective-permute-start | bytes 786440 | tf_op jit(solution)/shard_map/ppermute | solution.py:20
  61.0 12.5 %collective-permute-start.17 = (bf16[2,208,384]{2,1,0:T(8,128)(2,1)S(1)}, bf16[2,208,384]{2,1,0:T(8,128)(2,1)S(1)}, u32[]{:S(2)}, u32[]{:S(2)}) collective-permute-start(bf16[2,208,384]{2,1,0:T(8,128)(2,1)S(1)} %get-tuple-element.169), channel_id=1, source_target_pairs={{0,8},{2,10},{4,12},{6,14},{8,0},{10,2},{12,4},{14,6},{16,24},{18,... | collective-permute-start | bytes 958472 | tf_op jit(solution)/shard_map/ppermute | solution.py:20
  64.2 15.4 %collective-permute-start.21 = (bf16[2,208,384]{2,1,0:T(8,128)(2,1)S(1)}, bf16[2,208,384]{2,1,0:T(8,128)(2,1)S(1)}, u32[]{:S(2)}, u32[]{:S(2)}) collective-permute-start(bf16[2,208,384]{2,1,0:T(8,128)(2,1)S(1)} %get-tuple-element.173.refs_17_), channel_id=1, source_target_pairs={{0,8},{2,10},{4,12},{6,14},{8,0},{10,2},{12,4},{14,6},{16,24},{18,... | collective-permute-start | bytes 958472 | tf_op jit(solution)/shard_map/ppermute | solution.py:20
  81.6 18.3 %collective-permute-start.19 = (bf16[4,208,384]{2,1,0:T(8,128)(2,1)S(1)}, bf16[4,208,384]{2,1,0:T(8,128)(2,1)S(1)}, u32[]{:S(2)}, u32[]{:S(2)}) collective-permute-start(bf16[4,208,384]{2,1,0:T(8,128)(2,1)S(1)} %get-tuple-element.181.refs_5_), channel_id=1, source_target_pairs={{0,4},{2,6},{4,0},{6,2},{8,12},{10,14},{12,8},{14,10},{16,20},{18,... | collective-permute-start | bytes 1916936 | tf_op jit(solution)/shard_map/ppermute | solution.py:20
  87.5 12.4 %collective-permute-start.23 = (bf16[2,208,384]{2,1,0:T(8,128)(2,1)S(1)}, bf16[2,208,384]{2,1,0:T(8,128)(2,1)S(1)}, u32[]{:S(2)}, u32[]{:S(2)}) collective-permute-start(bf16[2,208,384]{2,1,0:T(8,128)(2,1)S(1)} %pad_maximum_fusion.2.refs_1_), channel_id=1, source_target_pairs={{0,8},{2,10},{4,12},{6,14},{8,0},{10,2},{12,4},{14,6},{16,24},{18,... | collective-permute-start | bytes 958472 | tf_op jit(solution)/shard_map/ppermute | solution.py:20
  91.9 12.2 %collective-permute-start.27 = (bf16[2,208,384]{2,1,0:T(8,128)(2,1)S(1)}, bf16[2,208,384]{2,1,0:T(8,128)(2,1)S(1)}, u32[]{:S(2)}, u32[]{:S(2)}) collective-permute-start(bf16[2,208,384]{2,1,0:T(8,128)(2,1)S(1)} %pad_maximum_fusion.2.refs_1_), channel_id=1, source_target_pairs={{0,2},{2,0},{4,6},{6,4},{8,10},{10,8},{12,14},{14,12},{16,18},{18,... | collective-permute-start | bytes 958472 | tf_op jit(solution)/shard_map/ppermute | solution.py:20
  93.3 16.3 %collective-permute-start.26 = (bf16[2,208,384]{2,1,0:T(8,128)(2,1)S(1)}, bf16[2,208,384]{2,1,0:T(8,128)(2,1)S(1)}, u32[]{:S(2)}, u32[]{:S(2)}) collective-permute-start(bf16[2,208,384]{2,1,0:T(8,128)(2,1)S(1)} %pad_maximum_fusion.2.refs_1_), channel_id=1, source_target_pairs={{0,24},{2,26},{4,28},{6,30},{8,16},{10,18},{12,20},{14,22},{16,8},... | collective-permute-start | bytes 958472 | tf_op jit(solution)/shard_map/ppermute | solution.py:20
  95.8 15.3 %collective-permute-start.25 = (bf16[2,208,384]{2,1,0:T(8,128)(2,1)S(1)}, bf16[2,208,384]{2,1,0:T(8,128)(2,1)S(1)}, u32[]{:S(2)}, u32[]{:S(2)}) collective-permute-start(bf16[2,208,384]{2,1,0:T(8,128)(2,1)S(1)} %pad_maximum_fusion.2.refs_1_), channel_id=1, source_target_pairs={{0,4},{2,6},{4,0},{6,2},{8,12},{10,14},{12,8},{14,10},{16,20},{18,... | collective-permute-start | bytes 958472 | tf_op jit(solution)/shard_map/ppermute | solution.py:20
  100.0 14.7 %collective-permute-start.24 = (bf16[2,208,384]{2,1,0:T(8,128)(2,1)S(1)}, bf16[2,208,384]{2,1,0:T(8,128)(2,1)S(1)}, u32[]{:S(2)}, u32[]{:S(2)}) collective-permute-start(bf16[2,208,384]{2,1,0:T(8,128)(2,1)S(1)} %slice.74), channel_id=1, source_target_pairs={{0,8},{2,10},{4,12},{6,14},{8,0},{10,2},{12,4},{14,6},{16,24},{18,... | collective-permute-start | bytes 958472 | tf_op jit(solution)/shard_map/ppermute | solution.py:20
  102.6 12.7 %collective-permute-start.31 = (bf16[2,208,384]{2,1,0:T(8,128)(2,1)S(1)}, bf16[2,208,384]{2,1,0:T(8,128)(2,1)S(1)}, u32[]{:S(2)}, u32[]{:S(2)}) collective-permute-start(bf16[2,208,384]{2,1,0:T(8,128)(2,1)S(1)} %collective-permute-done.23.refs_5_), channel_id=1, source_target_pairs={{0,2},{2,0},{4,6},{6,4},{8,10},{10,8},{12,14},{14,12},{16,18},{18,... | collective-permute-start | bytes 958472 | tf_op jit(solution)/shard_map/ppermute | solution.py:20
  104.1 11.3 %collective-permute-start.30 = (bf16[2,208,384]{2,1,0:T(8,128)(2,1)S(1)}, bf16[2,208,384]{2,1,0:T(8,128)(2,1)S(1)}, u32[]{:S(2)}, u32[]{:S(2)}) collective-permute-start(bf16[2,208,384]{2,1,0:T(8,128)(2,1)S(1)} %collective-permute-done.23.refs_5_), channel_id=1, source_target_pairs={{0,4},{2,6},{4,0},{6,2},{8,12},{10,14},{12,8},{14,10},{16,20},{18,... | collective-permute-start | bytes 958472 | tf_op jit(solution)/shard_map/ppermute | solution.py:20
  114.8 11.1 %collective-permute-start.29 = (bf16[2,208,384]{2,1,0:T(8,128)(2,1)S(1)}, bf16[2,208,384]{2,1,0:T(8,128)(2,1)S(1)}, u32[]{:S(2)}, u32[]{:S(2)}) collective-permute-start(bf16[2,208,384]{2,1,0:T(8,128)(2,1)S(1)} %collective-permute-done.26.refs_13_), channel_id=1, source_target_pairs={{0,4},{2,6},{4,0},{6,2},{8,12},{10,14},{12,8},{14,10},{16,20},{18,... | collective-permute-start | bytes 958472 | tf_op jit(solution)/shard_map/ppermute | solution.py:20
  118.5 14.2 %collective-permute-start.37 = (bf16[2,208,384]{2,1,0:T(8,128)(2,1)S(1)}, bf16[2,208,384]{2,1,0:T(8,128)(2,1)S(1)}, u32[]{:S(2)}, u32[]{:S(2)}) collective-permute-start(bf16[2,208,384]{2,1,0:T(8,128)(2,1)S(1)} %collective-permute-done.25.refs_3_), channel_id=1, source_target_pairs={{0,2},{2,0},{4,6},{6,4},{8,10},{10,8},{12,14},{14,12},{16,18},{18,... | collective-permute-start | bytes 958472 | tf_op jit(solution)/shard_map/ppermute | solution.py:20
  120.8 16.4 %collective-permute-start.36 = (bf16[2,208,384]{2,1,0:T(8,128)(2,1)S(1)}, bf16[2,208,384]{2,1,0:T(8,128)(2,1)S(1)}, u32[]{:S(2)}, u32[]{:S(2)}) collective-permute-start(bf16[2,208,384]{2,1,0:T(8,128)(2,1)S(1)} %collective-permute-done.33.refs_9_), channel_id=1, source_target_pairs={{0,2},{2,0},{4,6},{6,4},{8,10},{10,8},{12,14},{14,12},{16,18},{18,... | collective-permute-start | bytes 958472 | tf_op jit(solution)/shard_map/ppermute | solution.py:20
  125.9 11.3 %collective-permute-start.35 = (bf16[208,384]{1,0:T(8,128)(2,1)S(1)}, bf16[208,384]{1,0:T(8,128)(2,1)S(1)}, u32[]{:S(2)}, u32[]{:S(2)}) collective-permute-start(bf16[208,384]{1,0:T(8,128)(2,1)S(1)} %fusion.1), channel_id=1, source_target_pairs={{0,24},{2,26},{4,28},{6,30},{8,16},{10,18},{12,20},{14,22},{16,8},... | collective-permute-start | bytes 479240 | tf_op jit(solution)/shard_map/ppermute | solution.py:20
  128.4 31.0 %collective-permute-start.18 = (f32[256,1024]{1,0:T(8,128)S(1)}, f32[256,1024]{1,0:T(8,128)S(1)}, u32[]{:S(2)}, u32[]{:S(2)}) collective-permute-start(f32[256,1024]{1,0:T(8,128)S(1)} %shard_map.419.refs_1_), channel_id=1, source_target_pairs={{0,1},{1,0},{2,3},{3,2},{4,5},{5,4},{6,7},{7,6},{8,9},{9,8},{10,11... | collective-permute-start | bytes 3145736 | tf_op jit(solution)/shard_map/ppermute | solution.py:20
  137.2 12.8 %collective-permute-start.38 = (bf16[2,208,384]{2,1,0:T(8,128)(2,1)S(1)}, bf16[2,208,384]{2,1,0:T(8,128)(2,1)S(1)}, u32[]{:S(2)}, u32[]{:S(2)}) collective-permute-start(bf16[2,208,384]{2,1,0:T(8,128)(2,1)S(1)} %pad_maximum_fusion.3.refs_1_), channel_id=1, source_target_pairs={{0,8},{2,10},{4,12},{6,14},{8,0},{10,2},{12,4},{14,6},{16,24},{18,... | collective-permute-start | bytes 958472 | tf_op jit(solution)/shard_map/ppermute | solution.py:20
  138.4 15.9 %collective-permute-start.43 = (bf16[2,208,384]{2,1,0:T(8,128)(2,1)S(1)}, bf16[2,208,384]{2,1,0:T(8,128)(2,1)S(1)}, u32[]{:S(2)}, u32[]{:S(2)}) collective-permute-start(bf16[2,208,384]{2,1,0:T(8,128)(2,1)S(1)} %collective-permute-done.40.refs_16_), channel_id=1, source_target_pairs={{0,8},{2,10},{4,12},{6,14},{8,0},{10,2},{12,4},{14,6},{16,24},{18,... | collective-permute-start | bytes 958472 | tf_op jit(solution)/shard_map/ppermute | solution.py:20
  140.9 13.4 %collective-permute-start.42 = (bf16[2,208,384]{2,1,0:T(8,128)(2,1)S(1)}, bf16[2,208,384]{2,1,0:T(8,128)(2,1)S(1)}, u32[]{:S(2)}, u32[]{:S(2)}) collective-permute-start(bf16[2,208,384]{2,1,0:T(8,128)(2,1)S(1)} %pad_maximum_fusion.3.refs_1_), channel_id=1, source_target_pairs={{0,4},{2,6},{4,0},{6,2},{8,12},{10,14},{12,8},{14,10},{16,20},{18,... | collective-permute-start | bytes 958472 | tf_op jit(solution)/shard_map/ppermute | solution.py:20
  143.2 11.1 %collective-permute-start.41 = (bf16[2,208,384]{2,1,0:T(8,128)(2,1)S(1)}, bf16[2,208,384]{2,1,0:T(8,128)(2,1)S(1)}, u32[]{:S(2)}, u32[]{:S(2)}) collective-permute-start(bf16[2,208,384]{2,1,0:T(8,128)(2,1)S(1)} %pad_maximum_fusion.3.refs_1_), channel_id=1, source_target_pairs={{0,2},{2,0},{4,6},{6,4},{8,10},{10,8},{12,14},{14,12},{16,18},{18,... | collective-permute-start | bytes 958472 | tf_op jit(solution)/shard_map/ppermute | solution.py:20
  154.3 11.1 %collective-permute-start.44 = (bf16[2,208,384]{2,1,0:T(8,128)(2,1)S(1)}, bf16[2,208,384]{2,1,0:T(8,128)(2,1)S(1)}, u32[]{:S(2)}, u32[]{:S(2)}) collective-permute-start(bf16[2,208,384]{2,1,0:T(8,128)(2,1)S(1)} %collective-permute-done.41.refs_3_), channel_id=1, source_target_pairs={{0,8},{2,10},{4,12},{6,14},{8,0},{10,2},{12,4},{14,6},{16,24},{18,... | collective-permute-start | bytes 958472 | tf_op jit(solution)/shard_map/ppermute | solution.py:20
  (37 other events, 305.4 us)
